TPU v7x, 512 devices: a whole 4x4x16 slice. The times are simulated.
512 devices in a mesh: seq: 32 (over z, core), tp: 16 (over y, x).
Axes of the slice: x: 4, y: 4, z: 16, core: 2. Of those that a mesh axis runs over, the one named last changes fastest.
Arguments:
- inner_x: bfloat16 [12288, 8192], P('seq', 'tp'), may hold values from -9 to 9
- gate_z: bfloat16 [12288, 8192], P('seq', 'tp'), may hold values from -6 to 6
- bc_input: bfloat16 [12288, 256], P('seq'), may hold values from -3 to 3
- conv_inner: float32 [4, 8192], P(None, 'tp'), may hold values from -3 to 3
- conv_bc: float32 [4, 256], replicated, may hold values from -1.5 to 1.5
- step_size: float32 [128, 12288], P('tp', 'seq'), may hold values from 0 to 3
- log_decay: float32 [128, 12288], P('tp', 'seq'), may hold values from -0.8 to 0
- skip_gain: float32 [128], P('tp'), may hold values from 0.5 to 1.5
- norm_gain: float32 [8192], P('tp'), may hold values from 0.1 to 1.9
- out_weight: bfloat16 [8192, 2048], P('tp'), may hold values from -0.0625 to 0.0625
Outputs:
- mixed: bfloat16 [12288, 2048], P('seq', 'tp')
All inputs are finite; a program needn't handle non-finite values.
Results may differ from a plain program's by a relative error of at most 0.015.
Values may be sent and summed in bfloat16 or wider, within the bound.
No kernel may reach another device: no remote copies, remote signals or barrier semaphores. Data moves between devices by JAX's collectives and lax.ppermute only.
A program may use at most 64 MiB of HBM per device.

v0:
```python
import jax
import jax.numpy as jnp
from jax import lax
from jax.sharding import PartitionSpec as P

INNER = 8192


def passed_along(block, axis, distance):
    devices = range(lax.axis_size(axis))
    route = [(i - distance, i) for i in devices if i - distance in devices]
    return lax.ppermute(block, axis, route)


def entering(part, axis, combine, identity):
    place = lax.axis_index(axis)
    gathered = jax.tree.map(lambda a: lax.all_gather(a, axis), part)
    state = jax.tree.map(lambda a, e: jnp.zeros_like(a) + jnp.asarray(e, a.dtype), part, identity)

    def one(step, state):
        return combine(
            state, jax.tree.map(lambda a: lax.dynamic_index_in_dim(a, step, 0, False), gathered)
        )

    return lax.fori_loop(0, place, one, state)


def filtered_sigmoid_linear(leading, block, weights):
    whole = jnp.concatenate([leading, block], axis=0).astype(jnp.float32)
    length = block.shape[0]
    summed = weights[0] * whole[0:length]
    for offset in range(1, 4):
        summed = summed + weights[offset] * whole[offset : offset + length]
    return jax.nn.silu(summed).astype(jnp.bfloat16)


def local_ssd(inner_act, b_rows, c_rows, step_size, log_decay, skip_gain):
    length = inner_act.shape[0]
    cumulative = jnp.cumsum(log_decay, axis=1)
    scaled = (inner_act.astype(jnp.float32) * step_size.T[:, :, None]).astype(jnp.bfloat16)
    scores = lax.dot_general(
        c_rows, b_rows, (((1,), (1,)), ((), ())), preferred_element_type=jnp.float32
    )
    token_position = jnp.arange(length)
    causal_mask = token_position[:, None] >= token_position[None, :]
    spread = cumulative[:, :, None] - cumulative[:, None, :]
    decays = jnp.exp(jnp.where(causal_mask[None], spread, -jnp.inf))
    mixing = (scores[None] * decays).astype(jnp.bfloat16)
    within = jnp.einsum("hts,shp->thp", mixing, scaled, preferred_element_type=jnp.float32)
    tail = jnp.exp(cumulative[:, -1:] - cumulative)
    weighted = (scaled.astype(jnp.float32) * tail.T[:, :, None]).astype(jnp.bfloat16)
    summary = jnp.einsum("shp,sn->hpn", weighted, b_rows, preferred_element_type=jnp.float32)
    local_out = within + skip_gain[None, :, None] * inner_act.astype(jnp.float32)
    return (local_out, cumulative, summary, jnp.exp(cumulative[:, -1]))


def carried(cumulative, c_rows, incoming):
    product = jnp.einsum(
        "tn,hpn->thp", c_rows.astype(jnp.float32), incoming, precision=lax.Precision.HIGHEST
    )
    return jnp.exp(cumulative).T[:, :, None] * product


def combine_states(earlier, later):
    return (earlier[0] * later[0], later[0][:, None, None] * earlier[1] + later[1])


def shards(
    inner_x,
    gate_z,
    bc_input,
    conv_inner,
    conv_bc,
    step_size,
    log_decay,
    skip_gain,
    norm_gain,
    out_weight,
):
    length = inner_x.shape[0]
    heads = step_size.shape[0]
    width = inner_x.shape[1]
    head_dim = width // heads
    state_dim = bc_input.shape[1] // 2
    prior_x, prior_bc = passed_along((inner_x[length - 3 :], bc_input[length - 3 :]), "seq", 1)
    inner_act = filtered_sigmoid_linear(prior_x, inner_x, conv_inner).reshape(
        length, heads, head_dim
    )
    bc_act = filtered_sigmoid_linear(prior_bc, bc_input, conv_bc)
    b_rows = bc_act[:, :state_dim]
    c_rows = bc_act[:, state_dim:]
    local_out, cumulative, summary, decay_total = local_ssd(
        inner_act, b_rows, c_rows, step_size, log_decay, skip_gain
    )
    decay_in, incoming = entering(
        (decay_total, summary),
        "seq",
        combine_states,
        (jnp.ones_like(decay_total), jnp.zeros_like(summary)),
    )
    output = (local_out + carried(cumulative, c_rows, incoming)).reshape(length, width)
    gated = output * jax.nn.silu(gate_z.astype(jnp.float32))
    squares = lax.psum(jnp.sum(gated * gated, axis=1), "tp")
    normed = (gated * lax.rsqrt(squares / INNER + 1e-05)[:, None] * norm_gain).astype(jnp.bfloat16)
    share = lax.psum_scatter(
        lax.dot_general(
            out_weight, normed, (((0,), (1,)), ((), ())), preferred_element_type=jnp.float32
        ),
        "tp",
        scatter_dimension=0,
        tiled=True,
    )
    mixed = share.T.astype(jnp.bfloat16)
    return mixed


def solution(mesh):
    in_specs = (
        P("seq", "tp"),
        P("seq", "tp"),
        P("seq", None),
        P(None, "tp"),
        P(),
        P("tp", "seq"),
        P("tp", "seq"),
        P("tp"),
        P("tp"),
        P("tp", None),
    )
    out_specs = P("seq", "tp")
    return jax.shard_map(shards, mesh=mesh, in_specs=in_specs, out_specs=out_specs, check_vma=False)
```

profile of v0, /device:TPU:1, one launch (start us, length us, event | category | flops | bytes accessed | tf_op | source)
XLA Modules:
  0.0 276.1 jit_solution(11702241564414975467)
XLA Ops:
  6.5 0.0 copy-start
  6.5 0.0 copy-start.2
  6.5 0.0 all-gather.4.cloned.1.call-start
  6.5 0.9 slice.80
  7.4 4.9 %collective-permute-start.1 = (bf16[3,256]{1,0:T(4,128)(2,1)S(1)}, bf16[3,256]{1,0:T(4,128)(2,1)S(1)}, u32[]{:S(2)}, u32[]{:S(2)}) collective-permute-start(bf16[3,256]{1,0:T(4,128)(2,1)S(1)} %slice.80), channel_id=1, source_target_pairs={{0,16},{16,32},{32,48},{48,64},{64,80},{80,96},{96,112},{112,128},... | collective-permute-start | bytes 4616 | tf_op jit(solution)/shard_map/ppermute | solution.py:12
  12.3 0.7 slice.71
  13.0 1.9 collective-permute-start
  14.9 0.9 fusion.31
  15.8 1.9 reduce-window.6
  17.7 0.2 slice_reduce_fusion
  17.9 0.1 exponential_bitcast_fusion.1
  18.0 0.2 slice_reduce_fusion.1
  18.2 0.1 exponential_bitcast_fusion
  18.3 0.8 fusion.32
  19.1 0.0 collective-permute-done.1
  19.1 1.0 maximum_convert_fusion.1
  20.1 0.3 multiply_convert_fusion.13
  20.4 0.0 copy-start.4
  20.4 0.0 collective-permute-done
  20.4 1.1 maximum_convert_fusion
  21.5 1.4 fusion.21
  22.9 1.4 copy.21
  24.3 0.0 copy-done.2
  24.3 1.0 fusion.12
  25.3 0.0 all-gather.4.cloned.1.call-update
  25.3 0.0 reduce-scatter.2.cloned.1.call-start
  25.4 1.2 dynamic-slice
  27.2 0.2 dynamic-update-slice
  27.4 50.7 %all-reduce = f32[256]{0:T(256)S(1)} all-reduce(f32[256]{0:T(256)S(1)} %dynamic-update-slice), channel_id=2, replica_groups=mesh['seq'=32,'tp'=16] {'seq'}, use_global_device_ids=true, to_apply=%add | all-reduce | flops 256 | bytes 2048
  78.2 0.1 reshape.76
  78.3 0.1 iota_compare_fusion
  78.3 0.3 fusion.25
  78.6 0.0 copy-done.4
  78.6 2.5 fusion.4
  81.1 27.8 %all-gather.4.cloned.1.call-done = f32[256,64,128]{2,1,0:T(8,128)} async-done(((f32[8,64,128]{2,1,0:T(8,128)}), f32[256,64,128]{2,1,0:T(8,128)}) %all-gather.4.cloned.1.call-update) | async-done | bytes 8388624 | tf_op jit(solution)/shard_map/all_gather | solution.py:17
  108.9 1.1 while.12
  109.0 1.1 bitcast_add_fusion.2
  110.0 0.0 copy-done.1
  110.0 1.4 fusion.3
  111.4 1.4 copy.22
  112.8 1.3 multiply_reduce_fusion
  114.2 33.1 %psum.7 = f32[384]{0:T(512)S(1)} all-reduce(f32[384]{0:T(512)S(1)} %multiply_reduce_fusion), channel_id=1, replica_groups=mesh['seq'=32,'tp'=16] {'tp'}, use_global_device_ids=true, to_apply=%region_5.6 | all-reduce | flops 384 | bytes 3072 | tf_op jit(solution)/shard_map/psum | solution.py:103
  147.2 0.0 copy-done
  147.2 0.0 copy-done.3
  147.2 3.8 %convolution_bitcast_fusion = f32[2048,384]{0,1:T(8,128)} fusion(bf16[512,2048]{1,0:T(8,128)(2,1)S(1)} %copy-done, f32[512]{0:T(512)S(1)} %copy-done.3, f32[384]{0:T(512)S(1)} %add_rsqrt_fusion, f32[384,512]{1,0:T(8,128)S(1)} %copy.22, bf16[384,512]{1,0:T(8,128)(2,1)} %param.13), kind=kOutput, calls=%fused_computation.3 | convolution fusion | flops 807075840 | bytes 6426112 | tf_op jit(solution)/shard_map/dot_general | solution.py:106
  151.1 0.0 reduce-scatter.2.cloned.1.call-update
  151.1 116.6 %reduce-scatter.2.cloned.1.call-done = f32[128,384]{0,1:T(8,128)} async-done(((f32[2048,384]{0,1:T(8,128)}), f32[128,384]{0,1:T(8,128)}) %reduce-scatter.2.cloned.1.call-update) | async-done | bytes 196624 | tf_op jit(solution)/shard_map/reduce_scatter | solution.py:105
  267.7 1.6 convert_bitcast_fusion
  (7 shorter events, 0.1 us)
Async XLA Ops:
  6.5 140.7 %copy-start = (bf16[512,2048]{1,0:T(8,128)(2,1)S(1)}, bf16[512,2048]{1,0:T(8,128)(2,1)}, u32[]{:S(2)}) copy-start(bf16[512,2048]{1,0:T(8,128)(2,1)} %param.21) | copy-start | bytes 6291460
  6.5 17.7 %copy-start.2 = (f32[8,384]{1,0:T(8,128)S(1)}, f32[8,384]{1,0:T(8,128)}, u32[]{:S(2)}) copy-start(f32[8,384]{1,0:T(8,128)} %param.17) | copy-start | bytes 36868
  6.5 102.4 %all-gather.4.cloned.1.call-start = ((), (), s32[]{:S(2)}) async-start(), calls=%async_computation.2 | async-start | bytes 8650752 | tf_op jit(solution)/shard_map/all_gather | solution.py:17
  7.4 11.7 %collective-permute-start.1 = (bf16[3,256]{1,0:T(4,128)(2,1)S(1)}, bf16[3,256]{1,0:T(4,128)(2,1)S(1)}, u32[]{:S(2)}, u32[]{:S(2)}) collective-permute-start(bf16[3,256]{1,0:T(4,128)(2,1)S(1)} %slice.80), channel_id=1, source_target_pairs={{0,16},{16,32},{32,48},{48,64},{64,80},{80,96},{96,112},{112,128},... | collective-permute-start | bytes 4616 | tf_op jit(solution)/shard_map/ppermute | solution.py:12
  13.0 7.4 %collective-permute-start = (bf16[3,512]{1,0:T(4,128)(2,1)S(1)}, bf16[3,512]{1,0:T(4,128)(2,1)S(1)}, u32[]{:S(2)}, u32[]{:S(2)}) collective-permute-start(bf16[3,512]{1,0:T(4,128)(2,1)S(1)} %slice.71), channel_id=1, source_target_pairs={{0,16},{16,32},{32,48},{48,64},{64,80},{80,96},{96,112},{112,128},... | collective-permute-start | bytes 9224 | tf_op jit(solution)/shard_map/ppermute | solution.py:12
  20.4 58.2 %copy-start.4 = (f32[8]{0:T(128)S(1)}, f32[8]{0:T(128)}, u32[]{:S(2)}) copy-start(f32[8]{0:T(128)} %param.19) | copy-start | bytes 100
  25.3 242.4 %reduce-scatter.2.cloned.1.call-start = ((), (), s32[]{:S(2)}) async-start(), calls=%async_computation.1 | async-start | bytes 3342336 | tf_op jit(solution)/shard_map/reduce_scatter | solution.py:105
  81.1 28.9 %copy-start.1 = (f32[384,8,64]{0,2,1:T(8,128)S(1)}, f32[384,8,64]{0,2,1:T(8,128)}, u32[]{:S(2)}) copy-start(f32[384,8,64]{0,2,1:T(8,128)} %fusion.4) | copy-start | bytes 2359300
  81.1 66.1 %copy-start.3 = (f32[512]{0:T(512)S(1)}, f32[512]{0:T(512)}, u32[]{:S(2)}) copy-start(f32[512]{0:T(512)} %param.20) | copy-start | bytes 6148
Sparse Core Ops, SparseCore 0:
  25.4 83.4 all-gather.3
  151.2 116.4 reduce-scatter.1
where the time goes:
time: 278 us; the launch traced here: 276 us
  waiting for transfers between devices  144 us (52%)
  blocking collectives  83.8 us (30%)
  between operations  14.1 us (5%)
  other arithmetic  9.85 us (4%)
  matrix products  8.95 us (3%)
  local copies, waits for them, and re-layouts  8.02 us (3%)
  starting transfers between devices  6.88 us (2%)
    reduce_scatter x1, waiting for transfers between devices, shards(): lax.psum_scatter(lax.dot_general(out_weight, normed, (((0,), (1,)), ((),...  117 us
    unnamed x1, blocking collectives  50.7 us
    psum x1, blocking collectives, shards(): squares = lax.psum(jnp.sum(gated * gated, axis=1), 'tp')  33.1 us
    all_gather x1, waiting for transfers between devices, entering(): gathered = jax.tree.map(lambda a: lax.all_gather(a, axis), part)  27.8 us
    ppermute x2, starting transfers between devices, passed_along(): return lax.ppermute(block, axis, route)  6.83 us
  transfers between devices with their start and end apart: 4, of which 2 were waited for; matrix products, arithmetic and copies ran while one was open for 4% of the time, Pallas kernels for 0%

commit v1 on v0

v1 whole, which is shorter than its diff:
```python
import jax
import jax.numpy as jnp
from jax import lax
from jax.experimental import pallas as pl
from jax.experimental.pallas import tpu as pltpu
from jax.sharding import PartitionSpec as P

INNER = 8192
HEADS = 8
HEAD = 64
WIDTH = HEADS * HEAD
STATE = 128
LENGTH = 384
BLOCK = 128
BLOCKS = 32
GROUP = 8
SHARES = 16
EXTRA = 16

f32 = jnp.float32
bf16 = jnp.bfloat16


def parts3(a):
    high = a.astype(bf16)
    rest = a - high.astype(f32)
    middle = rest.astype(bf16)
    low = (rest - middle.astype(f32)).astype(bf16)
    return high, middle, low


def silu(a):
    return a * jax.nn.sigmoid(a)


def dot(a, b):
    return lax.dot_general(a, b, (((1,), (0,)), ((), ())), preferred_element_type=f32)


def columns_of(rows):
    padded = jnp.concatenate([rows, jnp.zeros((128 - rows.shape[0], LENGTH), f32)], axis=0)
    return padded.T


def spread_heads(columns):
    head = lax.broadcasted_iota(jnp.int32, (128, WIDTH), 0)
    channel = lax.broadcasted_iota(jnp.int32, (128, WIDTH), 1)
    chosen = jnp.where(channel // HEAD == head, 1.0, 0.0).astype(bf16)
    high, middle, low = parts3(columns)
    return dot(high, chosen) + (dot(middle, chosen) + dot(low, chosen))


def convolved(ext, weights):
    total = weights[0:1] * ext[5 : 5 + LENGTH]
    for k in range(1, 4):
        total = total + weights[k : k + 1] * ext[5 + k : 5 + k + LENGTH]
    return silu(total).astype(bf16)


def summary_kernel(
    x_ref, bc_ref, halo_ref, cx_ref, cbc_ref, step_ref, decay_ref,
    message_ref, act_ref, bc_act_ref, cum_ref, ext_x, ext_bc,
):
    halo = halo_ref[...].astype(f32)[8:16]
    ext_x[0:8] = halo[:, :WIDTH]
    ext_bc[0:8] = halo[:, WIDTH:]
    ext_x[8:] = x_ref[...].astype(f32)
    ext_bc[8:] = bc_ref[...].astype(f32)
    bc_act = convolved(ext_bc, cbc_ref)
    bc_act_ref[...] = bc_act
    act = convolved(ext_x, cx_ref)
    act_ref[...] = act

    s_at = lax.broadcasted_iota(jnp.int32, (LENGTH, LENGTH), 0)
    t_at = lax.broadcasted_iota(jnp.int32, (LENGTH, LENGTH), 1)
    upto = jnp.where(s_at <= t_at, 1.0, 0.0).astype(bf16)
    high, middle, low = parts3(decay_ref[...])
    cum = dot(high, upto) + (dot(middle, upto) + dot(low, upto))
    cum_ref[...] = cum
    last = cum[:, LENGTH - 1 : LENGTH]
    factor = step_ref[...] * jnp.exp(last - cum)
    weighted = (act.astype(f32) * spread_heads(columns_of(factor))).astype(bf16)
    b_rows = bc_act[:, :STATE].astype(f32)
    summary = dot(b_rows.T.astype(bf16), weighted)

    total = jnp.broadcast_to(jnp.exp(last), (HEADS, 128))
    low_lanes = lax.broadcasted_iota(jnp.int32, (HEAD, 128), 1) < HEAD
    row_at = lax.broadcasted_iota(jnp.int32, (EXTRA, 128), 0)
    for pair in range(HEADS // 2):
        top = summary[:HEAD, 128 * pair : 128 * (pair + 1)]
        bottom = summary[HEAD:, 128 * pair : 128 * (pair + 1)]
        even = jnp.where(low_lanes, top, pltpu.roll(bottom, HEAD, 1))
        odd = jnp.where(low_lanes, pltpu.roll(top, HEAD, 1), bottom)
        message_ref[2 * pair, 0:HEAD] = even.astype(bf16)
        message_ref[2 * pair + 1, 0:HEAD] = odd.astype(bf16)
    for h in range(HEADS):
        high, middle, low = (p.astype(f32) for p in parts3(total[h : h + 1]))
        rows = jnp.where(row_at == 0, high, jnp.where(row_at == 1, middle, jnp.where(row_at == 2, low, 0.0)))
        message_ref[h, HEAD:] = rows.astype(bf16)


def within_kernel(
    act_ref, bc_act_ref, cum_ref, step_ref, skip_ref, z_ref, local_ref, gate_ref
):
    cum = cum_ref[...]
    cum_columns = columns_of(cum)
    act = act_ref[...].astype(f32)
    scaled = (act * spread_heads(columns_of(step_ref[...]))).astype(bf16)
    gate = silu(z_ref[...].astype(f32))
    gate_ref[...] = gate * spread_heads(jnp.exp(cum_columns))
    b_rows = bc_act_ref[:, :STATE]
    c_rows = bc_act_ref[:, STATE:]
    skipped = skip_ref[...] * act
    t_at = lax.broadcasted_iota(jnp.int32, (BLOCK, BLOCK), 0)
    s_at = lax.broadcasted_iota(jnp.int32, (BLOCK, BLOCK), 1)
    causal = t_at >= s_at
    low_lanes = lax.broadcasted_iota(jnp.int32, (BLOCK, 128), 1) < HEAD
    for block in range(LENGTH // BLOCK):
        rows = slice(block * BLOCK, (block + 1) * BLOCK)
        scores = lax.dot_general(
            c_rows[rows], b_rows[: (block + 1) * BLOCK], (((1,), (1,)), ((), ())), preferred_element_type=f32
        )
        for pair in range(HEADS // 2):
            lanes = slice(128 * pair, 128 * (pair + 1))
            sums = []
            for h in (2 * pair, 2 * pair + 1):
                here = cum_columns[rows, h : h + 1]
                tiles = []
                for other in range(block + 1):
                    columns = slice(other * BLOCK, (other + 1) * BLOCK)
                    spread = here - cum[h : h + 1, columns]
                    if other == block:
                        spread = jnp.where(causal, spread, -jnp.inf)
                    tiles.append((scores[:, columns] * jnp.exp(spread)).astype(bf16))
                mixing = tiles[0] if block == 0 else jnp.concatenate(tiles, axis=1)
                sums.append(dot(mixing, scaled[: (block + 1) * BLOCK, lanes]))
            within = jnp.where(low_lanes, sums[0], sums[1])
            local_ref[rows, lanes] = (within + skipped[rows, lanes]) * gate[rows, lanes]


def prefix_kernel(message_ref, prefix_ref, scale_ref, total_ref):
    state = jnp.zeros((HEAD, 128), f32)
    scale = jnp.ones((8, 128), f32)
    for m in range(GROUP):
        prefix_ref[m] = state
        scale_ref[m] = scale
        rows = message_ref[m, HEAD:].astype(f32)
        decay = rows[0:1] + (rows[1:2] + rows[2:3])
        state = decay * state + message_ref[m, 0:HEAD].astype(f32)
        scale = decay * scale
    total_ref[0:HEAD] = state.astype(bf16)
    row_at = lax.broadcasted_iota(jnp.int32, (EXTRA, 128), 0)
    high, middle, low = (p.astype(f32)[0:1] for p in parts3(scale))
    rows = jnp.where(row_at == 0, high, jnp.where(row_at == 1, middle, jnp.where(row_at == 2, low, 0.0)))
    total_ref[HEAD:] = rows.astype(bf16)


def entering_kernel(prefix_ref, scale_ref, near_ref, next_ref, far_ref, state_ref):
    entering = far_ref[0:HEAD].astype(f32)
    for ref in (next_ref, near_ref):
        rows = ref[HEAD:].astype(f32)
        decay = rows[0:1] + (rows[1:2] + rows[2:3])
        entering = decay * entering + ref[0:HEAD].astype(f32)
    for m in range(GROUP):
        state_ref[m] = (prefix_ref[m] + scale_ref[m, 0:1] * entering).astype(bf16)


def output_kernel(state_ref, bc_act_ref, local_ref, gate_ref, gain_ref, weight_ref, share_ref):
    low_lanes = lax.broadcasted_iota(jnp.int32, (HEAD, 128), 1) < HEAD
    pairs = []
    for pair in range(HEADS // 2):
        even = state_ref[2 * pair].astype(f32)
        odd = state_ref[2 * pair + 1].astype(f32)
        top = jnp.where(low_lanes, even, pltpu.roll(odd, HEAD, 1))
        bottom = jnp.where(low_lanes, pltpu.roll(even, HEAD, 1), odd)
        pairs.append(jnp.concatenate([top, bottom], axis=0).astype(bf16))
    states = jnp.concatenate(pairs, axis=1)
    carried = dot(bc_act_ref[:, STATE:], states)
    gated = local_ref[...] + gate_ref[...] * carried
    squares = jnp.sum(gated * gated, axis=1, keepdims=True)
    scaled = (gated * gain_ref[...]).astype(bf16)
    wide = jnp.broadcast_to(squares, (LENGTH, 128))
    row_at = lax.broadcasted_iota(jnp.int32, (EXTRA, 128), 0)
    extra = jnp.zeros((EXTRA, 128), f32)
    for block in range(LENGTH // BLOCK):
        row = wide[block * BLOCK : (block + 1) * BLOCK].T[0:1]
        for k, part in enumerate(parts3(row)):
            extra = jnp.where(row_at == 3 * block + k, part.astype(f32), extra)
    extra = extra.astype(bf16)
    for pair in range(SHARES // 2):
        product = dot(scaled, weight_ref[:, 256 * pair : 256 * (pair + 1)]).astype(bf16)
        share_ref[2 * pair, 0:LENGTH] = product[:, :128]
        share_ref[2 * pair, LENGTH:] = extra
        share_ref[2 * pair + 1, 0:LENGTH] = product[:, 128:]
        share_ref[2 * pair + 1, LENGTH:] = extra


def sum_kernel(share_ref, out_ref):
    total = share_ref[0].astype(f32)
    for d in range(1, SHARES):
        total = total + share_ref[d].astype(f32)
    extra = total[LENGTH:]
    for block in range(LENGTH // BLOCK):
        rows = slice(block * BLOCK, (block + 1) * BLOCK)
        squares = extra[3 * block : 3 * block + 1] + (
            extra[3 * block + 1 : 3 * block + 2] + extra[3 * block + 2 : 3 * block + 3]
        )
        scale = lax.rsqrt(squares / INNER + 1e-05)
        column = jnp.broadcast_to(scale, (128, 128)).T
        out_ref[rows] = (total[rows] * column).astype(bf16)


def call(kernel, outs, *args, scratch=(), flops=1e8, transcendentals=0):
    whole = pl.BlockSpec(memory_space=pltpu.VMEM)
    return pl.pallas_call(
        kernel,
        out_shape=[jax.ShapeDtypeStruct(s, d) for s, d in outs],
        in_specs=[whole] * len(args),
        out_specs=[whole] * len(outs),
        scratch_shapes=list(scratch),
        compiler_params=pltpu.CompilerParams(vmem_limit_bytes=32 * 1024 * 1024),
        cost_estimate=pl.CostEstimate(
            flops=int(flops), bytes_accessed=2_000_000, transcendentals=int(transcendentals)
        ),
    )(*args)


def shards(
    inner_x, gate_z, bc_input, conv_inner, conv_bc, step_size, log_decay, skip_gain, norm_gain, out_weight
):
    tail = jnp.concatenate([inner_x[LENGTH - 16 :], bc_input[LENGTH - 16 :]], axis=1)
    halo = lax.ppermute(tail, "seq", [(i, i + 1) for i in range(BLOCKS - 1)])
    message, act, bc_act, cum = call(
        summary_kernel,
        [((HEADS, HEAD + EXTRA, 128), bf16), ((LENGTH, WIDTH), bf16), ((LENGTH, 2 * STATE), bf16), ((HEADS, LENGTH), f32)],
        inner_x, bc_input, halo, conv_inner, conv_bc, step_size, log_decay,
        scratch=[pltpu.VMEM((LENGTH + 8, WIDTH), f32), pltpu.VMEM((LENGTH + 8, 2 * STATE), f32)],
    )
    groups = [list(range(i, i + GROUP)) for i in range(0, BLOCKS, GROUP)]
    message = lax.all_to_all(message, "seq", 0, 0, tiled=True, axis_index_groups=groups)
    skip = jnp.repeat(skip_gain, HEAD)[None, :]
    local, gate = call(
        within_kernel,
        [((LENGTH, WIDTH), f32), ((LENGTH, WIDTH), f32)],
        act, bc_act, cum, step_size, skip, gate_z,
        flops=2e9, transcendentals=1.2e6,
    )
    prefix, scale, total = call(
        prefix_kernel,
        [((GROUP, HEAD, 128), f32), ((GROUP, 8, 128), f32), ((HEAD + EXTRA, 128), bf16)],
        message,
    )
    near, after, far = (
        lax.ppermute(total, "seq", [(i, i + d) for i in range(BLOCKS - d)]) for d in (GROUP, 2 * GROUP, 3 * GROUP)
    )
    (state,) = call(entering_kernel, [((GROUP, HEAD, 128), bf16)], prefix, scale, near, after, far)
    state = lax.all_to_all(state, "seq", 0, 0, tiled=True, axis_index_groups=groups)
    (share,) = call(
        output_kernel,
        [((SHARES, LENGTH + EXTRA, 128), bf16)],
        state, bc_act, local, gate, norm_gain[None, :], out_weight,
        flops=9e8,
    )
    share = lax.all_to_all(share, "tp", 0, 0, tiled=True)
    (mixed,) = call(sum_kernel, [((LENGTH, 128), bf16)], share)
    return mixed


def solution(mesh):
    in_specs = (
        P("seq", "tp"),
        P("seq", "tp"),
        P("seq", None),
        P(None, "tp"),
        P(),
        P("tp", "seq"),
        P("tp", "seq"),
        P("tp"),
        P("tp"),
        P("tp", None),
    )
    return jax.shard_map(shards, mesh=mesh, in_specs=in_specs, out_specs=P("seq", "tp"), check_vma=False)
```

time: 278 us -> 91.2 us (0.33)
  waiting for transfers between devices: 144 us -> 5.58 us
  blocking collectives: 83.8 us -> 39 us
  starting transfers between devices: 6.88 us -> 28.7 us
  between operations: 14.1 us -> 0.11 us
  other arithmetic: 9.85 us -> 0.01 us
  matrix products: 8.95 us -> 0 us
  Pallas kernels: 0 us -> 6.73 us
    reduce_scatter x1 -> x0, waiting for transfers between devices: 117 us -> none  [shards(): lax.psum_scatter(lax.dot_general(out_weight, normed, (((0,), (1,)), ((),...]
    unnamed x1 -> x0, blocking collectives: 50.7 us -> none
    all_to_all x0 -> x2, blocking collectives: none -> 39 us  [the longest x1 28.9 us: shards(): share = lax.all_to_all(share, 'tp', 0, 0, tiled=True)]
    psum x1 -> x0, blocking collectives: 33.1 us -> none  [shards(): squares = lax.psum(jnp.sum(gated * gated, axis=1), 'tp')]
    all_gather x1 -> x0, waiting for transfers between devices: 27.8 us -> none  [entering(): gathered = jax.tree.map(lambda a: lax.all_gather(a, axis), part)]
    ppermute x2 -> x4, starting transfers between devices: 6.83 us -> 23 us  [the longest x3 18.1 us: shards(): lax.ppermute(total, 'seq', [(i, i + d) for i in range(BLOCKS - d)])]
    dot_general x5 -> x0, matrix products: 8.95 us -> none  [the longest x1 3.81 us: shards(): lax.dot_general(out_weight, normed, (((0,), (1,)), ((), ())), preferred_e...]
    unnamed x13 -> x30, local copies, waits for them, and re-layouts: 1.51 us -> 8.74 us
  transfers between devices with their start and end apart: 4 -> 5, of which waited for: 2 -> 3; matrix products, arithmetic and copies ran while one was open for 4% -> 0% of each run, Pallas kernels for 0% -> 2%
where the time goes in v1:
time: 91.2 us; the launch traced here: 90.4 us
  blocking collectives  39 us (43%)
  starting transfers between devices  28.7 us (31%)
  local copies, waits for them, and re-layouts  10.3 us (11%)
  Pallas kernels  6.73 us (7%)
  waiting for transfers between devices  5.58 us (6%)
    all_to_all x1, blocking collectives, shards(): share = lax.all_to_all(share, 'tp', 0, 0, tiled=True)  28.9 us
    ppermute x3, starting transfers between devices, shards(): lax.ppermute(total, 'seq', [(i, i + d) for i in range(BLOCKS - d)])  18.1 us
    all_to_all x1, blocking collectives, shards(): lax.all_to_all(message, 'seq', 0, 0, tiled=True, axis_index_groups=groups)  10 us
    unnamed x30, local copies, waits for them, and re-layouts  8.74 us
    pallas_call x6, Pallas kernels, call(): pl.pallas_call(kernel, out_shape=[jax.ShapeDtypeStruct(s, d) for s, d in...  6.73 us
    all_to_all x1, starting transfers between devices, shards(): lax.all_to_all(state, 'seq', 0, 0, tiled=True, axis_index_groups=groups)  5.64 us
    ppermute x1, starting transfers between devices, shards(): halo = lax.ppermute(tail, 'seq', [(i, i + 1) for i in range(BLOCKS - 1)])  4.92 us
    ppermute x1, waiting for transfers between devices, shards(): halo = lax.ppermute(tail, 'seq', [(i, i + 1) for i in range(BLOCKS - 1)])  3.9 us
  transfers between devices with their start and end apart: 5, of which 3 were waited for; matrix products, arithmetic and copies ran while one was open for 0% of the time, Pallas kernels for 2%

profile of v1, /device:TPU:1, one launch (start us, length us, event | category | flops | bytes accessed | tf_op | source)
XLA Modules:
  0.0 90.4 jit_solution(9554910413628739905)
XLA Ops:
  0.0 0.0 copy-start.7
  0.0 0.0 copy-start.14
  0.0 0.7 slice.7
  0.7 0.7 slice.6
  1.5 4.9 %collective-permute-start = (bf16[16,768]{1,0:T(8,128)(2,1)S(1)}, bf16[16,768]{1,0:T(8,128)(2,1)S(1)}, u32[]{:S(2)}, u32[]{:S(2)}) collective-permute-start(bf16[16,768]{1,0:T(8,128)(2,1)S(1)} %pad_maximum_fusion), channel_id=1, source_target_pairs={{0,16},{16,32},{32,48},{48,64},{64,80},{80,96},{96,112},{112,128},... | collective-permute-start | bytes 73736 | tf_op jit(solution)/shard_map/ppermute | solution.py:232
  6.4 3.9 %collective-permute-done.halo_ref = bf16[16,768]{1,0:T(8,128)(2,1)S(1)} collective-permute-done((bf16[16,768]{1,0:T(8,128)(2,1)S(1)}, bf16[16,768]{1,0:T(8,128)(2,1)S(1)}, u32[]{:S(2)}, u32[]{:S(2)}) %collective-permute-start) | collective-permute-done | bytes 24608 | tf_op jit(solution)/shard_map/ppermute | solution.py:232
  10.3 0.0 copy-start.3
  10.3 1.0 %copy-done.3 = bf16[384,512]{1,0:T(8,128)(2,1)S(1)} copy-done((bf16[384,512]{1,0:T(8,128)(2,1)S(1)}, bf16[384,512]{1,0:T(8,128)(2,1)}, u32[]{:S(2)}) %copy-start.3) | copy-done | bytes 393240
  11.3 0.0 copy-start.4
  11.3 0.9 %copy-done.4 = bf16[384,256]{1,0:T(8,128)(2,1)S(1)} copy-done((bf16[384,256]{1,0:T(8,128)(2,1)S(1)}, bf16[384,256]{1,0:T(8,128)(2,1)}, u32[]{:S(2)}) %copy-start.4) | copy-done | bytes 196632
  12.2 0.0 copy-start.5
  12.2 0.7 copy-done.5
  12.9 0.0 copy-start.6
  12.9 0.7 copy-done.6
  13.6 0.0 copy-start.8
  13.6 0.7 copy-done.8
  14.3 0.0 copy-start.9
  14.3 0.7 copy-done.9
  15.0 1.9 %shard_map.100 = (bf16[8,80,128]{2,1,0:T(8,128)(2,1)S(1)}, bf16[384,512]{1,0:T(8,128)(2,1)S(1)}, bf16[384,256]{1,0:T(8,128)(2,1)S(1)}, f32[8,384]{1,0:T(8,128)S(1)}) custom-call(bf16[384,512]{1,0:T(8,128)(2,1)S(1)} %copy-done.3, bf16[384,256]{1,0:T(8,128)(2,1)S(1)} %copy-done.4, bf16[16,768]{1,0:T(8,128)(2,1)S(1)} %collective-permute-done.halo_ref, ...), custom_call_target="tpu_custom_call" | custom-call | flops 100000000 | bytes 2000000 | tf_op jit(solution)/shard_map/pallas_call | solution.py:215
  17.0 0.0 copy-start.12
  17.0 10.0 %all_to_all.15.message_ref = bf16[8,80,128]{2,1,0:T(8,128)(2,1)S(1)} all-to-all(bf16[8,80,128]{2,1,0:T(8,128)(2,1)S(1)} %get-tuple-element.14), channel_id=1, replica_groups={{0,16,32,48,64,80,96,112},{128,144,160,176,192,208,224,240},{256,272,28..., dimensions={0} | all-to-all | bytes 327680 | tf_op jit(solution)/shard_map/all_to_all | solution.py:240
  27.0 9.8 %collective-permute-start.3 = (bf16[80,128]{1,0:T(8,128)(2,1)S(1)}, bf16[80,128]{1,0:T(8,128)(2,1)S(1)}, u32[]{:S(2)}, u32[]{:S(2)}) collective-permute-start(bf16[80,128]{1,0:T(8,128)(2,1)S(1)} %get-tuple-element.17), channel_id=1, source_target_pairs={{0,384},{16,400},{32,416},{48,432},{64,448},{80,464},{96,480},{112... | collective-permute-start | bytes 61448 | tf_op jit(solution)/shard_map/ppermute | solution.py:254
  36.9 3.7 %collective-permute-start.2 = (bf16[80,128]{1,0:T(8,128)(2,1)S(1)}, bf16[80,128]{1,0:T(8,128)(2,1)S(1)}, u32[]{:S(2)}, u32[]{:S(2)}) collective-permute-start(bf16[80,128]{1,0:T(8,128)(2,1)S(1)} %get-tuple-element.17), channel_id=1, source_target_pairs={{0,256},{16,272},{32,288},{48,304},{64,320},{80,336},{96,352},{112... | collective-permute-start | bytes 61448 | tf_op jit(solution)/shard_map/ppermute | solution.py:254
  40.5 4.6 %collective-permute-start.1 = (bf16[80,128]{1,0:T(8,128)(2,1)S(1)}, bf16[80,128]{1,0:T(8,128)(2,1)S(1)}, u32[]{:S(2)}, u32[]{:S(2)}) collective-permute-start(bf16[80,128]{1,0:T(8,128)(2,1)S(1)} %get-tuple-element.17), channel_id=1, source_target_pairs={{0,128},{16,144},{32,160},{48,176},{64,192},{80,208},{96,224},{112... | collective-permute-start | bytes 61448 | tf_op jit(solution)/shard_map/ppermute | solution.py:254
  45.2 0.0 collective-permute-done.3.far_ref
  45.2 0.0 collective-permute-done.2.next_ref
  45.2 0.9 collective-permute-done.1.near_ref
  46.1 0.0 copy-done.12
  46.1 0.7 shard_map.102
  46.8 5.6 %all-to-all-start.1 = ((bf16[8,64,128]{2,1,0:T(8,128)(2,1)}), bf16[8,64,128]{2,1,0:T(8,128)(2,1)S(1)}, u32[]{:S(2)}, u32[]{:S(2)}) async-start(bf16[8,64,128]{2,1,0:T(8,128)(2,1)} %shard_map.102), calls=%async_computation.1 | async-start | bytes 262144 | tf_op jit(solution)/shard_map/all_to_all | solution.py:257
  52.4 0.0 copy-done.14
  52.4 0.1 broadcast_in_dim.6
  52.5 0.1 broadcast_in_dim_reshape.3.skip_ref
  52.6 0.0 copy-done.7
  52.6 0.0 copy-start.11
  52.6 1.0 %copy-done.11 = bf16[384,512]{1,0:T(8,128)(2,1)S(1)} copy-done((bf16[384,512]{1,0:T(8,128)(2,1)S(1)}, bf16[384,512]{1,0:T(8,128)(2,1)}, u32[]{:S(2)}) %copy-start.11) | copy-done | bytes 393240
  53.6 0.0 copy-start.13
  53.6 1.0 %copy-done.13 = bf16[384,512]{1,0:T(8,128)(2,1)S(1)} copy-done((bf16[384,512]{1,0:T(8,128)(2,1)S(1)}, bf16[384,512]{1,0:T(8,128)(2,1)}, u32[]{:S(2)}) %copy-start.13) | copy-done | bytes 393240
  54.6 2.0 %shard_map.103 = (f32[384,512]{1,0:T(8,128)S(1)}, f32[384,512]{1,0:T(8,128)S(1)}) custom-call(bf16[384,512]{1,0:T(8,128)(2,1)S(1)} %copy-done.13, bf16[384,256]{1,0:T(8,128)(2,1)S(1)} %get-tuple-element.18.bc_act_ref, f32[8,384]{1,0:T(8,128)S(1)} %get-tuple-element.20.cum_ref, f32[8,384]{1,0:T(8,128)S(1)} %copy-done.7, ...), custom_call_target="tpu_custom_call" | custom-call | flops 2000000000 | bytes 2000000 | tf_op jit(solution)/shard_map/pallas_call | solution.py:215
  56.5 0.0 copy-start.1
  56.6 0.9 copy-done.1
  57.4 0.8 all-to-all-done.1.state_ref
  58.2 0.0 copy-done
  58.2 0.0 copy-done.10
  58.2 1.1 %copy-done.2 = f32[384,512]{1,0:T(8,128)S(1)} copy-done((f32[384,512]{1,0:T(8,128)S(1)}, f32[384,512]{1,0:T(8,128)}, u32[]{:S(2)}) %copy-start.2) | copy-done | bytes 786456
  59.4 1.2 %shard_map.104 = bf16[16,400,128]{2,1,0:T(8,128)(2,1)S(1)} custom-call(bf16[8,64,128]{2,1,0:T(8,128)(2,1)S(1)} %all-to-all-done.1.state_ref, bf16[384,256]{1,0:T(8,128)(2,1)S(1)} %get-tuple-element.18.bc_act_ref, f32[384,512]{1,0:T(8,128)S(1)} %get-tuple-element.21.local_ref, f32[384,512]{1,0:T(8,128)S(1)} %copy-done.2, f32[1,512]{1,0:T(1,128)S(1)} %bitcast.1, ...), custom_call_target="tpu_custom_call" | custom-call | flops 900000000 | bytes 2000000 | tf_op jit(solution)/shard_map/pallas_call | solution.py:215
  60.6 28.9 %all_to_all.16.share_ref = bf16[16,400,128]{2,1,0:T(8,128)(2,1)S(1)} all-to-all(bf16[16,400,128]{2,1,0:T(8,128)(2,1)S(1)} %shard_map.104), channel_id=1, replica_groups=mesh['seq'=32,'tp'=16] {'tp'}, dimensions={0} | all-to-all | bytes 3276800 | tf_op jit(solution)/shard_map/all_to_all | solution.py:264
  89.5 0.9 shard_map.105
  (5 shorter events, 0.1 us)
Async XLA Ops:
  0.0 52.6 %copy-start.7 = (f32[8,384]{1,0:T(8,128)S(1)}, f32[8,384]{1,0:T(8,128)}, u32[]{:S(2)}) copy-start(f32[8,384]{1,0:T(8,128)} %step_ref.3) | copy-start | bytes 36868
  0.0 52.4 %copy-start.14 = (f32[8]{0:T(128)S(1)}, f32[8]{0:T(128)}, u32[]{:S(2)}) copy-start(f32[8]{0:T(128)} %param.17) | copy-start | bytes 100
  1.5 8.8 %collective-permute-start = (bf16[16,768]{1,0:T(8,128)(2,1)S(1)}, bf16[16,768]{1,0:T(8,128)(2,1)S(1)}, u32[]{:S(2)}, u32[]{:S(2)}) collective-permute-start(bf16[16,768]{1,0:T(8,128)(2,1)S(1)} %pad_maximum_fusion), channel_id=1, source_target_pairs={{0,16},{16,32},{32,48},{48,64},{64,80},{80,96},{96,112},{112,128},... | collective-permute-start | bytes 73736 | tf_op jit(solution)/shard_map/ppermute | solution.py:232
  10.3 1.0 %copy-start.3 = (bf16[384,512]{1,0:T(8,128)(2,1)S(1)}, bf16[384,512]{1,0:T(8,128)(2,1)}, u32[]{:S(2)}) copy-start(bf16[384,512]{1,0:T(8,128)(2,1)} %x_ref.1) | copy-start | bytes 1179652
  11.3 0.9 %copy-start.4 = (bf16[384,256]{1,0:T(8,128)(2,1)S(1)}, bf16[384,256]{1,0:T(8,128)(2,1)}, u32[]{:S(2)}) copy-start(bf16[384,256]{1,0:T(8,128)(2,1)} %bc_ref.1) | copy-start | bytes 589828
  12.2 0.7 copy-start.5
  12.9 0.7 copy-start.6
  13.6 0.7 copy-start.8
  14.3 0.7 copy-start.9
  17.0 29.1 %copy-start.12 = (bf16[384,512]{1,0:T(8,128)(2,1)}, bf16[384,512]{1,0:T(8,128)(2,1)S(1)}, u32[]{:S(2)}) copy-start(bf16[384,512]{1,0:T(8,128)(2,1)S(1)} %get-tuple-element.19.act_ref) | copy-start | bytes 1179652
  27.0 18.1 %collective-permute-start.3 = (bf16[80,128]{1,0:T(8,128)(2,1)S(1)}, bf16[80,128]{1,0:T(8,128)(2,1)S(1)}, u32[]{:S(2)}, u32[]{:S(2)}) collective-permute-start(bf16[80,128]{1,0:T(8,128)(2,1)S(1)} %get-tuple-element.17), channel_id=1, source_target_pairs={{0,384},{16,400},{32,416},{48,432},{64,448},{80,464},{96,480},{112... | collective-permute-start | bytes 61448 | tf_op jit(solution)/shard_map/ppermute | solution.py:254
  36.9 8.3 %collective-permute-start.2 = (bf16[80,128]{1,0:T(8,128)(2,1)S(1)}, bf16[80,128]{1,0:T(8,128)(2,1)S(1)}, u32[]{:S(2)}, u32[]{:S(2)}) collective-permute-start(bf16[80,128]{1,0:T(8,128)(2,1)S(1)} %get-tuple-element.17), channel_id=1, source_target_pairs={{0,256},{16,272},{32,288},{48,304},{64,320},{80,336},{96,352},{112... | collective-permute-start | bytes 61448 | tf_op jit(solution)/shard_map/ppermute | solution.py:254
  40.5 5.5 %collective-permute-start.1 = (bf16[80,128]{1,0:T(8,128)(2,1)S(1)}, bf16[80,128]{1,0:T(8,128)(2,1)S(1)}, u32[]{:S(2)}, u32[]{:S(2)}) collective-permute-start(bf16[80,128]{1,0:T(8,128)(2,1)S(1)} %get-tuple-element.17), channel_id=1, source_target_pairs={{0,128},{16,144},{32,160},{48,176},{64,192},{80,208},{96,224},{112... | collective-permute-start | bytes 61448 | tf_op jit(solution)/shard_map/ppermute | solution.py:254
  46.8 11.5 %all-to-all-start.1 = ((bf16[8,64,128]{2,1,0:T(8,128)(2,1)}), bf16[8,64,128]{2,1,0:T(8,128)(2,1)S(1)}, u32[]{:S(2)}, u32[]{:S(2)}) async-start(bf16[8,64,128]{2,1,0:T(8,128)(2,1)} %shard_map.102), calls=%async_computation.1 | async-start | bytes 262144 | tf_op jit(solution)/shard_map/all_to_all | solution.py:257
  52.6 1.0 %copy-start.11 = (bf16[384,512]{1,0:T(8,128)(2,1)S(1)}, bf16[384,512]{1,0:T(8,128)(2,1)}, u32[]{:S(2)}) copy-start(bf16[384,512]{1,0:T(8,128)(2,1)} %z_ref.1) | copy-start | bytes 1179652
  53.6 1.0 %copy-start.13 = (bf16[384,512]{1,0:T(8,128)(2,1)S(1)}, bf16[384,512]{1,0:T(8,128)(2,1)}, u32[]{:S(2)}) copy-start(bf16[384,512]{1,0:T(8,128)(2,1)} %copy-done.12) | copy-start | bytes 1179652
  54.5 3.7 %copy-start = (bf16[512,2048]{1,0:T(8,128)(2,1)S(1)}, bf16[512,2048]{1,0:T(8,128)(2,1)}, u32[]{:S(2)}) copy-start(bf16[512,2048]{1,0:T(8,128)(2,1)} %weight_ref.1) | copy-start | bytes 6291460
  54.5 3.7 %copy-start.10 = (f32[512]{0:T(512)S(1)}, f32[512]{0:T(512)}, u32[]{:S(2)}) copy-start(f32[512]{0:T(512)} %param.18) | copy-start | bytes 6148
  56.5 0.9 copy-start.1
  58.2 1.1 %copy-start.2 = (f32[384,512]{1,0:T(8,128)S(1)}, f32[384,512]{1,0:T(8,128)}, u32[]{:S(2)}) copy-start(f32[384,512]{1,0:T(8,128)} %copy-done.1) | copy-start | bytes 2359300

commit v2 on v1

--- a/solution.py
+++ b/solution.py
@@ -57,10 +57,23 @@
     return silu(total).astype(bf16)
 
 
+def fetch(pairs, sems):
+    copies = [pltpu.make_async_copy(there, here, sems.at[i]) for i, (there, here) in enumerate(pairs)]
+    for copy in copies:
+        copy.start()
+    return copies
+
+
 def summary_kernel(
-    x_ref, bc_ref, halo_ref, cx_ref, cbc_ref, step_ref, decay_ref,
-    message_ref, act_ref, bc_act_ref, cum_ref, ext_x, ext_bc,
+    x_at, bc_at, halo_ref, cx_at, cbc_at, step_at, decay_at,
+    message_ref, act_ref, bc_act_ref, cum_ref,
+    ext_x, ext_bc, x_ref, bc_ref, cx_ref, cbc_ref, step_ref, decay_ref, sems,
 ):
+    for copy in fetch(
+        [(decay_at, decay_ref), (step_at, step_ref), (cx_at, cx_ref), (cbc_at, cbc_ref), (bc_at, bc_ref), (x_at, x_ref)],
+        sems,
+    ):
+        copy.wait()
     halo = halo_ref[...].astype(f32)[8:16]
     ext_x[0:8] = halo[:, :WIDTH]
     ext_bc[0:8] = halo[:, WIDTH:]
@@ -100,8 +113,15 @@
 
 
 def within_kernel(
-    act_ref, bc_act_ref, cum_ref, step_ref, skip_ref, z_ref, local_ref, gate_ref
+    act_ref, bc_act_ref, cum_ref, step_at, skip_ref, z_at, gain_at, local_ref, gate_ref, gain_ref,
+    step_ref, z_ref, sems,
 ):
+    for copy in fetch([(step_at, step_ref), (z_at, z_ref), (gain_at, gain_ref)], sems):
+        copy.wait()
+    head_at = lax.broadcasted_iota(jnp.int32, (1, WIDTH), 1) // HEAD
+    skip = jnp.zeros((1, WIDTH), f32)
+    for h in range(HEADS):
+        skip = jnp.where(head_at == h, skip_ref[h], skip)
     cum = cum_ref[...]
     cum_columns = columns_of(cum)
     act = act_ref[...].astype(f32)
@@ -110,7 +130,7 @@
     gate_ref[...] = gate * spread_heads(jnp.exp(cum_columns))
     b_rows = bc_act_ref[:, :STATE]
     c_rows = bc_act_ref[:, STATE:]
-    skipped = skip_ref[...] * act
+    skipped = skip * act
     t_at = lax.broadcasted_iota(jnp.int32, (BLOCK, BLOCK), 0)
     s_at = lax.broadcasted_iota(jnp.int32, (BLOCK, BLOCK), 1)
     causal = t_at >= s_at
@@ -155,7 +175,7 @@
     total_ref[HEAD:] = rows.astype(bf16)
 
 
-def entering_kernel(prefix_ref, scale_ref, near_ref, next_ref, far_ref, state_ref):
+def entering_kernel(prefix_ref, scale_ref, far_ref, near_ref, next_ref, state_ref):
     entering = far_ref[0:HEAD].astype(f32)
     for ref in (next_ref, near_ref):
         rows = ref[HEAD:].astype(f32)
@@ -210,19 +230,27 @@
         out_ref[rows] = (total[rows] * column).astype(bf16)
 
 
-def call(kernel, outs, *args, scratch=(), flops=1e8, transcendentals=0):
-    whole = pl.BlockSpec(memory_space=pltpu.VMEM)
+HERE = pl.BlockSpec(memory_space=pltpu.VMEM)
+SCALARS = pl.BlockSpec(memory_space=pltpu.SMEM)
+THERE = pl.BlockSpec(memory_space=pltpu.HBM)
+
+
+def stay(a):
+    return pltpu.with_memory_space_constraint(a, pltpu.HBM)
+
+
+def call(kernel, outs, *args, specs=None, scratch=(), flops=1e8, transcendentals=0):
     return pl.pallas_call(
         kernel,
         out_shape=[jax.ShapeDtypeStruct(s, d) for s, d in outs],
-        in_specs=[whole] * len(args),
-        out_specs=[whole] * len(outs),
+        in_specs=specs or [HERE] * len(args),
+        out_specs=[HERE] * len(outs),
         scratch_shapes=list(scratch),
         compiler_params=pltpu.CompilerParams(vmem_limit_bytes=32 * 1024 * 1024),
         cost_estimate=pl.CostEstimate(
             flops=int(flops), bytes_accessed=2_000_000, transcendentals=int(transcendentals)
         ),
-    )(*args)
+    )(*(stay(a) if spec is THERE else a for a, spec in zip(args, specs or [HERE] * len(args))))
 
 
 def shards(
@@ -234,31 +262,41 @@
         summary_kernel,
         [((HEADS, HEAD + EXTRA, 128), bf16), ((LENGTH, WIDTH), bf16), ((LENGTH, 2 * STATE), bf16), ((HEADS, LENGTH), f32)],
         inner_x, bc_input, halo, conv_inner, conv_bc, step_size, log_decay,
-        scratch=[pltpu.VMEM((LENGTH + 8, WIDTH), f32), pltpu.VMEM((LENGTH + 8, 2 * STATE), f32)],
+        specs=[THERE, THERE, HERE, THERE, THERE, THERE, THERE],
+        scratch=[
+            pltpu.VMEM((LENGTH + 8, WIDTH), f32), pltpu.VMEM((LENGTH + 8, 2 * STATE), f32),
+            pltpu.VMEM((LENGTH, WIDTH), bf16), pltpu.VMEM((LENGTH, 2 * STATE), bf16),
+            pltpu.VMEM((4, WIDTH), f32), pltpu.VMEM((4, 2 * STATE), f32),
+            pltpu.VMEM((HEADS, LENGTH), f32), pltpu.VMEM((HEADS, LENGTH), f32),
+            pltpu.SemaphoreType.DMA((6,)),
+        ],
     )
     groups = [list(range(i, i + GROUP)) for i in range(0, BLOCKS, GROUP)]
     message = lax.all_to_all(message, "seq", 0, 0, tiled=True, axis_index_groups=groups)
-    skip = jnp.repeat(skip_gain, HEAD)[None, :]
-    local, gate = call(
-        within_kernel,
-        [((LENGTH, WIDTH), f32), ((LENGTH, WIDTH), f32)],
-        act, bc_act, cum, step_size, skip, gate_z,
-        flops=2e9, transcendentals=1.2e6,
-    )
     prefix, scale, total = call(
         prefix_kernel,
         [((GROUP, HEAD, 128), f32), ((GROUP, 8, 128), f32), ((HEAD + EXTRA, 128), bf16)],
         message,
     )
-    near, after, far = (
-        lax.ppermute(total, "seq", [(i, i + d) for i in range(BLOCKS - d)]) for d in (GROUP, 2 * GROUP, 3 * GROUP)
-    )
-    (state,) = call(entering_kernel, [((GROUP, HEAD, 128), bf16)], prefix, scale, near, after, far)
+    local, gate, gain = call(
+        within_kernel,
+        [((LENGTH, WIDTH), f32), ((LENGTH, WIDTH), f32), ((1, WIDTH), f32)],
+        act, bc_act, cum, step_size, skip_gain, gate_z, norm_gain[None, :],
+        specs=[HERE, HERE, HERE, THERE, SCALARS, THERE, THERE],
+        scratch=[pltpu.VMEM((HEADS, LENGTH), f32), pltpu.VMEM((LENGTH, WIDTH), bf16), pltpu.SemaphoreType.DMA((3,))],
+        flops=2e9, transcendentals=1.2e6,
+    )
+
+    def later(distance):
+        return lax.ppermute(total, "seq", [(i, i + distance) for i in range(BLOCKS - distance)])
+
+    far, near, after = later(3 * GROUP), later(GROUP), later(2 * GROUP)
+    (state,) = call(entering_kernel, [((GROUP, HEAD, 128), bf16)], prefix, scale, far, near, after)
     state = lax.all_to_all(state, "seq", 0, 0, tiled=True, axis_index_groups=groups)
     (share,) = call(
         output_kernel,
         [((SHARES, LENGTH + EXTRA, 128), bf16)],
-        state, bc_act, local, gate, norm_gain[None, :], out_weight,
+        state, bc_act, local, gate, gain, out_weight,
         flops=9e8,
     )
     share = lax.all_to_all(share, "tp", 0, 0, tiled=True)

time: 91.2 us -> 88.2 us (0.967)
  local copies, waits for them, and re-layouts: 10.3 us -> 5.2 us
  Pallas kernels: 6.73 us -> 9.58 us
    unnamed x30 -> x12, local copies, waits for them, and re-layouts: 8.74 us -> 3.78 us
    pallas_call x6, Pallas kernels: 6.73 us -> 9.58 us  [call(): pl.pallas_call(kernel, out_shape=[jax.ShapeDtypeStruct(s, d) for s, d in...]
  transfers between devices with their start and end apart: 5 -> 5, of which waited for: 3 -> 3; matrix products, arithmetic and copies ran while one was open for 0% -> 0% of each run, Pallas kernels for 2% -> 4%
where the time goes in v2:
time: 88.2 us; the launch traced here: 87.6 us
  blocking collectives  39 us (44%)
  starting transfers between devices  28.7 us (33%)
  Pallas kernels  9.58 us (11%)
  local copies, waits for them, and re-layouts  5.2 us (6%)
  waiting for transfers between devices  5.05 us (6%)
    all_to_all x1, blocking collectives, shards(): share = lax.all_to_all(share, 'tp', 0, 0, tiled=True)  28.9 us
    ppermute x3, starting transfers between devices, later(): lax.ppermute(total, 'seq', [(i, i + distance) for i in range(BLOCKS - dis...  18.1 us
    all_to_all x1, blocking collectives, shards(): lax.all_to_all(message, 'seq', 0, 0, tiled=True, axis_index_groups=groups)  10 us
    pallas_call x6, Pallas kernels, call(): pl.pallas_call(kernel, out_shape=[jax.ShapeDtypeStruct(s, d) for s, d in...  9.58 us
    all_to_all x1, starting transfers between devices, shards(): lax.all_to_all(state, 'seq', 0, 0, tiled=True, axis_index_groups=groups)  5.64 us
    ppermute x1, starting transfers between devices, shards(): halo = lax.ppermute(tail, 'seq', [(i, i + 1) for i in range(BLOCKS - 1)])  4.92 us
    ppermute x1, waiting for transfers between devices, shards(): halo = lax.ppermute(tail, 'seq', [(i, i + 1) for i in range(BLOCKS - 1)])  3.9 us
    unnamed x12, local copies, waits for them, and re-layouts  3.78 us
  transfers between devices with their start and end apart: 5, of which 3 were waited for; matrix products, arithmetic and copies ran while one was open for 0% of the time, Pallas kernels for 4%

profile of v2, /device:TPU:1, one launch (start us, length us, event | category | flops | bytes accessed | tf_op | source)
XLA Modules:
  0.0 87.6 jit_solution(8898165958195969215)
XLA Ops:
  0.0 0.0 copy-start.5
  0.0 0.7 slice.7
  0.7 0.7 slice.6
  1.4 4.9 %collective-permute-start = (bf16[16,768]{1,0:T(8,128)(2,1)S(1)}, bf16[16,768]{1,0:T(8,128)(2,1)S(1)}, u32[]{:S(2)}, u32[]{:S(2)}) collective-permute-start(bf16[16,768]{1,0:T(8,128)(2,1)S(1)} %pad_maximum_fusion), channel_id=1, source_target_pairs={{0,16},{16,32},{32,48},{48,64},{64,80},{80,96},{96,112},{112,128},... | collective-permute-start | bytes 73736 | tf_op jit(solution)/shard_map/ppermute | solution.py:260
  6.4 3.9 %collective-permute-done.halo_ref = bf16[16,768]{1,0:T(8,128)(2,1)S(1)} collective-permute-done((bf16[16,768]{1,0:T(8,128)(2,1)S(1)}, bf16[16,768]{1,0:T(8,128)(2,1)S(1)}, u32[]{:S(2)}, u32[]{:S(2)}) %collective-permute-start) | collective-permute-done | bytes 24608 | tf_op jit(solution)/shard_map/ppermute | solution.py:260
  10.3 3.2 %shard_map.100 = (bf16[8,80,128]{2,1,0:T(8,128)(2,1)S(1)}, bf16[384,512]{1,0:T(8,128)(2,1)S(1)}, bf16[384,256]{1,0:T(8,128)(2,1)S(1)}, f32[8,384]{1,0:T(8,128)S(1)}) custom-call(bf16[384,512]{1,0:T(8,128)(2,1)} %x_at.1, bf16[384,256]{1,0:T(8,128)(2,1)} %bc_at.1, bf16[16,768]{1,0:T(8,128)(2,1)S(1)} %collective-permute-done.halo_ref, f32[4,512]{1,0:T(4,128)} %cx_at.1, ...), custom_call_target="tpu_custom_call" | custom-call | flops 100000000 | bytes 2000000 | tf_op jit(solution)/shard_map/pallas_call | solution.py:243
  13.4 0.0 copy-start.3
  13.4 0.7 copy-done.3
  14.2 10.0 %all_to_all.15.message_ref = bf16[8,80,128]{2,1,0:T(8,128)(2,1)S(1)} all-to-all(bf16[8,80,128]{2,1,0:T(8,128)(2,1)S(1)} %get-tuple-element.15), channel_id=1, replica_groups={{0,16,32,48,64,80,96,112},{128,144,160,176,192,208,224,240},{256,272,28..., dimensions={0} | all-to-all | bytes 327680 | tf_op jit(solution)/shard_map/all_to_all | solution.py:275
  24.2 12.8 %collective-permute-start.3 = (bf16[80,128]{1,0:T(8,128)(2,1)S(1)}, bf16[80,128]{1,0:T(8,128)(2,1)S(1)}, u32[]{:S(2)}, u32[]{:S(2)}) collective-permute-start(bf16[80,128]{1,0:T(8,128)(2,1)S(1)} %get-tuple-element.18), channel_id=1, source_target_pairs={{0,256},{16,272},{32,288},{48,304},{64,320},{80,336},{96,352},{112... | collective-permute-start | bytes 61448 | tf_op jit(solution)/shard_map/ppermute | solution.py:291
  37.0 4.0 %collective-permute-start.2 = (bf16[80,128]{1,0:T(8,128)(2,1)S(1)}, bf16[80,128]{1,0:T(8,128)(2,1)S(1)}, u32[]{:S(2)}, u32[]{:S(2)}) collective-permute-start(bf16[80,128]{1,0:T(8,128)(2,1)S(1)} %get-tuple-element.18), channel_id=1, source_target_pairs={{0,128},{16,144},{32,160},{48,176},{64,192},{80,208},{96,224},{112... | collective-permute-start | bytes 61448 | tf_op jit(solution)/shard_map/ppermute | solution.py:291
  41.1 1.3 %collective-permute-start.1 = (bf16[80,128]{1,0:T(8,128)(2,1)S(1)}, bf16[80,128]{1,0:T(8,128)(2,1)S(1)}, u32[]{:S(2)}, u32[]{:S(2)}) collective-permute-start(bf16[80,128]{1,0:T(8,128)(2,1)S(1)} %get-tuple-element.18), channel_id=1, source_target_pairs={{0,384},{16,400},{32,416},{48,432},{64,448},{80,464},{96,480},{112... | collective-permute-start | bytes 61448 | tf_op jit(solution)/shard_map/ppermute | solution.py:291
  42.4 0.0 collective-permute-done.3.next_ref
  42.4 0.0 collective-permute-done.2.near_ref
  42.4 0.9 collective-permute-done.1.far_ref
  43.3 0.7 shard_map.102
  43.9 5.6 %all-to-all-start.1 = ((bf16[8,64,128]{2,1,0:T(8,128)(2,1)}), bf16[8,64,128]{2,1,0:T(8,128)(2,1)S(1)}, u32[]{:S(2)}, u32[]{:S(2)}) async-start(bf16[8,64,128]{2,1,0:T(8,128)(2,1)} %shard_map.102), calls=%async_computation.1 | async-start | bytes 262144 | tf_op jit(solution)/shard_map/all_to_all | solution.py:295
  49.6 0.0 copy-done.5
  49.6 0.0 copy-start.4
  49.6 1.0 %copy-done.4 = bf16[384,512]{1,0:T(8,128)(2,1)S(1)} copy-done((bf16[384,512]{1,0:T(8,128)(2,1)S(1)}, bf16[384,512]{1,0:T(8,128)(2,1)}, u32[]{:S(2)}) %copy-start.4) | copy-done | bytes 393240
  50.6 0.0 copy-start
  50.6 3.6 %shard_map.103 = (f32[384,512]{1,0:T(8,128)S(1)}, f32[384,512]{1,0:T(8,128)S(1)}, f32[1,512]{1,0:T(1,128)S(1)}) custom-call(bf16[384,512]{1,0:T(8,128)(2,1)S(1)} %copy-done.4, bf16[384,256]{1,0:T(8,128)(2,1)S(1)} %get-tuple-element.19.bc_act_ref, f32[8,384]{1,0:T(8,128)S(1)} %get-tuple-element.21.cum_ref, f32[8,384]{1,0:T(8,128)} %step_at.3, ...), custom_call_target="tpu_custom_call" | custom-call | flops 2000000000 | bytes 2000000 | tf_op jit(solution)/shard_map/pallas_call | solution.py:243
  54.2 0.0 copy-start.1
  54.2 0.9 %copy-done.1 = f32[384,512]{1,0:T(8,128)} copy-done((f32[384,512]{1,0:T(8,128)}, f32[384,512]{1,0:T(8,128)S(1)}, u32[]{:S(2)}) %copy-start.1) | copy-done | bytes 786456
  55.1 0.3 all-to-all-done.1.state_ref
  55.4 0.0 copy-done
  55.4 0.0 copy-start.2
  55.4 1.1 %copy-done.2 = f32[384,512]{1,0:T(8,128)S(1)} copy-done((f32[384,512]{1,0:T(8,128)S(1)}, f32[384,512]{1,0:T(8,128)}, u32[]{:S(2)}) %copy-start.2) | copy-done | bytes 786456
  56.6 1.2 %shard_map.104 = bf16[16,400,128]{2,1,0:T(8,128)(2,1)S(1)} custom-call(bf16[8,64,128]{2,1,0:T(8,128)(2,1)S(1)} %all-to-all-done.1.state_ref, bf16[384,256]{1,0:T(8,128)(2,1)S(1)} %get-tuple-element.19.bc_act_ref, f32[384,512]{1,0:T(8,128)S(1)} %get-tuple-element.22.local_ref, f32[384,512]{1,0:T(8,128)S(1)} %copy-done.2, ...), custom_call_target="tpu_custom_call" | custom-call | flops 900000000 | bytes 2000000 | tf_op jit(solution)/shard_map/pallas_call | solution.py:243
  57.8 28.9 %all_to_all.16.share_ref = bf16[16,400,128]{2,1,0:T(8,128)(2,1)S(1)} all-to-all(bf16[16,400,128]{2,1,0:T(8,128)(2,1)S(1)} %shard_map.104), channel_id=1, replica_groups=mesh['seq'=32,'tp'=16] {'tp'}, dimensions={0} | all-to-all | bytes 3276800 | tf_op jit(solution)/shard_map/all_to_all | solution.py:302
  86.7 0.9 %shard_map.105 = bf16[384,128]{1,0:T(8,128)(2,1)} custom-call(bf16[16,400,128]{2,1,0:T(8,128)(2,1)S(1)} %all_to_all.16.share_ref), custom_call_target="tpu_custom_call" | custom-call | flops 100000000 | bytes 2000000 | tf_op jit(solution)/shard_map/pallas_call | solution.py:243
  (2 shorter events, 0.1 us)
Async XLA Ops:
  0.0 49.6 %copy-start.5 = (f32[8]{0:T(128)S(1)}, f32[8]{0:T(128)}, u32[]{:S(2)}) copy-start(f32[8]{0:T(128)} %skip_ref.1) | copy-start | bytes 100
  1.4 8.8 %collective-permute-start = (bf16[16,768]{1,0:T(8,128)(2,1)S(1)}, bf16[16,768]{1,0:T(8,128)(2,1)S(1)}, u32[]{:S(2)}, u32[]{:S(2)}) collective-permute-start(bf16[16,768]{1,0:T(8,128)(2,1)S(1)} %pad_maximum_fusion), channel_id=1, source_target_pairs={{0,16},{16,32},{32,48},{48,64},{64,80},{80,96},{96,112},{112,128},... | collective-permute-start | bytes 73736 | tf_op jit(solution)/shard_map/ppermute | solution.py:260
  13.4 0.7 copy-start.3
  24.2 18.1 %collective-permute-start.3 = (bf16[80,128]{1,0:T(8,128)(2,1)S(1)}, bf16[80,128]{1,0:T(8,128)(2,1)S(1)}, u32[]{:S(2)}, u32[]{:S(2)}) collective-permute-start(bf16[80,128]{1,0:T(8,128)(2,1)S(1)} %get-tuple-element.18), channel_id=1, source_target_pairs={{0,256},{16,272},{32,288},{48,304},{64,320},{80,336},{96,352},{112... | collective-permute-start | bytes 61448 | tf_op jit(solution)/shard_map/ppermute | solution.py:291
  37.0 5.3 %collective-permute-start.2 = (bf16[80,128]{1,0:T(8,128)(2,1)S(1)}, bf16[80,128]{1,0:T(8,128)(2,1)S(1)}, u32[]{:S(2)}, u32[]{:S(2)}) collective-permute-start(bf16[80,128]{1,0:T(8,128)(2,1)S(1)} %get-tuple-element.18), channel_id=1, source_target_pairs={{0,128},{16,144},{32,160},{48,176},{64,192},{80,208},{96,224},{112... | collective-permute-start | bytes 61448 | tf_op jit(solution)/shard_map/ppermute | solution.py:291
  41.1 2.2 %collective-permute-start.1 = (bf16[80,128]{1,0:T(8,128)(2,1)S(1)}, bf16[80,128]{1,0:T(8,128)(2,1)S(1)}, u32[]{:S(2)}, u32[]{:S(2)}) collective-permute-start(bf16[80,128]{1,0:T(8,128)(2,1)S(1)} %get-tuple-element.18), channel_id=1, source_target_pairs={{0,384},{16,400},{32,416},{48,432},{64,448},{80,464},{96,480},{112... | collective-permute-start | bytes 61448 | tf_op jit(solution)/shard_map/ppermute | solution.py:291
  43.9 11.5 %all-to-all-start.1 = ((bf16[8,64,128]{2,1,0:T(8,128)(2,1)}), bf16[8,64,128]{2,1,0:T(8,128)(2,1)S(1)}, u32[]{:S(2)}, u32[]{:S(2)}) async-start(bf16[8,64,128]{2,1,0:T(8,128)(2,1)} %shard_map.102), calls=%async_computation.1 | async-start | bytes 262144 | tf_op jit(solution)/shard_map/all_to_all | solution.py:295
  49.6 1.0 %copy-start.4 = (bf16[384,512]{1,0:T(8,128)(2,1)S(1)}, bf16[384,512]{1,0:T(8,128)(2,1)}, u32[]{:S(2)}) copy-start(bf16[384,512]{1,0:T(8,128)(2,1)} %copy-done.3) | copy-start | bytes 1179652
  50.6 4.8 %copy-start = (bf16[512,2048]{1,0:T(8,128)(2,1)S(1)}, bf16[512,2048]{1,0:T(8,128)(2,1)}, u32[]{:S(2)}) copy-start(bf16[512,2048]{1,0:T(8,128)(2,1)} %weight_ref.1) | copy-start | bytes 6291460
  54.2 0.9 %copy-start.1 = (f32[384,512]{1,0:T(8,128)}, f32[384,512]{1,0:T(8,128)S(1)}, u32[]{:S(2)}) copy-start(f32[384,512]{1,0:T(8,128)S(1)} %get-tuple-element.23.gate_ref) | copy-start | bytes 2359300
  55.4 1.1 %copy-start.2 = (f32[384,512]{1,0:T(8,128)S(1)}, f32[384,512]{1,0:T(8,128)}, u32[]{:S(2)}) copy-start(f32[384,512]{1,0:T(8,128)} %copy-done.1) | copy-start | bytes 2359300

commit v3 on v2

--- a/solution.py
+++ b/solution.py
@@ -15,6 +15,7 @@
 BLOCKS = 32
 GROUP = 8
 SHARES = 16
+EDGE = 3
 EXTRA = 16
 
 f32 = jnp.float32
@@ -50,11 +51,32 @@
     return dot(high, chosen) + (dot(middle, chosen) + dot(low, chosen))
 
 
-def convolved(ext, weights):
+def rolled(a, distance, axis):
+    return pltpu.roll(a, distance % a.shape[axis], axis)
+
+
+def iota(shape, axis):
+    return lax.broadcasted_iota(jnp.int32, shape, axis)
+
+
+def before_taps(ext, weights):
     total = weights[0:1] * ext[5 : 5 + LENGTH]
     for k in range(1, 4):
         total = total + weights[k : k + 1] * ext[5 + k : 5 + k + LENGTH]
-    return silu(total).astype(bf16)
+    return total
+
+
+def earlier_taps(last, taps):
+    total = taps[0] * last + taps[1] * rolled(last, -1, 0) + taps[2] * rolled(last, -2, 0)
+    return jnp.where(iota(last.shape, 0) < EDGE, total, 0.0)
+
+
+def own_taps(first, taps):
+    return taps[3] * first + taps[2] * rolled(first, 1, 0) + taps[1] * rolled(first, 2, 0)
+
+
+def rounded(a):
+    return a.astype(bf16).astype(f32)
 
 
 def fetch(pairs, sems):
@@ -65,55 +87,76 @@
 
 
 def summary_kernel(
-    x_at, bc_at, halo_ref, cx_at, cbc_at, step_at, decay_at,
-    message_ref, act_ref, bc_act_ref, cum_ref,
-    ext_x, ext_bc, x_ref, bc_ref, cx_ref, cbc_ref, step_ref, decay_ref, sems,
+    x_at, bc_at, cx_at, cbc_at, step_at, decay_at,
+    message_ref, act_ref, bc_act_ref, cum_ref, first_x_ref, first_bc_ref, taps_x_ref, taps_bc_ref,
+    ext_x, ext_bc, x_ref, bc_ref, step_ref, decay_ref, sems,
 ):
     for copy in fetch(
-        [(decay_at, decay_ref), (step_at, step_ref), (cx_at, cx_ref), (cbc_at, cbc_ref), (bc_at, bc_ref), (x_at, x_ref)],
+        [
+            (decay_at, decay_ref), (step_at, step_ref), (cx_at, taps_x_ref),
+            (cbc_at, taps_bc_ref), (bc_at, bc_ref), (x_at, x_ref),
+        ],
         sems,
     ):
         copy.wait()
-    halo = halo_ref[...].astype(f32)[8:16]
-    ext_x[0:8] = halo[:, :WIDTH]
-    ext_bc[0:8] = halo[:, WIDTH:]
+    ext_x[0:8] = jnp.zeros((8, WIDTH), f32)
+    ext_bc[0:8] = jnp.zeros((8, 2 * STATE), f32)
     ext_x[8:] = x_ref[...].astype(f32)
     ext_bc[8:] = bc_ref[...].astype(f32)
-    bc_act = convolved(ext_bc, cbc_ref)
+    sums = before_taps(ext_bc, taps_bc_ref)
+    first_bc_ref[...] = sums[0:8]
+    bc_act = silu(sums).astype(bf16)
     bc_act_ref[...] = bc_act
-    act = convolved(ext_x, cx_ref)
+    sums = before_taps(ext_x, taps_x_ref)
+    first_x_ref[...] = sums[0:8]
+    act = silu(sums).astype(bf16)
     act_ref[...] = act
 
-    s_at = lax.broadcasted_iota(jnp.int32, (LENGTH, LENGTH), 0)
-    t_at = lax.broadcasted_iota(jnp.int32, (LENGTH, LENGTH), 1)
-    upto = jnp.where(s_at <= t_at, 1.0, 0.0).astype(bf16)
+    upto = jnp.where(iota((LENGTH, LENGTH), 0) <= iota((LENGTH, LENGTH), 1), 1.0, 0.0).astype(bf16)
     high, middle, low = parts3(decay_ref[...])
     cum = dot(high, upto) + (dot(middle, upto) + dot(low, upto))
     cum_ref[...] = cum
     last = cum[:, LENGTH - 1 : LENGTH]
     factor = step_ref[...] * jnp.exp(last - cum)
-    weighted = (act.astype(f32) * spread_heads(columns_of(factor))).astype(bf16)
+    inside = jnp.where(iota((HEADS, LENGTH), 1) < EDGE, 0.0, factor)
+    weighted = (act.astype(f32) * spread_heads(columns_of(inside))).astype(bf16)
     b_rows = bc_act[:, :STATE].astype(f32)
     summary = dot(b_rows.T.astype(bf16), weighted)
 
     total = jnp.broadcast_to(jnp.exp(last), (HEADS, 128))
-    low_lanes = lax.broadcasted_iota(jnp.int32, (HEAD, 128), 1) < HEAD
-    row_at = lax.broadcasted_iota(jnp.int32, (EXTRA, 128), 0)
-    for pair in range(HEADS // 2):
-        top = summary[:HEAD, 128 * pair : 128 * (pair + 1)]
-        bottom = summary[HEAD:, 128 * pair : 128 * (pair + 1)]
-        even = jnp.where(low_lanes, top, pltpu.roll(bottom, HEAD, 1))
-        odd = jnp.where(low_lanes, pltpu.roll(top, HEAD, 1), bottom)
-        message_ref[2 * pair, 0:HEAD] = even.astype(bf16)
-        message_ref[2 * pair + 1, 0:HEAD] = odd.astype(bf16)
+    scalars = jnp.where(iota((HEADS, 128), 1) < HEAD, factor[:, :128], total)
+    high, middle, _ = (p.astype(f32) for p in parts3(scalars))
+    tap_high, tap_middle, _ = (p.astype(f32) for p in parts3(taps_x_ref[...]))
+    low_lanes = iota((HEAD, 128), 1) < HEAD
+    few = iota((8, 128), 1) < HEAD
+    row = iota((8, 128), 0)
+    b_first = rolled(ext_bc[8:16, :STATE], 3, 0)
+    bc_last = rolled(ext_bc[LENGTH : LENGTH + 8], 3, 0)
     for h in range(HEADS):
-        high, middle, low = (p.astype(f32) for p in parts3(total[h : h + 1]))
-        rows = jnp.where(row_at == 0, high, jnp.where(row_at == 1, middle, jnp.where(row_at == 2, low, 0.0)))
-        message_ref[h, HEAD:] = rows.astype(bf16)
+        lanes = slice(128 * (h // 2), 128 * (h // 2 + 1))
+        even = h % 2 == 0
+
+        def side_by_side(left, right, where):
+            if even:
+                return jnp.where(where, left, rolled(right, HEAD, 1))
+            return jnp.where(where, rolled(left, HEAD, 1), right)
+
+        message_ref[h, 0:HEAD] = side_by_side(summary[:HEAD, lanes], summary[HEAD:, lanes], low_lanes).astype(bf16)
+        x_edges = side_by_side(ext_x[8:16, lanes], rolled(ext_x[LENGTH : LENGTH + 8, lanes], 3, 0), few)
+        tile = jnp.where(row < 3, x_edges, b_first)
+        tile = jnp.where(row == 6, high[h : h + 1], jnp.where(row == 7, middle[h : h + 1], tile))
+        other = bc_last[:, :STATE]
+        for at, (part, k) in enumerate(((tap_high, 0), (tap_high, 2), (tap_middle, 0), (tap_middle, 2))):
+            pair = side_by_side(part[k : k + 1, lanes], part[k + 1 : k + 2, lanes], few[0:1])
+            other = jnp.where(row == 3 + at, pair, other)
+        c_row = bc_last[h : h + 1, STATE:] if h < EDGE else jnp.zeros((1, STATE), f32)
+        other = jnp.where(row == 7, c_row, other)
+        message_ref[h, HEAD:] = jnp.concatenate([tile, other], axis=0).astype(bf16)
 
 
 def within_kernel(
-    act_ref, bc_act_ref, cum_ref, step_at, skip_ref, z_at, gain_at, local_ref, gate_ref, gain_ref,
+    act_ref, bc_act_ref, cum_ref, step_at, skip_ref, z_at, gain_at, after_ref,
+    local_ref, gate_ref, gain_ref, lead_ref, gate_first_ref,
     step_ref, z_ref, sems,
 ):
     for copy in fetch([(step_at, step_ref), (z_at, z_ref), (gain_at, gain_ref)], sems):
@@ -125,12 +168,16 @@
     cum = cum_ref[...]
     cum_columns = columns_of(cum)
     act = act_ref[...].astype(f32)
-    scaled = (act * spread_heads(columns_of(step_ref[...]))).astype(bf16)
+    step = step_ref[...]
+    inside = jnp.where(iota((HEADS, LENGTH), 1) < EDGE, 0.0, step)
+    scaled = (act * spread_heads(columns_of(inside))).astype(bf16)
+    lead_ref[...] = spread_heads(columns_of(step)[0:8] * jnp.exp(-cum_columns[0:8]))
     gate = silu(z_ref[...].astype(f32))
+    gate_first_ref[...] = gate[0:8] * skip
     gate_ref[...] = gate * spread_heads(jnp.exp(cum_columns))
     b_rows = bc_act_ref[:, :STATE]
     c_rows = bc_act_ref[:, STATE:]
-    skipped = skip * act
+    skipped = jnp.where(iota((LENGTH, WIDTH), 0) < EDGE, 0.0, skip * act)
     t_at = lax.broadcasted_iota(jnp.int32, (BLOCK, BLOCK), 0)
     s_at = lax.broadcasted_iota(jnp.int32, (BLOCK, BLOCK), 1)
     causal = t_at >= s_at
@@ -158,45 +205,134 @@
             local_ref[rows, lanes] = (within + skipped[rows, lanes]) * gate[rows, lanes]
 
 
-def prefix_kernel(message_ref, prefix_ref, scale_ref, total_ref):
-    state = jnp.zeros((HEAD, 128), f32)
-    scale = jnp.ones((8, 128), f32)
-    for m in range(GROUP):
+def all_lanes(row):
+    return jnp.where(iota((1, 128), 1) < HEAD, rolled(row, HEAD, 1), row)
+
+
+def taps_of(tile):
+    pairs = tile[3:5] + tile[5:7]
+    return [pairs[0:1], rolled(pairs[0:1], HEAD, 1), pairs[1:2], rolled(pairs[1:2], HEAD, 1)]
+
+
+def edge_rows(tile, before, before_last, scalars, taps_x, taps_b):
+    row = iota((8, 128), 0)
+    lane = iota((8, 128), 1)
+    sums = own_taps(jnp.where(row < EDGE, tile, 0.0), taps_x)
+    sums_b = own_taps(jnp.where(row < EDGE, rolled(tile, -EDGE, 0), 0.0), taps_b)
+    if before is not None:
+        sums = sums + earlier_taps(jnp.where(row < EDGE, rolled(before, HEAD, 1), 0.0), taps_x)
+        sums_b = sums_b + earlier_taps(jnp.where(row < EDGE, before_last, 0.0), taps_b)
+    factor = jnp.sum(jnp.where(lane == row, scalars, 0.0), axis=1, keepdims=True)
+    weighted = rounded(silu(sums)) * factor
+    weighted = jnp.where((row < EDGE) & (lane < HEAD), weighted, 0.0)
+    return weighted, jnp.where(row < EDGE, rounded(silu(sums_b)), 0.0)
+
+
+def edge_states(entries):
+    zeros = jnp.zeros((HEAD - 8 * len(entries), 128), f32)
+    pad = [zeros] if zeros.shape[0] else []
+    weighted = jnp.concatenate([e[0] for e in entries] + pad, axis=0)
+    weighted = jnp.concatenate([weighted, rolled(weighted, HEAD, 1)], axis=0)
+    b_rows = jnp.concatenate([e[1] for e in entries] + pad + [jnp.zeros((HEAD, 128), f32)], axis=0).T
+    left = jnp.where(iota((HEAD, 128), 1) < HEAD, b_rows[:HEAD], rolled(b_rows[HEAD:], HEAD, 1)).astype(bf16)
+    owner = (iota((128, 128), 0) % HEAD) // 8
+    return [dot(left, jnp.where(owner == e, weighted, 0.0).astype(bf16)) for e in range(len(entries))]
+
+
+def prefix_kernel(message_ref, taps_ref, prefix_ref, scale_ref, total_ref):
+    tiles = [message_ref[m, HEAD:].astype(f32) for m in range(GROUP)]
+    scalars = [t[6:7] + t[7:8] for t in tiles]
+    decays = [all_lanes(s) for s in scalars]
+    taps_x = taps_of(tiles[0][8:])
+    taps_b = [taps_ref[k : k + 1, :STATE] for k in range(4)]
+    entries = [
+        edge_rows(tiles[m][:8], tiles[m - 1][:8], tiles[m - 1][8:], scalars[m], taps_x, taps_b) for m in range(1, GROUP)
+    ]
+    edges = edge_states(entries)
+    state = message_ref[0, 0:HEAD].astype(f32)
+    scale = jnp.ones((1, 128), f32)
+    for m in range(1, GROUP):
         prefix_ref[m] = state
-        scale_ref[m] = scale
-        rows = message_ref[m, HEAD:].astype(f32)
-        decay = rows[0:1] + (rows[1:2] + rows[2:3])
-        state = decay * state + message_ref[m, 0:HEAD].astype(f32)
-        scale = decay * scale
+        scale_ref[m] = jnp.broadcast_to(scale, (8, 128))
+        state = decays[m] * state + (message_ref[m, 0:HEAD].astype(f32) + edges[m - 1])
+        scale = decays[m] * scale
     total_ref[0:HEAD] = state.astype(bf16)
-    row_at = lax.broadcasted_iota(jnp.int32, (EXTRA, 128), 0)
-    high, middle, low = (p.astype(f32)[0:1] for p in parts3(scale))
-    rows = jnp.where(row_at == 0, high, jnp.where(row_at == 1, middle, jnp.where(row_at == 2, low, 0.0)))
-    total_ref[HEAD:] = rows.astype(bf16)
-
-
-def entering_kernel(prefix_ref, scale_ref, far_ref, near_ref, next_ref, state_ref):
-    entering = far_ref[0:HEAD].astype(f32)
-    for ref in (next_ref, near_ref):
-        rows = ref[HEAD:].astype(f32)
-        decay = rows[0:1] + (rows[1:2] + rows[2:3])
-        entering = decay * entering + ref[0:HEAD].astype(f32)
-    for m in range(GROUP):
-        state_ref[m] = (prefix_ref[m] + scale_ref[m, 0:1] * entering).astype(bf16)
-
-
-def output_kernel(state_ref, bc_act_ref, local_ref, gate_ref, gain_ref, weight_ref, share_ref):
-    low_lanes = lax.broadcasted_iota(jnp.int32, (HEAD, 128), 1) < HEAD
+    lane = iota((1, 128), 1)
+    high, middle, _ = (p.astype(f32) for p in parts3(jnp.where(lane < HEAD, scalars[0] * scale, decays[0] * scale)))
+    row = iota((8, 128), 0)
+    first, last = tiles[0][:8], tiles[GROUP - 1]
+    tile = jnp.where((row < EDGE) & (iota((8, 128), 1) >= HEAD), last[:8], first)
+    tile = jnp.where(row == 6, high, jnp.where(row == 7, middle, tile))
+    total_ref[HEAD:] = jnp.concatenate([tile, last[8:]], axis=0).astype(bf16)
+
+
+def entering_kernel(gain_ref, message_ref, taps_ref, prefix_ref, scale_ref, far_ref, near_ref, next_ref, state_ref):
+    own = message_ref[0, HEAD:].astype(f32)
+    taps_x = taps_of(own[8:])
+    taps_b = [taps_ref[k : k + 1, :STATE] for k in range(4)]
+    refs = [far_ref, next_ref, near_ref]
+    tiles = [r[HEAD:].astype(f32) for r in refs] + [own]
+    scalars = [t[6:7] + t[7:8] for t in tiles]
+    entries = [edge_rows(tiles[0][:8], None, None, scalars[0], taps_x, taps_b)]
+    for e in range(1, 4):
+        entries.append(edge_rows(tiles[e][:8], tiles[e - 1][:8], tiles[e - 1][8:], scalars[e], taps_x, taps_b))
+    edges = edge_states(entries)
+    entering = far_ref[0:HEAD].astype(f32) + edges[0]
+    for e in range(1, 3):
+        entering = all_lanes(scalars[e]) * entering + (refs[e][0:HEAD].astype(f32) + edges[e])
+    state_ref[0, 0:HEAD] = entering.astype(bf16)
+    state_ref[0, HEAD:] = near_ref[HEAD:]
+    after_first = all_lanes(scalars[3]) * entering + edges[3]
+    for m in range(1, GROUP):
+        state_ref[m, 0:HEAD] = (prefix_ref[m] + scale_ref[m, 0:1] * after_first).astype(bf16)
+        state_ref[m, HEAD:] = message_ref[m - 1, HEAD:]
+
+
+def output_kernel(
+    state_ref, bc_act_ref, first_x_ref, first_bc_ref, taps_x_ref, taps_bc_ref, lead_ref, gate_first_ref,
+    local_ref, gate_ref, gain_ref, weight_ref, share_ref,
+):
+    row = iota((8, 128), 0)
+    few = iota((8, 128), 1) < HEAD
+    low_lanes = iota((HEAD, 128), 1) < HEAD
+    tiles = [state_ref[h, HEAD:].astype(f32) for h in range(HEADS)]
+
+    last_x = jnp.concatenate(
+        [jnp.where(few, rolled(tiles[h][:8], HEAD, 1), tiles[h + 1][:8]) for h in range(0, HEADS, 2)], axis=1
+    )
+    last_c = jnp.zeros((8, 128), f32)
+    for h in range(EDGE):
+        last_c = jnp.where(row == h, tiles[h][15:16], last_c)
+    last_bc = jnp.concatenate([tiles[0][8:], last_c], axis=1)
+    last_x = jnp.where(iota((8, WIDTH), 0) < EDGE, last_x, 0.0)
+    last_bc = jnp.where(iota((8, 2 * STATE), 0) < EDGE, last_bc, 0.0)
+    taps_x = [taps_x_ref[k : k + 1] for k in range(4)]
+    taps_bc = [taps_bc_ref[k : k + 1] for k in range(4)]
+    act = rounded(silu(first_x_ref[...] + earlier_taps(last_x, taps_x)))
+    bc_act = rounded(silu(first_bc_ref[...] + earlier_taps(last_bc, taps_bc)))
+    b_first, c_first = bc_act[:, :STATE], bc_act[:, STATE:]
+    lead = rounded(jnp.where(iota((8, WIDTH), 0) < EDGE, act * lead_ref[...], 0.0))
+
     pairs = []
     for pair in range(HEADS // 2):
-        even = state_ref[2 * pair].astype(f32)
-        odd = state_ref[2 * pair + 1].astype(f32)
-        top = jnp.where(low_lanes, even, pltpu.roll(odd, HEAD, 1))
-        bottom = jnp.where(low_lanes, pltpu.roll(even, HEAD, 1), odd)
-        pairs.append(jnp.concatenate([top, bottom], axis=0).astype(bf16))
+        even = state_ref[2 * pair, 0:HEAD].astype(f32)
+        odd = state_ref[2 * pair + 1, 0:HEAD].astype(f32)
+        top = jnp.where(low_lanes, even, rolled(odd, HEAD, 1))
+        bottom = jnp.where(low_lanes, rolled(even, HEAD, 1), odd)
+        pairs.append(jnp.concatenate([top, bottom], axis=0))
     states = jnp.concatenate(pairs, axis=1)
-    carried = dot(bc_act_ref[:, STATE:], states)
-    gated = local_ref[...] + gate_ref[...] * carried
+    b_columns = jnp.concatenate([b_first, jnp.zeros((120, STATE), f32)], axis=0).T.astype(bf16)
+    lead_rows = jnp.concatenate([lead, jnp.zeros((120, WIDTH), f32)], axis=0).astype(bf16)
+    states = (states + dot(b_columns, lead_rows)).astype(bf16)
+    c_rows = jnp.concatenate([c_first, bc_act_ref[:, STATE:].astype(f32)[8:]], axis=0).astype(bf16)
+    gated = local_ref[...] + gate_ref[...] * dot(c_rows, states)
+    ahead = jnp.zeros((8, WIDTH), f32)
+    for s in range(1, EDGE):
+        score = jnp.sum(c_first * b_first[s : s + 1], axis=1, keepdims=True)
+        ahead = ahead + jnp.where(iota((8, WIDTH), 0) < s, score * lead[s : s + 1], 0.0)
+    skipped = jnp.where(iota((8, WIDTH), 0) < EDGE, gate_first_ref[...] * act, 0.0)
+    gated = jnp.concatenate([gated[0:8] + (skipped - gate_ref[0:8] * ahead), gated[8:]], axis=0)
+
     squares = jnp.sum(gated * gated, axis=1, keepdims=True)
     scaled = (gated * gain_ref[...]).astype(bf16)
     wide = jnp.broadcast_to(squares, (LENGTH, 128))
@@ -256,17 +392,17 @@
 def shards(
     inner_x, gate_z, bc_input, conv_inner, conv_bc, step_size, log_decay, skip_gain, norm_gain, out_weight
 ):
-    tail = jnp.concatenate([inner_x[LENGTH - 16 :], bc_input[LENGTH - 16 :]], axis=1)
-    halo = lax.ppermute(tail, "seq", [(i, i + 1) for i in range(BLOCKS - 1)])
-    message, act, bc_act, cum = call(
+    message, act, bc_act, cum, first_x, first_bc, taps_x, taps_bc = call(
         summary_kernel,
-        [((HEADS, HEAD + EXTRA, 128), bf16), ((LENGTH, WIDTH), bf16), ((LENGTH, 2 * STATE), bf16), ((HEADS, LENGTH), f32)],
-        inner_x, bc_input, halo, conv_inner, conv_bc, step_size, log_decay,
-        specs=[THERE, THERE, HERE, THERE, THERE, THERE, THERE],
+        [
+            ((HEADS, HEAD + EXTRA, 128), bf16), ((LENGTH, WIDTH), bf16), ((LENGTH, 2 * STATE), bf16),
+            ((HEADS, LENGTH), f32), ((8, WIDTH), f32), ((8, 2 * STATE), f32), ((4, WIDTH), f32), ((4, 2 * STATE), f32),
+        ],
+        inner_x, bc_input, conv_inner, conv_bc, step_size, log_decay,
+        specs=[THERE] * 6,
         scratch=[
             pltpu.VMEM((LENGTH + 8, WIDTH), f32), pltpu.VMEM((LENGTH + 8, 2 * STATE), f32),
             pltpu.VMEM((LENGTH, WIDTH), bf16), pltpu.VMEM((LENGTH, 2 * STATE), bf16),
-            pltpu.VMEM((4, WIDTH), f32), pltpu.VMEM((4, 2 * STATE), f32),
             pltpu.VMEM((HEADS, LENGTH), f32), pltpu.VMEM((HEADS, LENGTH), f32),
             pltpu.SemaphoreType.DMA((6,)),
         ],
@@ -276,13 +412,13 @@
     prefix, scale, total = call(
         prefix_kernel,
         [((GROUP, HEAD, 128), f32), ((GROUP, 8, 128), f32), ((HEAD + EXTRA, 128), bf16)],
-        message,
-    )
-    local, gate, gain = call(
+        message, taps_bc,
+    )
+    local, gate, gain, lead, gate_first = call(
         within_kernel,
-        [((LENGTH, WIDTH), f32), ((LENGTH, WIDTH), f32), ((1, WIDTH), f32)],
-        act, bc_act, cum, step_size, skip_gain, gate_z, norm_gain[None, :],
-        specs=[HERE, HERE, HERE, THERE, SCALARS, THERE, THERE],
+        [((LENGTH, WIDTH), f32), ((LENGTH, WIDTH), f32), ((1, WIDTH), f32), ((8, WIDTH), f32), ((8, WIDTH), f32)],
+        act, bc_act, cum, step_size, skip_gain, gate_z, norm_gain[None, :], total,
+        specs=[HERE, HERE, HERE, THERE, SCALARS, THERE, THERE, HERE],
         scratch=[pltpu.VMEM((HEADS, LENGTH), f32), pltpu.VMEM((LENGTH, WIDTH), bf16), pltpu.SemaphoreType.DMA((3,))],
         flops=2e9, transcendentals=1.2e6,
     )
@@ -291,12 +427,16 @@
         return lax.ppermute(total, "seq", [(i, i + distance) for i in range(BLOCKS - distance)])
 
     far, near, after = later(3 * GROUP), later(GROUP), later(2 * GROUP)
-    (state,) = call(entering_kernel, [((GROUP, HEAD, 128), bf16)], prefix, scale, far, near, after)
+    (state,) = call(
+        entering_kernel,
+        [((GROUP, HEAD + EXTRA, 128), bf16)],
+        gain, message, taps_bc, prefix, scale, far, near, after,
+    )
     state = lax.all_to_all(state, "seq", 0, 0, tiled=True, axis_index_groups=groups)
     (share,) = call(
         output_kernel,
         [((SHARES, LENGTH + EXTRA, 128), bf16)],
-        state, bc_act, local, gate, gain, out_weight,
+        state, bc_act, first_x, first_bc, taps_x, taps_bc, lead, gate_first, local, gate, gain, out_weight,
         flops=9e8,
     )
     share = lax.all_to_all(share, "tp", 0, 0, tiled=True)

time: 88.2 us -> 81.6 us (0.925)
  blocking collectives: 39 us -> 54.6 us
  starting transfers between devices: 28.7 us -> 16 us
  waiting for transfers between devices: 5.05 us -> 0.01 us
  local copies, waits for them, and re-layouts: 5.2 us -> 0.65 us
    all_to_all x0 -> x1, blocking collectives: none -> 10.5 us  [shards(): lax.all_to_all(state, 'seq', 0, 0, tiled=True, axis_index_groups=groups)]
    all_to_all x1 -> x0, starting transfers between devices: 5.64 us -> none  [shards(): lax.all_to_all(state, 'seq', 0, 0, tiled=True, axis_index_groups=groups)]
    all_to_all x1, blocking collectives: 10 us -> 15.3 us  [shards(): lax.all_to_all(message, 'seq', 0, 0, tiled=True, axis_index_groups=groups)]
    ppermute x1 -> x0, starting transfers between devices: 4.92 us -> none  [shards(): halo = lax.ppermute(tail, 'seq', [(i, i + 1) for i in range(BLOCKS - 1)])]
    ppermute x1 -> x0, waiting for transfers between devices: 3.9 us -> none  [shards(): halo = lax.ppermute(tail, 'seq', [(i, i + 1) for i in range(BLOCKS - 1)])]
    unnamed x12 -> x4, local copies, waits for them, and re-layouts: 3.78 us -> 0.65 us
    ppermute x3, starting transfers between devices: 18.1 us -> 16 us  [later(): lax.ppermute(total, 'seq', [(i, i + distance) for i in range(BLOCKS - dis...]
    slice x2 -> x0, local copies, waits for them, and re-layouts: 1.43 us -> none  [the longest x1 0.72 us: shards(): inner_x[LENGTH - 16:]]
  transfers between devices with their start and end apart: 5 -> 3, of which waited for: 3 -> 0; matrix products, arithmetic and copies ran while one was open for 0% -> 0% of each run, Pallas kernels for 4% -> 5%
where the time goes in v3:
time: 81.6 us; the launch traced here: 81.1 us
  blocking collectives  54.6 us (67%)
  starting transfers between devices  16 us (20%)
  Pallas kernels  9.8 us (12%)
    all_to_all x1, blocking collectives, shards(): share = lax.all_to_all(share, 'tp', 0, 0, tiled=True)  28.8 us
    ppermute x3, starting transfers between devices, later(): lax.ppermute(total, 'seq', [(i, i + distance) for i in range(BLOCKS - dis...  16 us
    all_to_all x1, blocking collectives, shards(): lax.all_to_all(message, 'seq', 0, 0, tiled=True, axis_index_groups=groups)  15.3 us
    all_to_all x1, blocking collectives, shards(): lax.all_to_all(state, 'seq', 0, 0, tiled=True, axis_index_groups=groups)  10.5 us
    pallas_call x6, Pallas kernels, call(): pl.pallas_call(kernel, out_shape=[jax.ShapeDtypeStruct(s, d) for s, d in...  9.8 us
  transfers between devices with their start and end apart: 3, of which 0 were waited for; matrix products, arithmetic and copies ran while one was open for 0% of the time, Pallas kernels for 5%

profile of v3, /device:TPU:1, one launch (start us, length us, event | category | flops | bytes accessed | tf_op | source)
XLA Modules:
  0.0 81.1 jit_solution(3590011043590663434)
XLA Ops:
  0.0 3.1 %shard_map.100 = (bf16[8,80,128]{2,1,0:T(8,128)(2,1)S(1)}, bf16[384,512]{1,0:T(8,128)(2,1)S(1)}, bf16[384,256]{1,0:T(8,128)(2,1)S(1)}, f32[8,384]{1,0:T(8,128)S(...) custom-call(bf16[384,512]{1,0:T(8,128)(2,1)} %x_at.1, ...), custom_call_target="tpu_custom_call" | custom-call | flops 100000000 | bytes 2000000 | tf_op jit(solution)/shard_map/pallas_call | solution.py:379
  3.1 15.3 %all_to_all.15.message_ref = bf16[8,80,128]{2,1,0:T(8,128)(2,1)S(1)} all-to-all(bf16[8,80,128]{2,1,0:T(8,128)(2,1)S(1)} %get-tuple-element.24), channel_id=1, replica_groups={{0,16,32,48,64,80,96,112},{128,144,160,176,192,208,224,240},{256,272,28..., dimensions={0} | all-to-all | bytes 327680 | tf_op jit(solution)/shard_map/all_to_all | solution.py:411
  18.4 0.4 shard_map.101
  18.8 10.7 %collective-permute-start.2 = (bf16[80,128]{1,0:T(8,128)(2,1)S(1)}, bf16[80,128]{1,0:T(8,128)(2,1)S(1)}, u32[]{:S(2)}, u32[]{:S(2)}) collective-permute-start(bf16[80,128]{1,0:T(8,128)(2,1)S(1)} %get-tuple-element.26.after_ref), channel_id=1, source_target_pairs={{0,256},{16,272},{32,288},{48,304},{64,320},{80,336},{96,352},{112... | collective-permute-start | bytes 61448 | tf_op jit(solution)/shard_map/ppermute | solution.py:427
  29.5 4.0 %collective-permute-start.1 = (bf16[80,128]{1,0:T(8,128)(2,1)S(1)}, bf16[80,128]{1,0:T(8,128)(2,1)S(1)}, u32[]{:S(2)}, u32[]{:S(2)}) collective-permute-start(bf16[80,128]{1,0:T(8,128)(2,1)S(1)} %get-tuple-element.26.after_ref), channel_id=1, source_target_pairs={{0,128},{16,144},{32,160},{48,176},{64,192},{80,208},{96,224},{112... | collective-permute-start | bytes 61448 | tf_op jit(solution)/shard_map/ppermute | solution.py:427
  33.5 1.3 %collective-permute-start = (bf16[80,128]{1,0:T(8,128)(2,1)S(1)}, bf16[80,128]{1,0:T(8,128)(2,1)S(1)}, u32[]{:S(2)}, u32[]{:S(2)}) collective-permute-start(bf16[80,128]{1,0:T(8,128)(2,1)S(1)} %get-tuple-element.26.after_ref), channel_id=1, source_target_pairs={{0,384},{16,400},{32,416},{48,432},{64,448},{80,464},{96,480},{112... | collective-permute-start | bytes 61448 | tf_op jit(solution)/shard_map/ppermute | solution.py:427
  34.8 0.0 copy-start.1
  34.8 0.6 copy-done.1
  35.4 0.0 copy-start
  35.4 3.7 %shard_map.102 = (f32[384,512]{1,0:T(8,128)S(1)}, f32[384,512]{1,0:T(8,128)S(1)}, f32[1,512]{1,0:T(1,128)S(1)}, f32[8,512]{1,0:T(8,128)S(1)}, f32[8,512]{1,0:T(8,128)S(1)}) custom-call(bf16[384,512]{1,0:T(8,128)(2,1)S(1)} %get-tuple-element.21.act_ref, bf16[384,256]{1,0:T(8,128)(2,1)S(1)} %get-tuple-element.22.bc_act_ref, ...), custom_call_target="tpu_custom_call" | custom-call | flops 2000000000 | bytes 2000000 | tf_op jit(solution)/shard_map/pallas_call | solution.py:379
  39.1 0.0 collective-permute-done.2.next_ref
  39.1 0.0 collective-permute-done.1.near_ref
  39.1 0.0 collective-permute-done.far_ref
  39.1 0.4 shard_map.103
  39.5 10.5 %all_to_all.16.state_ref = bf16[8,80,128]{2,1,0:T(8,128)(2,1)S(1)} all-to-all(bf16[8,80,128]{2,1,0:T(8,128)(2,1)S(1)} %shard_map.103), channel_id=1, replica_groups={{0,16,32,48,64,80,96,112},{128,144,160,176,192,208,224,240},{256,272,28..., dimensions={0} | all-to-all | bytes 327680 | tf_op jit(solution)/shard_map/all_to_all | solution.py:435
  50.1 0.0 copy-done
  50.1 1.4 %shard_map.104 = bf16[16,400,128]{2,1,0:T(8,128)(2,1)S(1)} custom-call(bf16[8,80,128]{2,1,0:T(8,128)(2,1)S(1)} %all_to_all.16.state_ref, bf16[384,256]{1,0:T(8,128)(2,1)S(1)} %get-tuple-element.22.bc_act_ref, f32[8,512]{1,0:T(8,128)S(1)} %get-tuple-element.30.first_x_ref, f32[8,256]{1,0:T(8,128)S(1)} %get-tuple-element.31.first_bc_ref, ...), custom_call_target="tpu_custom_call" | custom-call | flops 900000000 | bytes 2000000 | tf_op jit(solution)/shard_map/pallas_call | solution.py:379
  51.4 28.8 %all_to_all.17.share_ref = bf16[16,400,128]{2,1,0:T(8,128)(2,1)S(1)} all-to-all(bf16[16,400,128]{2,1,0:T(8,128)(2,1)S(1)} %shard_map.104), channel_id=1, replica_groups=mesh['seq'=32,'tp'=16] {'tp'}, dimensions={0} | all-to-all | bytes 3276800 | tf_op jit(solution)/shard_map/all_to_all | solution.py:442
  80.3 0.9 %shard_map.105 = bf16[384,128]{1,0:T(8,128)(2,1)} custom-call(bf16[16,400,128]{2,1,0:T(8,128)(2,1)S(1)} %all_to_all.17.share_ref), custom_call_target="tpu_custom_call" | custom-call | flops 100000000 | bytes 2000000 | tf_op jit(solution)/shard_map/pallas_call | solution.py:379
Async XLA Ops:
  18.8 20.3 %collective-permute-start.2 = (bf16[80,128]{1,0:T(8,128)(2,1)S(1)}, bf16[80,128]{1,0:T(8,128)(2,1)S(1)}, u32[]{:S(2)}, u32[]{:S(2)}) collective-permute-start(bf16[80,128]{1,0:T(8,128)(2,1)S(1)} %get-tuple-element.26.after_ref), channel_id=1, source_target_pairs={{0,256},{16,272},{32,288},{48,304},{64,320},{80,336},{96,352},{112... | collective-permute-start | bytes 61448 | tf_op jit(solution)/shard_map/ppermute | solution.py:427
  29.5 9.7 %collective-permute-start.1 = (bf16[80,128]{1,0:T(8,128)(2,1)S(1)}, bf16[80,128]{1,0:T(8,128)(2,1)S(1)}, u32[]{:S(2)}, u32[]{:S(2)}) collective-permute-start(bf16[80,128]{1,0:T(8,128)(2,1)S(1)} %get-tuple-element.26.after_ref), channel_id=1, source_target_pairs={{0,128},{16,144},{32,160},{48,176},{64,192},{80,208},{96,224},{112... | collective-permute-start | bytes 61448 | tf_op jit(solution)/shard_map/ppermute | solution.py:427
  33.5 5.6 %collective-permute-start = (bf16[80,128]{1,0:T(8,128)(2,1)S(1)}, bf16[80,128]{1,0:T(8,128)(2,1)S(1)}, u32[]{:S(2)}, u32[]{:S(2)}) collective-permute-start(bf16[80,128]{1,0:T(8,128)(2,1)S(1)} %get-tuple-element.26.after_ref), channel_id=1, source_target_pairs={{0,384},{16,400},{32,416},{48,432},{64,448},{80,464},{96,480},{112... | collective-permute-start | bytes 61448 | tf_op jit(solution)/shard_map/ppermute | solution.py:427
  34.8 0.7 copy-start.1
  35.4 14.6 %copy-start = (bf16[512,2048]{1,0:T(8,128)(2,1)S(1)}, bf16[512,2048]{1,0:T(8,128)(2,1)}, u32[]{:S(2)}) copy-start(bf16[512,2048]{1,0:T(8,128)(2,1)} %weight_ref.1) | copy-start | bytes 6291460

commit v4 on v3

--- a/solution.py
+++ b/solution.py
@@ -39,16 +39,18 @@
 
 
 def columns_of(rows):
-    padded = jnp.concatenate([rows, jnp.zeros((128 - rows.shape[0], LENGTH), f32)], axis=0)
+    padded = jnp.concatenate([rows, jnp.zeros((128 - rows.shape[0], rows.shape[1]), f32)], axis=0)
     return padded.T
 
 
+def part_columns(rows):
+    return columns_of(jnp.concatenate([p.astype(f32) for p in parts3(rows)], axis=0)).astype(bf16)
+
+
 def spread_heads(columns):
-    head = lax.broadcasted_iota(jnp.int32, (128, WIDTH), 0)
-    channel = lax.broadcasted_iota(jnp.int32, (128, WIDTH), 1)
-    chosen = jnp.where(channel // HEAD == head, 1.0, 0.0).astype(bf16)
-    high, middle, low = parts3(columns)
-    return dot(high, chosen) + (dot(middle, chosen) + dot(low, chosen))
+    part = iota((128, WIDTH), 0)
+    chosen = (part < 3 * HEADS) & (part % HEADS == iota((128, WIDTH), 1) // HEAD)
+    return dot(columns, jnp.where(chosen, 1.0, 0.0).astype(bf16))
 
 
 def rolled(a, distance, axis):
@@ -91,13 +93,24 @@
     message_ref, act_ref, bc_act_ref, cum_ref, first_x_ref, first_bc_ref, taps_x_ref, taps_bc_ref,
     ext_x, ext_bc, x_ref, bc_ref, step_ref, decay_ref, sems,
 ):
-    for copy in fetch(
+    copies = fetch(
         [
             (decay_at, decay_ref), (step_at, step_ref), (cx_at, taps_x_ref),
             (cbc_at, taps_bc_ref), (bc_at, bc_ref), (x_at, x_ref),
         ],
         sems,
-    ):
+    )
+    copies[0].wait()
+    copies[1].wait()
+    upto = jnp.where(iota((LENGTH, LENGTH), 0) <= iota((LENGTH, LENGTH), 1), 1.0, 0.0).astype(bf16)
+    sums = dot(jnp.concatenate([p.astype(f32) for p in parts3(decay_ref[...])], axis=0).astype(bf16), upto)
+    cum = sums[0:8] + (sums[8:16] + sums[16:24])
+    cum_ref[...] = cum
+    last = cum[:, LENGTH - 1 : LENGTH]
+    factor = step_ref[...] * jnp.exp(last - cum)
+    inside = jnp.where(iota((HEADS, LENGTH), 1) < EDGE, 0.0, factor)
+    factor_spread = spread_heads(part_columns(inside))
+    for copy in copies[2:]:
         copy.wait()
     ext_x[0:8] = jnp.zeros((8, WIDTH), f32)
     ext_bc[0:8] = jnp.zeros((8, 2 * STATE), f32)
@@ -112,14 +125,7 @@
     act = silu(sums).astype(bf16)
     act_ref[...] = act
 
-    upto = jnp.where(iota((LENGTH, LENGTH), 0) <= iota((LENGTH, LENGTH), 1), 1.0, 0.0).astype(bf16)
-    high, middle, low = parts3(decay_ref[...])
-    cum = dot(high, upto) + (dot(middle, upto) + dot(low, upto))
-    cum_ref[...] = cum
-    last = cum[:, LENGTH - 1 : LENGTH]
-    factor = step_ref[...] * jnp.exp(last - cum)
-    inside = jnp.where(iota((HEADS, LENGTH), 1) < EDGE, 0.0, factor)
-    weighted = (act.astype(f32) * spread_heads(columns_of(inside))).astype(bf16)
+    weighted = (act.astype(f32) * factor_spread).astype(bf16)
     b_rows = bc_act[:, :STATE].astype(f32)
     summary = dot(b_rows.T.astype(bf16), weighted)
 
@@ -155,13 +161,14 @@
 
 
 def within_kernel(
-    act_ref, bc_act_ref, cum_ref, step_at, skip_ref, z_at, gain_at, after_ref,
+    act_ref, bc_act_ref, cum_ref, step_at, skip_at, z_at, gain_at, after_ref,
     local_ref, gate_ref, gain_ref, lead_ref, gate_first_ref,
-    step_ref, z_ref, sems,
+    step_ref, z_ref, skip_ref, sems,
 ):
-    for copy in fetch([(step_at, step_ref), (z_at, z_ref), (gain_at, gain_ref)], sems):
-        copy.wait()
-    head_at = lax.broadcasted_iota(jnp.int32, (1, WIDTH), 1) // HEAD
+    copies = fetch([(step_at, step_ref), (skip_at, skip_ref), (gain_at, gain_ref), (z_at, z_ref)], sems)
+    copies[0].wait()
+    copies[1].wait()
+    head_at = iota((1, WIDTH), 1) // HEAD
     skip = jnp.zeros((1, WIDTH), f32)
     for h in range(HEADS):
         skip = jnp.where(head_at == h, skip_ref[h], skip)
@@ -170,11 +177,16 @@
     act = act_ref[...].astype(f32)
     step = step_ref[...]
     inside = jnp.where(iota((HEADS, LENGTH), 1) < EDGE, 0.0, step)
-    scaled = (act * spread_heads(columns_of(inside))).astype(bf16)
-    lead_ref[...] = spread_heads(columns_of(step)[0:8] * jnp.exp(-cum_columns[0:8]))
+    scaled = (act * spread_heads(part_columns(inside))).astype(bf16)
+    early = iota((HEADS, 128), 1) < 8
+    lead = jnp.where(early, step[:, :128] * jnp.exp(jnp.where(early, -cum[:, :128], 0.0)), 0.0)
+    lead_ref[...] = spread_heads(part_columns(lead)[0:16])[0:8]
+    cum_spread = spread_heads(part_columns(jnp.exp(cum)))
+    copies[2].wait()
+    copies[3].wait()
     gate = silu(z_ref[...].astype(f32))
     gate_first_ref[...] = gate[0:8] * skip
-    gate_ref[...] = gate * spread_heads(jnp.exp(cum_columns))
+    gate_ref[...] = gate * cum_spread
     b_rows = bc_act_ref[:, :STATE]
     c_rows = bc_act_ref[:, STATE:]
     skipped = jnp.where(iota((LENGTH, WIDTH), 0) < EDGE, 0.0, skip * act)
@@ -189,7 +201,7 @@
         )
         for pair in range(HEADS // 2):
             lanes = slice(128 * pair, 128 * (pair + 1))
-            sums = []
+            mixing = []
             for h in (2 * pair, 2 * pair + 1):
                 here = cum_columns[rows, h : h + 1]
                 tiles = []
@@ -199,9 +211,9 @@
                     if other == block:
                         spread = jnp.where(causal, spread, -jnp.inf)
                     tiles.append((scores[:, columns] * jnp.exp(spread)).astype(bf16))
-                mixing = tiles[0] if block == 0 else jnp.concatenate(tiles, axis=1)
-                sums.append(dot(mixing, scaled[: (block + 1) * BLOCK, lanes]))
-            within = jnp.where(low_lanes, sums[0], sums[1])
+                mixing.append(tiles[0] if block == 0 else jnp.concatenate(tiles, axis=1))
+            sums = dot(jnp.concatenate(mixing, axis=0), scaled[: (block + 1) * BLOCK, lanes])
+            within = jnp.where(low_lanes, sums[:BLOCK], sums[BLOCK:])
             local_ref[rows, lanes] = (within + skipped[rows, lanes]) * gate[rows, lanes]
 
 
@@ -266,22 +278,25 @@
     total_ref[HEAD:] = jnp.concatenate([tile, last[8:]], axis=0).astype(bf16)
 
 
-def entering_kernel(gain_ref, message_ref, taps_ref, prefix_ref, scale_ref, far_ref, near_ref, next_ref, state_ref):
+def entering_kernel(
+    gain_ref, message_ref, taps_ref, prefix_ref, scale_ref,
+    other_ref, relayed_ref, skipped_ref, near_ref, far_ref, state_ref,
+):
     own = message_ref[0, HEAD:].astype(f32)
     taps_x = taps_of(own[8:])
     taps_b = [taps_ref[k : k + 1, :STATE] for k in range(4)]
-    refs = [far_ref, next_ref, near_ref]
-    tiles = [r[HEAD:].astype(f32) for r in refs] + [own]
+    totals = [far_ref[...].astype(f32), relayed_ref[...].astype(f32) + skipped_ref[...].astype(f32), near_ref[...].astype(f32) + other_ref[...].astype(f32)]
+    tiles = [t[HEAD:] for t in totals] + [own]
     scalars = [t[6:7] + t[7:8] for t in tiles]
     entries = [edge_rows(tiles[0][:8], None, None, scalars[0], taps_x, taps_b)]
     for e in range(1, 4):
         entries.append(edge_rows(tiles[e][:8], tiles[e - 1][:8], tiles[e - 1][8:], scalars[e], taps_x, taps_b))
     edges = edge_states(entries)
-    entering = far_ref[0:HEAD].astype(f32) + edges[0]
+    entering = totals[0][0:HEAD] + edges[0]
     for e in range(1, 3):
-        entering = all_lanes(scalars[e]) * entering + (refs[e][0:HEAD].astype(f32) + edges[e])
+        entering = all_lanes(scalars[e]) * entering + (totals[e][0:HEAD] + edges[e])
     state_ref[0, 0:HEAD] = entering.astype(bf16)
-    state_ref[0, HEAD:] = near_ref[HEAD:]
+    state_ref[0, HEAD:] = tiles[2].astype(bf16)
     after_first = all_lanes(scalars[3]) * entering + edges[3]
     for m in range(1, GROUP):
         state_ref[m, 0:HEAD] = (prefix_ref[m] + scale_ref[m, 0:1] * after_first).astype(bf16)
@@ -367,7 +382,6 @@
 
 
 HERE = pl.BlockSpec(memory_space=pltpu.VMEM)
-SCALARS = pl.BlockSpec(memory_space=pltpu.SMEM)
 THERE = pl.BlockSpec(memory_space=pltpu.HBM)
 
 
@@ -414,23 +428,28 @@
         [((GROUP, HEAD, 128), f32), ((GROUP, 8, 128), f32), ((HEAD + EXTRA, 128), bf16)],
         message, taps_bc,
     )
+    def later(a, distance, first, last):
+        return lax.ppermute(a, "seq", [(i, i + distance * GROUP) for i in range(first * GROUP, (last + 1) * GROUP)])
+
+    pairs = [(i, i + GROUP) for i in (*range(GROUP), *range(2 * GROUP, 3 * GROUP))]
+    near, far, skipped = lax.ppermute(total, "seq", pairs), later(total, 3, 0, 0), later(total, 2, 1, 1)
+    relayed, other = later(near, 1, 1, 1), later(total, 1, 1, 1)
     local, gate, gain, lead, gate_first = call(
         within_kernel,
         [((LENGTH, WIDTH), f32), ((LENGTH, WIDTH), f32), ((1, WIDTH), f32), ((8, WIDTH), f32), ((8, WIDTH), f32)],
-        act, bc_act, cum, step_size, skip_gain, gate_z, norm_gain[None, :], total,
-        specs=[HERE, HERE, HERE, THERE, SCALARS, THERE, THERE, HERE],
-        scratch=[pltpu.VMEM((HEADS, LENGTH), f32), pltpu.VMEM((LENGTH, WIDTH), bf16), pltpu.SemaphoreType.DMA((3,))],
+        act, bc_act, cum, step_size, skip_gain, gate_z, norm_gain[None, :], near,
+        specs=[HERE, HERE, HERE, THERE, THERE, THERE, THERE, HERE],
+        scratch=[
+            pltpu.VMEM((HEADS, LENGTH), f32), pltpu.VMEM((LENGTH, WIDTH), bf16), pltpu.SMEM((HEADS,), f32),
+            pltpu.SemaphoreType.DMA((4,)),
+        ],
         flops=2e9, transcendentals=1.2e6,
     )
 
-    def later(distance):
-        return lax.ppermute(total, "seq", [(i, i + distance) for i in range(BLOCKS - distance)])
-
-    far, near, after = later(3 * GROUP), later(GROUP), later(2 * GROUP)
     (state,) = call(
         entering_kernel,
         [((GROUP, HEAD + EXTRA, 128), bf16)],
-        gain, message, taps_bc, prefix, scale, far, near, after,
+        gain, message, taps_bc, prefix, scale, other, relayed, skipped, near, far,
     )
     state = lax.all_to_all(state, "seq", 0, 0, tiled=True, axis_index_groups=groups)
     (share,) = call(

time: 81.6 us -> 75 us (0.919)
  starting transfers between devices: 16 us -> 11 us
  Pallas kernels: 9.8 us -> 8.35 us
    ppermute x3 -> x5, starting transfers between devices: 16 us -> 11 us  [the longest x1 6.75 us: shards(): lax.ppermute(total, 'seq', pairs)]
    pallas_call x6, Pallas kernels: 9.8 us -> 8.35 us  [call(): pl.pallas_call(kernel, out_shape=[jax.ShapeDtypeStruct(s, d) for s, d in...]
  transfers between devices with their start and end apart: 3 -> 5, of which waited for: 0 -> 0; matrix products, arithmetic and copies ran while one was open for 0% -> 0% of each run, Pallas kernels for 5% -> 3%
where the time goes in v4:
time: 75 us; the launch traced here: 73.8 us
  blocking collectives  54.3 us (72%)
  starting transfers between devices  11 us (15%)
  Pallas kernels  8.35 us (11%)
    all_to_all x1, blocking collectives, shards(): share = lax.all_to_all(share, 'tp', 0, 0, tiled=True)  28.8 us
    all_to_all x1, blocking collectives, shards(): lax.all_to_all(message, 'seq', 0, 0, tiled=True, axis_index_groups=groups)  15.3 us
    all_to_all x1, blocking collectives, shards(): lax.all_to_all(state, 'seq', 0, 0, tiled=True, axis_index_groups=groups)  10.3 us
    pallas_call x6, Pallas kernels, call(): pl.pallas_call(kernel, out_shape=[jax.ShapeDtypeStruct(s, d) for s, d in...  8.35 us
    ppermute x1, starting transfers between devices, shards(): lax.ppermute(total, 'seq', pairs)  6.75 us
    ppermute x4, starting transfers between devices, later(): lax.ppermute(a, 'seq', [(i, i + distance * GROUP) for i in range(first *...  4.21 us
  transfers between devices with their start and end apart: 5, of which 0 were waited for; matrix products, arithmetic and copies ran while one was open for 0% of the time, Pallas kernels for 3%

profile of v4, /device:TPU:1, one launch (start us, length us, event | category | flops | bytes accessed | tf_op | source)
XLA Modules:
  0.0 73.8 jit_solution(16185085373622122009)
XLA Ops:
  0.0 2.7 %shard_map.100 = (bf16[8,80,128]{2,1,0:T(8,128)(2,1)S(1)}, bf16[384,512]{1,0:T(8,128)(2,1)S(1)}, bf16[384,256]{1,0:T(8,128)(2,1)S(1)}, f32[8,384]{1,0:T(8,128)S(...) custom-call(bf16[384,512]{1,0:T(8,128)(2,1)} %x_at.1, ...), custom_call_target="tpu_custom_call" | custom-call | flops 100000000 | bytes 2000000 | tf_op jit(solution)/shard_map/pallas_call | solution.py:393
  2.7 15.3 %all_to_all.15.message_ref = bf16[8,80,128]{2,1,0:T(8,128)(2,1)S(1)} all-to-all(bf16[8,80,128]{2,1,0:T(8,128)(2,1)S(1)} %get-tuple-element.24), channel_id=1, replica_groups={{0,16,32,48,64,80,96,112},{128,144,160,176,192,208,224,240},{256,272,28..., dimensions={0} | all-to-all | bytes 327680 | tf_op jit(solution)/shard_map/all_to_all | solution.py:425
  18.0 0.4 shard_map.101
  18.4 6.8 %collective-permute-start = (bf16[80,128]{1,0:T(8,128)(2,1)S(1)}, bf16[80,128]{1,0:T(8,128)(2,1)S(1)}, u32[]{:S(2)}, u32[]{:S(2)}) collective-permute-start(bf16[80,128]{1,0:T(8,128)(2,1)S(1)} %get-tuple-element.26), channel_id=1, source_target_pairs={{0,128},{16,144},{32,160},{48,176},{64,192},{80,208},{96,224},{112... | collective-permute-start | bytes 61448 | tf_op jit(solution)/shard_map/ppermute | solution.py:435
  25.2 2.2 %collective-permute-start.4 = (bf16[80,128]{1,0:T(8,128)(2,1)S(1)}, bf16[80,128]{1,0:T(8,128)(2,1)S(1)}, u32[]{:S(2)}, u32[]{:S(2)}) collective-permute-start(bf16[80,128]{1,0:T(8,128)(2,1)S(1)} %get-tuple-element.26), channel_id=1, source_target_pairs={{0,384},{16,400},{32,416},{48,432},{64,448},{80,464},{96,480},{112... | collective-permute-start | bytes 61448 | tf_op jit(solution)/shard_map/ppermute | solution.py:432
  27.4 0.7 collective-permute-start.3
  28.1 0.7 collective-permute-start.1
  28.7 0.0 collective-permute-done.after_ref.near_ref
  28.7 0.7 collective-permute-start.2
  29.4 0.0 copy-start
  29.4 2.6 %shard_map.102 = (f32[384,512]{1,0:T(8,128)S(1)}, f32[384,512]{1,0:T(8,128)S(1)}, f32[1,512]{1,0:T(1,128)S(1)}, f32[8,512]{1,0:T(8,128)S(1)}, f32[8,512]{1,0:T(8,128)S(1)}) custom-call(bf16[384,512]{1,0:T(8,128)(2,1)S(1)} %get-tuple-element.21.act_ref, bf16[384,256]{1,0:T(8,128)(2,1)S(1)} %get-tuple-element.22.bc_act_ref, ...), custom_call_target="tpu_custom_call" | custom-call | flops 2000000000 | bytes 2000000 | tf_op jit(solution)/shard_map/pallas_call | solution.py:393
  32.0 0.0 collective-permute-done.4.far_ref
  32.0 0.0 collective-permute-done.3.skipped_ref
  32.0 0.0 collective-permute-done.1.other_ref
  32.0 0.0 collective-permute-done.2.relayed_ref
  32.0 0.4 shard_map.103
  32.4 10.3 %all_to_all.16.state_ref = bf16[8,80,128]{2,1,0:T(8,128)(2,1)S(1)} all-to-all(bf16[8,80,128]{2,1,0:T(8,128)(2,1)S(1)} %shard_map.103), channel_id=1, replica_groups={{0,16,32,48,64,80,96,112},{128,144,160,176,192,208,224,240},{256,272,28..., dimensions={0} | all-to-all | bytes 327680 | tf_op jit(solution)/shard_map/all_to_all | solution.py:454
  42.7 0.0 copy-done
  42.7 1.4 %shard_map.104 = bf16[16,400,128]{2,1,0:T(8,128)(2,1)S(1)} custom-call(bf16[8,80,128]{2,1,0:T(8,128)(2,1)S(1)} %all_to_all.16.state_ref, bf16[384,256]{1,0:T(8,128)(2,1)S(1)} %get-tuple-element.22.bc_act_ref, f32[8,512]{1,0:T(8,128)S(1)} %get-tuple-element.30.first_x_ref, f32[8,256]{1,0:T(8,128)S(1)} %get-tuple-element.31.first_bc_ref, ...), custom_call_target="tpu_custom_call" | custom-call | flops 900000000 | bytes 2000000 | tf_op jit(solution)/shard_map/pallas_call | solution.py:393
  44.1 28.8 %all_to_all.17.share_ref = bf16[16,400,128]{2,1,0:T(8,128)(2,1)S(1)} all-to-all(bf16[16,400,128]{2,1,0:T(8,128)(2,1)S(1)} %shard_map.104), channel_id=1, replica_groups=mesh['seq'=32,'tp'=16] {'tp'}, dimensions={0} | all-to-all | bytes 3276800 | tf_op jit(solution)/shard_map/all_to_all | solution.py:461
  72.9 0.9 %shard_map.105 = bf16[384,128]{1,0:T(8,128)(2,1)} custom-call(bf16[16,400,128]{2,1,0:T(8,128)(2,1)S(1)} %all_to_all.17.share_ref), custom_call_target="tpu_custom_call" | custom-call | flops 100000000 | bytes 2000000 | tf_op jit(solution)/shard_map/pallas_call | solution.py:393
Async XLA Ops:
  18.4 10.3 %collective-permute-start = (bf16[80,128]{1,0:T(8,128)(2,1)S(1)}, bf16[80,128]{1,0:T(8,128)(2,1)S(1)}, u32[]{:S(2)}, u32[]{:S(2)}) collective-permute-start(bf16[80,128]{1,0:T(8,128)(2,1)S(1)} %get-tuple-element.26), channel_id=1, source_target_pairs={{0,128},{16,144},{32,160},{48,176},{64,192},{80,208},{96,224},{112... | collective-permute-start | bytes 61448 | tf_op jit(solution)/shard_map/ppermute | solution.py:435
  25.2 6.8 %collective-permute-start.4 = (bf16[80,128]{1,0:T(8,128)(2,1)S(1)}, bf16[80,128]{1,0:T(8,128)(2,1)S(1)}, u32[]{:S(2)}, u32[]{:S(2)}) collective-permute-start(bf16[80,128]{1,0:T(8,128)(2,1)S(1)} %get-tuple-element.26), channel_id=1, source_target_pairs={{0,384},{16,400},{32,416},{48,432},{64,448},{80,464},{96,480},{112... | collective-permute-start | bytes 61448 | tf_op jit(solution)/shard_map/ppermute | solution.py:432
  27.4 4.6 %collective-permute-start.3 = (bf16[80,128]{1,0:T(8,128)(2,1)S(1)}, bf16[80,128]{1,0:T(8,128)(2,1)S(1)}, u32[]{:S(2)}, u32[]{:S(2)}) collective-permute-start(bf16[80,128]{1,0:T(8,128)(2,1)S(1)} %get-tuple-element.26), channel_id=1, source_target_pairs={{128,384},{144,400},{160,416},{176,432},{192,448},{208,464},{224,4... | collective-permute-start | bytes 61448 | tf_op jit(solution)/shard_map/ppermute | solution.py:432
  28.1 4.0 %collective-permute-start.1 = (bf16[80,128]{1,0:T(8,128)(2,1)S(1)}, bf16[80,128]{1,0:T(8,128)(2,1)S(1)}, u32[]{:S(2)}, u32[]{:S(2)}) collective-permute-start(bf16[80,128]{1,0:T(8,128)(2,1)S(1)} %get-tuple-element.26), channel_id=1, source_target_pairs={{128,256},{144,272},{160,288},{176,304},{192,320},{208,336},{224,3... | collective-permute-start | bytes 61448 | tf_op jit(solution)/shard_map/ppermute | solution.py:432
  28.7 3.3 %collective-permute-start.2 = (bf16[80,128]{1,0:T(8,128)(2,1)S(1)}, bf16[80,128]{1,0:T(8,128)(2,1)S(1)}, u32[]{:S(2)}, u32[]{:S(2)}) collective-permute-start(bf16[80,128]{1,0:T(8,128)(2,1)S(1)} %collective-permute-done.after_ref.near_ref), channel_id=1, source_target_pairs={{128,256},{144,272},{160,288},{176,304},{192,320},{208,336},{224,3... | collective-permute-start | bytes 61448 | tf_op jit(solution)/shard_map/ppermute | solution.py:432
  29.4 13.3 %copy-start = (bf16[512,2048]{1,0:T(8,128)(2,1)S(1)}, bf16[512,2048]{1,0:T(8,128)(2,1)}, u32[]{:S(2)}) copy-start(bf16[512,2048]{1,0:T(8,128)(2,1)} %weight_ref.1) | copy-start | bytes 6291460

commit v5 on v4

--- a/solution.py
+++ b/solution.py
@@ -89,14 +89,16 @@
 
 
 def summary_kernel(
-    x_at, bc_at, cx_at, cbc_at, step_at, decay_at,
+    x_at, bc_at, cx_at, cbc_at, step_at, decay_at, z_at, gain_at, skip_at,
     message_ref, act_ref, bc_act_ref, cum_ref, first_x_ref, first_bc_ref, taps_x_ref, taps_bc_ref,
-    ext_x, ext_bc, x_ref, bc_ref, step_ref, decay_ref, sems,
+    step_ref, z_ref, gain_ref, skip_row_ref,
+    ext_x, ext_bc, x_ref, bc_ref, decay_ref, skip_ref, sems,
 ):
     copies = fetch(
         [
             (decay_at, decay_ref), (step_at, step_ref), (cx_at, taps_x_ref),
             (cbc_at, taps_bc_ref), (bc_at, bc_ref), (x_at, x_ref),
+            (z_at, z_ref), (gain_at, gain_ref), (skip_at, skip_ref),
         ],
         sems,
     )
@@ -110,7 +112,7 @@
     factor = step_ref[...] * jnp.exp(last - cum)
     inside = jnp.where(iota((HEADS, LENGTH), 1) < EDGE, 0.0, factor)
     factor_spread = spread_heads(part_columns(inside))
-    for copy in copies[2:]:
+    for copy in copies[2:6]:
         copy.wait()
     ext_x[0:8] = jnp.zeros((8, WIDTH), f32)
     ext_bc[0:8] = jnp.zeros((8, 2 * STATE), f32)
@@ -159,19 +161,20 @@
         other = jnp.where(row == 7, c_row, other)
         message_ref[h, HEAD:] = jnp.concatenate([tile, other], axis=0).astype(bf16)
 
-
-def within_kernel(
-    act_ref, bc_act_ref, cum_ref, step_at, skip_at, z_at, gain_at, after_ref,
-    local_ref, gate_ref, gain_ref, lead_ref, gate_first_ref,
-    step_ref, z_ref, skip_ref, sems,
-):
-    copies = fetch([(step_at, step_ref), (skip_at, skip_ref), (gain_at, gain_ref), (z_at, z_ref)], sems)
-    copies[0].wait()
-    copies[1].wait()
+    for copy in copies[6:]:
+        copy.wait()
     head_at = iota((1, WIDTH), 1) // HEAD
     skip = jnp.zeros((1, WIDTH), f32)
     for h in range(HEADS):
         skip = jnp.where(head_at == h, skip_ref[h], skip)
+    skip_row_ref[...] = skip
+
+
+def within_kernel(
+    act_ref, bc_act_ref, cum_ref, step_ref, skip_row_ref, z_ref, after_ref,
+    local_ref, gate_ref, lead_ref, gate_first_ref,
+):
+    skip = skip_row_ref[...]
     cum = cum_ref[...]
     cum_columns = columns_of(cum)
     act = act_ref[...].astype(f32)
@@ -182,8 +185,6 @@
     lead = jnp.where(early, step[:, :128] * jnp.exp(jnp.where(early, -cum[:, :128], 0.0)), 0.0)
     lead_ref[...] = spread_heads(part_columns(lead)[0:16])[0:8]
     cum_spread = spread_heads(part_columns(jnp.exp(cum)))
-    copies[2].wait()
-    copies[3].wait()
     gate = silu(z_ref[...].astype(f32))
     gate_first_ref[...] = gate[0:8] * skip
     gate_ref[...] = gate * cum_spread
@@ -279,13 +280,19 @@
 
 
 def entering_kernel(
-    gain_ref, message_ref, taps_ref, prefix_ref, scale_ref,
-    other_ref, relayed_ref, skipped_ref, near_ref, far_ref, state_ref,
+    lead_ref, message_ref, taps_ref, prefix_ref, scale_ref,
+    relayed_ref, other_ref, skipped_ref, near_ref, state_ref,
 ):
     own = message_ref[0, HEAD:].astype(f32)
     taps_x = taps_of(own[8:])
     taps_b = [taps_ref[k : k + 1, :STATE] for k in range(4)]
-    totals = [far_ref[...].astype(f32), relayed_ref[...].astype(f32) + skipped_ref[...].astype(f32), near_ref[...].astype(f32) + other_ref[...].astype(f32)]
+    third = lax.axis_index("seq") // GROUP == 2
+    other = other_ref[...].astype(f32)
+    totals = [
+        jnp.where(third, 0.0, other),
+        relayed_ref[...].astype(f32) + skipped_ref[...].astype(f32),
+        near_ref[...].astype(f32) + jnp.where(third, other, 0.0),
+    ]
     tiles = [t[HEAD:] for t in totals] + [own]
     scalars = [t[6:7] + t[7:8] for t in tiles]
     entries = [edge_rows(tiles[0][:8], None, None, scalars[0], taps_x, taps_b)]
@@ -406,19 +413,20 @@
 def shards(
     inner_x, gate_z, bc_input, conv_inner, conv_bc, step_size, log_decay, skip_gain, norm_gain, out_weight
 ):
-    message, act, bc_act, cum, first_x, first_bc, taps_x, taps_bc = call(
+    message, act, bc_act, cum, first_x, first_bc, taps_x, taps_bc, step, z, gain, skip = call(
         summary_kernel,
         [
             ((HEADS, HEAD + EXTRA, 128), bf16), ((LENGTH, WIDTH), bf16), ((LENGTH, 2 * STATE), bf16),
             ((HEADS, LENGTH), f32), ((8, WIDTH), f32), ((8, 2 * STATE), f32), ((4, WIDTH), f32), ((4, 2 * STATE), f32),
+            ((HEADS, LENGTH), f32), ((LENGTH, WIDTH), bf16), ((1, WIDTH), f32), ((1, WIDTH), f32),
         ],
-        inner_x, bc_input, conv_inner, conv_bc, step_size, log_decay,
-        specs=[THERE] * 6,
+        inner_x, bc_input, conv_inner, conv_bc, step_size, log_decay, gate_z, norm_gain[None, :], skip_gain,
+        specs=[THERE] * 9,
         scratch=[
             pltpu.VMEM((LENGTH + 8, WIDTH), f32), pltpu.VMEM((LENGTH + 8, 2 * STATE), f32),
             pltpu.VMEM((LENGTH, WIDTH), bf16), pltpu.VMEM((LENGTH, 2 * STATE), bf16),
-            pltpu.VMEM((HEADS, LENGTH), f32), pltpu.VMEM((HEADS, LENGTH), f32),
-            pltpu.SemaphoreType.DMA((6,)),
+            pltpu.VMEM((HEADS, LENGTH), f32), pltpu.SMEM((HEADS,), f32),
+            pltpu.SemaphoreType.DMA((9,)),
         ],
     )
     groups = [list(range(i, i + GROUP)) for i in range(0, BLOCKS, GROUP)]
@@ -431,25 +439,21 @@
     def later(a, distance, first, last):
         return lax.ppermute(a, "seq", [(i, i + distance * GROUP) for i in range(first * GROUP, (last + 1) * GROUP)])
 
-    pairs = [(i, i + GROUP) for i in (*range(GROUP), *range(2 * GROUP, 3 * GROUP))]
-    near, far, skipped = lax.ppermute(total, "seq", pairs), later(total, 3, 0, 0), later(total, 2, 1, 1)
-    relayed, other = later(near, 1, 1, 1), later(total, 1, 1, 1)
-    local, gate, gain, lead, gate_first = call(
+    def permuted(a, *ways):
+        return lax.ppermute(a, "seq", [(i + f * GROUP, i + t * GROUP) for f, t in ways for i in range(GROUP)])
+
+    near, skipped, other = permuted(total, (0, 1), (2, 3)), permuted(total, (1, 3)), permuted(total, (0, 3), (1, 2))
+    relayed = permuted(near, (1, 2))
+    local, gate, lead, gate_first = call(
         within_kernel,
-        [((LENGTH, WIDTH), f32), ((LENGTH, WIDTH), f32), ((1, WIDTH), f32), ((8, WIDTH), f32), ((8, WIDTH), f32)],
-        act, bc_act, cum, step_size, skip_gain, gate_z, norm_gain[None, :], near,
-        specs=[HERE, HERE, HERE, THERE, THERE, THERE, THERE, HERE],
-        scratch=[
-            pltpu.VMEM((HEADS, LENGTH), f32), pltpu.VMEM((LENGTH, WIDTH), bf16), pltpu.SMEM((HEADS,), f32),
-            pltpu.SemaphoreType.DMA((4,)),
-        ],
+        [((LENGTH, WIDTH), f32), ((LENGTH, WIDTH), f32), ((8, WIDTH), f32), ((8, WIDTH), f32)],
+        act, bc_act, cum, step, skip, z, near,
         flops=2e9, transcendentals=1.2e6,
     )
-
     (state,) = call(
         entering_kernel,
         [((GROUP, HEAD + EXTRA, 128), bf16)],
-        gain, message, taps_bc, prefix, scale, other, relayed, skipped, near, far,
+        lead, message, taps_bc, prefix, scale, relayed, other, skipped, near,
     )
     state = lax.all_to_all(state, "seq", 0, 0, tiled=True, axis_index_groups=groups)
     (share,) = call(

time: 75 us -> 73.5 us (0.980)
  Pallas kernels: 8.35 us -> 7.38 us
    pallas_call x6, Pallas kernels: 8.35 us -> 7.38 us  [call(): pl.pallas_call(kernel, out_shape=[jax.ShapeDtypeStruct(s, d) for s, d in...]
    ppermute x5 -> x4, starting transfers between devices: 11 us -> 10.9 us  [permuted(): lax.ppermute(a, 'seq', [(i + f * GROUP, i + t * GROUP) for f, t in ways f...]
  transfers between devices with their start and end apart: 5 -> 4, of which waited for: 0 -> 0; matrix products, arithmetic and copies ran while one was open for 0% -> 0% of each run, Pallas kernels for 3% -> 2%
where the time goes in v5:
time: 73.5 us; the launch traced here: 72.8 us
  blocking collectives  54.3 us (74%)
  starting transfers between devices  10.9 us (15%)
  Pallas kernels  7.38 us (10%)
    all_to_all x1, blocking collectives, shards(): share = lax.all_to_all(share, 'tp', 0, 0, tiled=True)  28.8 us
    all_to_all x1, blocking collectives, shards(): lax.all_to_all(message, 'seq', 0, 0, tiled=True, axis_index_groups=groups)  15.3 us
    ppermute x4, starting transfers between devices, permuted(): lax.ppermute(a, 'seq', [(i + f * GROUP, i + t * GROUP) for f, t in ways f...  10.9 us
    all_to_all x1, blocking collectives, shards(): lax.all_to_all(state, 'seq', 0, 0, tiled=True, axis_index_groups=groups)  10.2 us
    pallas_call x6, Pallas kernels, call(): pl.pallas_call(kernel, out_shape=[jax.ShapeDtypeStruct(s, d) for s, d in...  7.38 us
  transfers between devices with their start and end apart: 4, of which 0 were waited for; matrix products, arithmetic and copies ran while one was open for 0% of the time, Pallas kernels for 2%

profile of v5, /device:TPU:1, one launch (start us, length us, event | category | flops | bytes accessed | tf_op | source)
XLA Modules:
  0.0 72.8 jit_solution(10060775695959438481)
XLA Ops:
  0.0 2.8 %shard_map.100 = (bf16[8,80,128]{2,1,0:T(8,128)(2,1)S(1)}, bf16[384,512]{1,0:T(8,128)(2,1)S(1)}, bf16[384,256]{1,0:T(8,128)(2,1)S(1)}, f32[8,384]{1,0:T(8,128)S(...) custom-call(bf16[384,512]{1,0:T(8,128)(2,1)} %x_at.1, ...), custom_call_target="tpu_custom_call" | custom-call | flops 100000000 | bytes 2000000 | tf_op jit(solution)/shard_map/pallas_call | solution.py:400
  2.8 15.3 %all_to_all.15.message_ref = bf16[8,80,128]{2,1,0:T(8,128)(2,1)S(1)} all-to-all(bf16[8,80,128]{2,1,0:T(8,128)(2,1)S(1)} %get-tuple-element.30), channel_id=1, replica_groups={{0,16,32,48,64,80,96,112},{128,144,160,176,192,208,224,240},{256,272,28..., dimensions={0} | all-to-all | bytes 327680 | tf_op jit(solution)/shard_map/all_to_all | solution.py:433
  18.0 0.4 shard_map.101
  18.4 6.8 %collective-permute-start = (bf16[80,128]{1,0:T(8,128)(2,1)S(1)}, bf16[80,128]{1,0:T(8,128)(2,1)S(1)}, u32[]{:S(2)}, u32[]{:S(2)}) collective-permute-start(bf16[80,128]{1,0:T(8,128)(2,1)S(1)} %get-tuple-element.32), channel_id=1, source_target_pairs={{0,128},{16,144},{32,160},{48,176},{64,192},{80,208},{96,224},{112... | collective-permute-start | bytes 61448 | tf_op jit(solution)/shard_map/ppermute | solution.py:443
  25.2 0.7 collective-permute-start.3
  25.9 2.9 %collective-permute-start.2 = (bf16[80,128]{1,0:T(8,128)(2,1)S(1)}, bf16[80,128]{1,0:T(8,128)(2,1)S(1)}, u32[]{:S(2)}, u32[]{:S(2)}) collective-permute-start(bf16[80,128]{1,0:T(8,128)(2,1)S(1)} %get-tuple-element.32), channel_id=1, source_target_pairs={{0,384},{16,400},{32,416},{48,432},{64,448},{80,464},{96,480},{112... | collective-permute-start | bytes 61448 | tf_op jit(solution)/shard_map/ppermute | solution.py:443
  28.7 0.0 collective-permute-done.after_ref.near_ref
  28.8 0.7 collective-permute-start.1
  29.4 0.0 copy-start
  29.4 1.6 %shard_map.102 = (f32[384,512]{1,0:T(8,128)S(1)}, f32[384,512]{1,0:T(8,128)S(1)}, f32[8,512]{1,0:T(8,128)S(1)}, f32[8,512]{1,0:T(8,128)S(1)}) custom-call(bf16[384,512]{1,0:T(8,128)(2,1)S(1)} %get-tuple-element.24.act_ref, bf16[384,256]{1,0:T(8,128)(2,1)S(1)} %get-tuple-element.25.bc_act_ref, f32[8,384]{1,0:T(8,128)S(1)} %get-tuple-element.26.cum_ref, ...), custom_call_target="tpu_custom_call" | custom-call | flops 2000000000 | bytes 2000000 | tf_op jit(solution)/shard_map/pallas_call | solution.py:400
  31.0 0.0 collective-permute-done.3.skipped_ref
  31.0 0.0 collective-permute-done.2.other_ref
  31.0 0.0 collective-permute-done.1.relayed_ref
  31.0 0.4 shard_map.103
  31.4 10.2 %all_to_all.16.state_ref = bf16[8,80,128]{2,1,0:T(8,128)(2,1)S(1)} all-to-all(bf16[8,80,128]{2,1,0:T(8,128)(2,1)S(1)} %shard_map.103), channel_id=1, replica_groups={{0,16,32,48,64,80,96,112},{128,144,160,176,192,208,224,240},{256,272,28..., dimensions={0} | all-to-all | bytes 327680 | tf_op jit(solution)/shard_map/all_to_all | solution.py:458
  41.7 0.0 copy-done
  41.7 1.4 %shard_map.104 = bf16[16,400,128]{2,1,0:T(8,128)(2,1)S(1)} custom-call(bf16[8,80,128]{2,1,0:T(8,128)(2,1)S(1)} %all_to_all.16.state_ref, bf16[384,256]{1,0:T(8,128)(2,1)S(1)} %get-tuple-element.25.bc_act_ref, f32[8,512]{1,0:T(8,128)S(1)} %get-tuple-element.36.first_x_ref, f32[8,256]{1,0:T(8,128)S(1)} %get-tuple-element.37.first_bc_ref, ...), custom_call_target="tpu_custom_call" | custom-call | flops 900000000 | bytes 2000000 | tf_op jit(solution)/shard_map/pallas_call | solution.py:400
  43.1 28.8 %all_to_all.17.share_ref = bf16[16,400,128]{2,1,0:T(8,128)(2,1)S(1)} all-to-all(bf16[16,400,128]{2,1,0:T(8,128)(2,1)S(1)} %shard_map.104), channel_id=1, replica_groups=mesh['seq'=32,'tp'=16] {'tp'}, dimensions={0} | all-to-all | bytes 3276800 | tf_op jit(solution)/shard_map/all_to_all | solution.py:465
  71.9 0.9 %shard_map.105 = bf16[384,128]{1,0:T(8,128)(2,1)} custom-call(bf16[16,400,128]{2,1,0:T(8,128)(2,1)S(1)} %all_to_all.17.share_ref), custom_call_target="tpu_custom_call" | custom-call | flops 100000000 | bytes 2000000 | tf_op jit(solution)/shard_map/pallas_call | solution.py:400
Async XLA Ops:
  18.4 10.3 %collective-permute-start = (bf16[80,128]{1,0:T(8,128)(2,1)S(1)}, bf16[80,128]{1,0:T(8,128)(2,1)S(1)}, u32[]{:S(2)}, u32[]{:S(2)}) collective-permute-start(bf16[80,128]{1,0:T(8,128)(2,1)S(1)} %get-tuple-element.32), channel_id=1, source_target_pairs={{0,128},{16,144},{32,160},{48,176},{64,192},{80,208},{96,224},{112... | collective-permute-start | bytes 61448 | tf_op jit(solution)/shard_map/ppermute | solution.py:443
  25.2 5.8 %collective-permute-start.3 = (bf16[80,128]{1,0:T(8,128)(2,1)S(1)}, bf16[80,128]{1,0:T(8,128)(2,1)S(1)}, u32[]{:S(2)}, u32[]{:S(2)}) collective-permute-start(bf16[80,128]{1,0:T(8,128)(2,1)S(1)} %get-tuple-element.32), channel_id=1, source_target_pairs={{128,384},{144,400},{160,416},{176,432},{192,448},{208,464},{224,4... | collective-permute-start | bytes 61448 | tf_op jit(solution)/shard_map/ppermute | solution.py:443
  25.9 5.1 %collective-permute-start.2 = (bf16[80,128]{1,0:T(8,128)(2,1)S(1)}, bf16[80,128]{1,0:T(8,128)(2,1)S(1)}, u32[]{:S(2)}, u32[]{:S(2)}) collective-permute-start(bf16[80,128]{1,0:T(8,128)(2,1)S(1)} %get-tuple-element.32), channel_id=1, source_target_pairs={{0,384},{16,400},{32,416},{48,432},{64,448},{80,464},{96,480},{112... | collective-permute-start | bytes 61448 | tf_op jit(solution)/shard_map/ppermute | solution.py:443
  28.8 2.3 %collective-permute-start.1 = (bf16[80,128]{1,0:T(8,128)(2,1)S(1)}, bf16[80,128]{1,0:T(8,128)(2,1)S(1)}, u32[]{:S(2)}, u32[]{:S(2)}) collective-permute-start(bf16[80,128]{1,0:T(8,128)(2,1)S(1)} %collective-permute-done.after_ref.near_ref), channel_id=1, source_target_pairs={{128,256},{144,272},{160,288},{176,304},{192,320},{208,336},{224,3... | collective-permute-start | bytes 61448 | tf_op jit(solution)/shard_map/ppermute | solution.py:443
  29.4 12.2 %copy-start = (bf16[512,2048]{1,0:T(8,128)(2,1)S(1)}, bf16[512,2048]{1,0:T(8,128)(2,1)}, u32[]{:S(2)}) copy-start(bf16[512,2048]{1,0:T(8,128)(2,1)} %weight_ref.1) | copy-start | bytes 6291460

commit v6 on v5

--- a/solution.py
+++ b/solution.py
@@ -61,11 +61,10 @@
     return lax.broadcasted_iota(jnp.int32, shape, axis)
 
 
-def before_taps(ext, weights):
-    total = weights[0:1] * ext[5 : 5 + LENGTH]
-    for k in range(1, 4):
-        total = total + weights[k : k + 1] * ext[5 + k : 5 + k + LENGTH]
-    return total
+def before_taps(ext, late, weights):
+    here, back = ext[8 : 8 + LENGTH], ext[7 : 7 + LENGTH]
+    late[8:] = weights[1:2] * here + weights[0:1] * back
+    return weights[3:4] * here + weights[2:3] * back + late[6 : 6 + LENGTH]
 
 
 def earlier_taps(last, taps):
@@ -92,7 +91,7 @@
     x_at, bc_at, cx_at, cbc_at, step_at, decay_at, z_at, gain_at, skip_at,
     message_ref, act_ref, bc_act_ref, cum_ref, first_x_ref, first_bc_ref, taps_x_ref, taps_bc_ref,
     step_ref, z_ref, gain_ref, skip_row_ref,
-    ext_x, ext_bc, x_ref, bc_ref, decay_ref, skip_ref, sems,
+    ext_x, ext_bc, late_x, late_bc, x_ref, bc_ref, decay_ref, skip_ref, sems,
 ):
     copies = fetch(
         [
@@ -118,11 +117,13 @@
     ext_bc[0:8] = jnp.zeros((8, 2 * STATE), f32)
     ext_x[8:] = x_ref[...].astype(f32)
     ext_bc[8:] = bc_ref[...].astype(f32)
-    sums = before_taps(ext_bc, taps_bc_ref)
+    late_bc[0:8] = jnp.zeros((8, 2 * STATE), f32)
+    late_x[0:8] = jnp.zeros((8, WIDTH), f32)
+    sums = before_taps(ext_bc, late_bc, taps_bc_ref)
     first_bc_ref[...] = sums[0:8]
     bc_act = silu(sums).astype(bf16)
     bc_act_ref[...] = bc_act
-    sums = before_taps(ext_x, taps_x_ref)
+    sums = before_taps(ext_x, late_x, taps_x_ref)
     first_x_ref[...] = sums[0:8]
     act = silu(sums).astype(bf16)
     act_ref[...] = act
@@ -279,32 +280,48 @@
     total_ref[HEAD:] = jnp.concatenate([tile, last[8:]], axis=0).astype(bf16)
 
 
+def joined_kernel(lead_ref, total_ref, swapped_ref, taps_ref, joined_ref, own_ref):
+    zeroth = lax.axis_index("seq") // GROUP == 0
+    total, swapped = total_ref[...].astype(f32), swapped_ref[...].astype(f32)
+    first, second = jnp.where(zeroth, total, swapped), jnp.where(zeroth, swapped, total)
+    taps_x = taps_of(total[HEAD + 8 :])
+    taps_b = [taps_ref[k : k + 1, :STATE] for k in range(4)]
+    tiles = [first[HEAD:], second[HEAD:]]
+    scalars = [t[6:7] + t[7:8] for t in tiles]
+    edges = edge_states(
+        [
+            edge_rows(tiles[0][:8], None, None, scalars[0], taps_x, taps_b),
+            edge_rows(tiles[1][:8], tiles[0][:8], tiles[0][8:], scalars[1], taps_x, taps_b),
+        ]
+    )
+    state = all_lanes(scalars[1]) * (first[:HEAD] + edges[0]) + (second[:HEAD] + edges[1])
+    joined_ref[0:HEAD] = state.astype(bf16)
+    joined_ref[HEAD:] = tiles[1].astype(bf16)
+    own_ref[...] = total_ref[...]
+
+
 def entering_kernel(
-    lead_ref, message_ref, taps_ref, prefix_ref, scale_ref,
-    relayed_ref, other_ref, skipped_ref, near_ref, state_ref,
+    message_ref, taps_ref, prefix_ref, scale_ref, swapped_ref, crossed_ref, passed_ref, state_ref
 ):
+    group = lax.axis_index("seq") // GROUP
+    crossed = crossed_ref[...].astype(f32)
+    near = jnp.where(group == 1, swapped_ref[...].astype(f32), passed_ref[...].astype(f32))
     own = message_ref[0, HEAD:].astype(f32)
+    before = jnp.where(group == 2, crossed[HEAD:], near[HEAD:])
     taps_x = taps_of(own[8:])
     taps_b = [taps_ref[k : k + 1, :STATE] for k in range(4)]
-    third = lax.axis_index("seq") // GROUP == 2
-    other = other_ref[...].astype(f32)
-    totals = [
-        jnp.where(third, 0.0, other),
-        relayed_ref[...].astype(f32) + skipped_ref[...].astype(f32),
-        near_ref[...].astype(f32) + jnp.where(third, other, 0.0),
-    ]
-    tiles = [t[HEAD:] for t in totals] + [own]
-    scalars = [t[6:7] + t[7:8] for t in tiles]
-    entries = [edge_rows(tiles[0][:8], None, None, scalars[0], taps_x, taps_b)]
-    for e in range(1, 4):
-        entries.append(edge_rows(tiles[e][:8], tiles[e - 1][:8], tiles[e - 1][8:], scalars[e], taps_x, taps_b))
-    edges = edge_states(entries)
-    entering = totals[0][0:HEAD] + edges[0]
-    for e in range(1, 3):
-        entering = all_lanes(scalars[e]) * entering + (totals[e][0:HEAD] + edges[e])
+    scalars = [t[6:7] + t[7:8] for t in (near[HEAD:], own)]
+    edges = edge_states(
+        [
+            edge_rows(near[HEAD : HEAD + 8], crossed[HEAD : HEAD + 8], crossed[HEAD + 8 :], scalars[0], taps_x, taps_b),
+            edge_rows(own[:8], before[:8], before[8:], scalars[1], taps_x, taps_b),
+        ]
+    )
+    entering = all_lanes(scalars[0]) * crossed[:HEAD] + (near[:HEAD] + edges[0])
+    entering = jnp.where(group == 2, crossed[:HEAD], entering)
     state_ref[0, 0:HEAD] = entering.astype(bf16)
-    state_ref[0, HEAD:] = tiles[2].astype(bf16)
-    after_first = all_lanes(scalars[3]) * entering + edges[3]
+    state_ref[0, HEAD:] = before.astype(bf16)
+    after_first = all_lanes(scalars[1]) * entering + edges[1]
     for m in range(1, GROUP):
         state_ref[m, 0:HEAD] = (prefix_ref[m] + scale_ref[m, 0:1] * after_first).astype(bf16)
         state_ref[m, HEAD:] = message_ref[m - 1, HEAD:]
@@ -424,6 +441,7 @@
         specs=[THERE] * 9,
         scratch=[
             pltpu.VMEM((LENGTH + 8, WIDTH), f32), pltpu.VMEM((LENGTH + 8, 2 * STATE), f32),
+            pltpu.VMEM((LENGTH + 8, WIDTH), f32), pltpu.VMEM((LENGTH + 8, 2 * STATE), f32),
             pltpu.VMEM((LENGTH, WIDTH), bf16), pltpu.VMEM((LENGTH, 2 * STATE), bf16),
             pltpu.VMEM((HEADS, LENGTH), f32), pltpu.SMEM((HEADS,), f32),
             pltpu.SemaphoreType.DMA((9,)),
@@ -442,18 +460,23 @@
     def permuted(a, *ways):
         return lax.ppermute(a, "seq", [(i + f * GROUP, i + t * GROUP) for f, t in ways for i in range(GROUP)])
 
-    near, skipped, other = permuted(total, (0, 1), (2, 3)), permuted(total, (1, 3)), permuted(total, (0, 3), (1, 2))
-    relayed = permuted(near, (1, 2))
+    swapped = permuted(total, (0, 1), (1, 0))
     local, gate, lead, gate_first = call(
         within_kernel,
         [((LENGTH, WIDTH), f32), ((LENGTH, WIDTH), f32), ((8, WIDTH), f32), ((8, WIDTH), f32)],
-        act, bc_act, cum, step, skip, z, near,
+        act, bc_act, cum, step, skip, z, total,
         flops=2e9, transcendentals=1.2e6,
     )
+    joined, own = call(
+        joined_kernel,
+        [((HEAD + EXTRA, 128), bf16), ((HEAD + EXTRA, 128), bf16)],
+        lead, total, swapped, taps_bc,
+    )
+    crossed, passed = permuted(joined, (1, 2), (0, 3)), permuted(own, (2, 3))
     (state,) = call(
         entering_kernel,
         [((GROUP, HEAD + EXTRA, 128), bf16)],
-        lead, message, taps_bc, prefix, scale, relayed, other, skipped, near,
+        message, taps_bc, prefix, scale, swapped, crossed, passed,
     )
     state = lax.all_to_all(state, "seq", 0, 0, tiled=True, axis_index_groups=groups)
     (share,) = call(

time: 73.5 us -> 72 us (0.980)
  starting transfers between devices: 10.9 us -> 8.76 us
    ppermute x4 -> x3, starting transfers between devices: 10.9 us -> 8.76 us  [permuted(): lax.ppermute(a, 'seq', [(i + f * GROUP, i + t * GROUP) for f, t in ways f...]
    all_to_all x1, blocking collectives: 10.2 us -> 11.4 us  [shards(): lax.all_to_all(state, 'seq', 0, 0, tiled=True, axis_index_groups=groups)]
    pallas_call x6 -> x7, Pallas kernels: 7.38 us -> 7.38 us  [call(): pl.pallas_call(kernel, out_shape=[jax.ShapeDtypeStruct(s, d) for s, d in...]
  transfers between devices with their start and end apart: 4 -> 3, of which waited for: 0 -> 2; matrix products, arithmetic and copies ran while one was open for 0% -> 0% of each run, Pallas kernels for 2% -> 2%
where the time goes in v6:
time: 72 us; the launch traced here: 71.6 us
  blocking collectives  54.8 us (76%)
  starting transfers between devices  8.76 us (12%)
  Pallas kernels  7.38 us (10%)
    all_to_all x1, blocking collectives, shards(): share = lax.all_to_all(share, 'tp', 0, 0, tiled=True)  28.2 us
    all_to_all x1, blocking collectives, shards(): lax.all_to_all(message, 'seq', 0, 0, tiled=True, axis_index_groups=groups)  15.3 us
    all_to_all x1, blocking collectives, shards(): lax.all_to_all(state, 'seq', 0, 0, tiled=True, axis_index_groups=groups)  11.4 us
    ppermute x3, starting transfers between devices, permuted(): lax.ppermute(a, 'seq', [(i + f * GROUP, i + t * GROUP) for f, t in ways f...  8.76 us
    pallas_call x7, Pallas kernels, call(): pl.pallas_call(kernel, out_shape=[jax.ShapeDtypeStruct(s, d) for s, d in...  7.38 us
  transfers between devices with their start and end apart: 3, of which 2 were waited for; matrix products, arithmetic and copies ran while one was open for 0% of the time, Pallas kernels for 2%

profile of v6, /device:TPU:1, one launch (start us, length us, event | category | flops | bytes accessed | tf_op | source)
XLA Modules:
  0.0 71.6 jit_solution(11571437508566300550)
XLA Ops:
  0.0 2.4 %shard_map.100 = (bf16[8,80,128]{2,1,0:T(8,128)(2,1)S(1)}, bf16[384,512]{1,0:T(8,128)(2,1)S(1)}, bf16[384,256]{1,0:T(8,128)(2,1)S(1)}, f32[8,384]{1,0:T(8,128)S(...) custom-call(bf16[384,512]{1,0:T(8,128)(2,1)} %x_at.1, ...), custom_call_target="tpu_custom_call" | custom-call | flops 100000000 | bytes 2000000 | tf_op jit(solution)/shard_map/pallas_call | solution.py:417
  2.5 15.3 %all_to_all.15.message_ref = bf16[8,80,128]{2,1,0:T(8,128)(2,1)S(1)} all-to-all(bf16[8,80,128]{2,1,0:T(8,128)(2,1)S(1)} %get-tuple-element.26), channel_id=1, replica_groups={{0,16,32,48,64,80,96,112},{128,144,160,176,192,208,224,240},{256,272,28..., dimensions={0} | all-to-all | bytes 327680 | tf_op jit(solution)/shard_map/all_to_all | solution.py:451
  17.7 0.4 shard_map.101
  18.1 6.8 %collective-permute-start = (bf16[80,128]{1,0:T(8,128)(2,1)S(1)}, bf16[80,128]{1,0:T(8,128)(2,1)S(1)}, u32[]{:S(2)}, u32[]{:S(2)}) collective-permute-start(bf16[80,128]{1,0:T(8,128)(2,1)S(1)} %get-tuple-element.30.after_ref.total_ref), channel_id=1, source_target_pairs={{0,128},{16,144},{32,160},{48,176},{64,192},{80,208},{96,224},{112... | collective-permute-start | bytes 61448 | tf_op jit(solution)/shard_map/ppermute | solution.py:461
  24.9 0.0 copy-start
  24.9 1.6 %shard_map.102 = (f32[384,512]{1,0:T(8,128)S(1)}, f32[384,512]{1,0:T(8,128)S(1)}, f32[8,512]{1,0:T(8,128)S(1)}, f32[8,512]{1,0:T(8,128)S(1)}) custom-call(bf16[384,512]{1,0:T(8,128)(2,1)S(1)} %get-tuple-element.31.act_ref, bf16[384,256]{1,0:T(8,128)(2,1)S(1)} %get-tuple-element.32.bc_act_ref, f32[8,384]{1,0:T(8,128)S(1)} %get-tuple-element.33.cum_ref, ...), custom_call_target="tpu_custom_call" | custom-call | flops 2000000000 | bytes 2000000 | tf_op jit(solution)/shard_map/pallas_call | solution.py:417
  26.4 0.3 collective-permute-done.swapped_ref
  26.7 0.3 shard_map.103
  27.1 1.3 %collective-permute-start.1 = (bf16[80,128]{1,0:T(8,128)(2,1)S(1)}, bf16[80,128]{1,0:T(8,128)(2,1)S(1)}, u32[]{:S(2)}, u32[]{:S(2)}) collective-permute-start(bf16[80,128]{1,0:T(8,128)(2,1)S(1)} %get-tuple-element.38), channel_id=1, source_target_pairs={{128,256},{144,272},{160,288},{176,304},{192,320},{208,336},{224,3... | collective-permute-start | bytes 61448 | tf_op jit(solution)/shard_map/ppermute | solution.py:461
  28.4 0.7 collective-permute-start.2
  29.1 0.3 collective-permute-done.1.crossed_ref
  29.4 0.0 collective-permute-done.2.passed_ref
  29.4 0.4 shard_map.104
  29.8 11.4 %all_to_all.16.state_ref = bf16[8,80,128]{2,1,0:T(8,128)(2,1)S(1)} all-to-all(bf16[8,80,128]{2,1,0:T(8,128)(2,1)S(1)} %shard_map.104), channel_id=1, replica_groups={{0,16,32,48,64,80,96,112},{128,144,160,176,192,208,224,240},{256,272,28..., dimensions={0} | all-to-all | bytes 327680 | tf_op jit(solution)/shard_map/all_to_all | solution.py:481
  41.1 0.0 copy-done
  41.1 1.4 %shard_map.105 = bf16[16,400,128]{2,1,0:T(8,128)(2,1)S(1)} custom-call(bf16[8,80,128]{2,1,0:T(8,128)(2,1)S(1)} %all_to_all.16.state_ref, bf16[384,256]{1,0:T(8,128)(2,1)S(1)} %get-tuple-element.32.bc_act_ref, f32[8,512]{1,0:T(8,128)S(1)} %get-tuple-element.40.first_x_ref, f32[8,256]{1,0:T(8,128)S(1)} %get-tuple-element.41.first_bc_ref, ...), custom_call_target="tpu_custom_call" | custom-call | flops 900000000 | bytes 2000000 | tf_op jit(solution)/shard_map/pallas_call | solution.py:417
  42.5 28.2 %all_to_all.17.share_ref = bf16[16,400,128]{2,1,0:T(8,128)(2,1)S(1)} all-to-all(bf16[16,400,128]{2,1,0:T(8,128)(2,1)S(1)} %shard_map.105), channel_id=1, replica_groups=mesh['seq'=32,'tp'=16] {'tp'}, dimensions={0} | all-to-all | bytes 3276800 | tf_op jit(solution)/shard_map/all_to_all | solution.py:488
  70.7 0.9 %shard_map.106 = bf16[384,128]{1,0:T(8,128)(2,1)} custom-call(bf16[16,400,128]{2,1,0:T(8,128)(2,1)S(1)} %all_to_all.17.share_ref), custom_call_target="tpu_custom_call" | custom-call | flops 100000000 | bytes 2000000 | tf_op jit(solution)/shard_map/pallas_call | solution.py:417
Async XLA Ops:
  18.1 8.6 %collective-permute-start = (bf16[80,128]{1,0:T(8,128)(2,1)S(1)}, bf16[80,128]{1,0:T(8,128)(2,1)S(1)}, u32[]{:S(2)}, u32[]{:S(2)}) collective-permute-start(bf16[80,128]{1,0:T(8,128)(2,1)S(1)} %get-tuple-element.30.after_ref.total_ref), channel_id=1, source_target_pairs={{0,128},{16,144},{32,160},{48,176},{64,192},{80,208},{96,224},{112... | collective-permute-start | bytes 61448 | tf_op jit(solution)/shard_map/ppermute | solution.py:461
  24.9 16.3 %copy-start = (bf16[512,2048]{1,0:T(8,128)(2,1)S(1)}, bf16[512,2048]{1,0:T(8,128)(2,1)}, u32[]{:S(2)}) copy-start(bf16[512,2048]{1,0:T(8,128)(2,1)} %weight_ref.1) | copy-start | bytes 6291460
  27.1 2.3 %collective-permute-start.1 = (bf16[80,128]{1,0:T(8,128)(2,1)S(1)}, bf16[80,128]{1,0:T(8,128)(2,1)S(1)}, u32[]{:S(2)}, u32[]{:S(2)}) collective-permute-start(bf16[80,128]{1,0:T(8,128)(2,1)S(1)} %get-tuple-element.38), channel_id=1, source_target_pairs={{128,256},{144,272},{160,288},{176,304},{192,320},{208,336},{224,3... | collective-permute-start | bytes 61448 | tf_op jit(solution)/shard_map/ppermute | solution.py:461
  28.4 1.0 %collective-permute-start.2 = (bf16[80,128]{1,0:T(8,128)(2,1)S(1)}, bf16[80,128]{1,0:T(8,128)(2,1)S(1)}, u32[]{:S(2)}, u32[]{:S(2)}) collective-permute-start(bf16[80,128]{1,0:T(8,128)(2,1)S(1)} %get-tuple-element.39), channel_id=1, source_target_pairs={{256,384},{272,400},{288,416},{304,432},{320,448},{336,464},{352,4... | collective-permute-start | bytes 61448 | tf_op jit(solution)/shard_map/ppermute | solution.py:461

commit v7 on v6

--- a/solution.py
+++ b/solution.py
@@ -133,7 +133,9 @@
     summary = dot(b_rows.T.astype(bf16), weighted)
 
     total = jnp.broadcast_to(jnp.exp(last), (HEADS, 128))
-    scalars = jnp.where(iota((HEADS, 128), 1) < HEAD, factor[:, :128], total)
+    lane = iota((HEADS, 128), 1)
+    lead = step_ref[:, :128] * jnp.exp(jnp.where(lane < EDGE, -cum[:, :128], 0.0))
+    scalars = jnp.where(lane < HEAD, lead, total)
     high, middle, _ = (p.astype(f32) for p in parts3(scalars))
     tap_high, tap_middle, _ = (p.astype(f32) for p in parts3(taps_x_ref[...]))
     low_lanes = iota((HEAD, 128), 1) < HEAD
@@ -253,7 +255,7 @@
     return [dot(left, jnp.where(owner == e, weighted, 0.0).astype(bf16)) for e in range(len(entries))]
 
 
-def prefix_kernel(message_ref, taps_ref, prefix_ref, scale_ref, total_ref):
+def prefix_kernel(message_ref, taps_ref, prefix_ref, scale_ref, edge_ref, total_ref):
     tiles = [message_ref[m, HEAD:].astype(f32) for m in range(GROUP)]
     scalars = [t[6:7] + t[7:8] for t in tiles]
     decays = [all_lanes(s) for s in scalars]
@@ -268,11 +270,12 @@
     for m in range(1, GROUP):
         prefix_ref[m] = state
         scale_ref[m] = jnp.broadcast_to(scale, (8, 128))
-        state = decays[m] * state + (message_ref[m, 0:HEAD].astype(f32) + edges[m - 1])
+        edge_ref[m] = edges[m - 1]
+        state = decays[m] * (state + edges[m - 1]) + message_ref[m, 0:HEAD].astype(f32)
         scale = decays[m] * scale
     total_ref[0:HEAD] = state.astype(bf16)
     lane = iota((1, 128), 1)
-    high, middle, _ = (p.astype(f32) for p in parts3(jnp.where(lane < HEAD, scalars[0] * scale, decays[0] * scale)))
+    high, middle, _ = (p.astype(f32) for p in parts3(jnp.where(lane < HEAD, scalars[0], decays[0] * scale)))
     row = iota((8, 128), 0)
     first, last = tiles[0][:8], tiles[GROUP - 1]
     tile = jnp.where((row < EDGE) & (iota((8, 128), 1) >= HEAD), last[:8], first)
@@ -294,14 +297,15 @@
             edge_rows(tiles[1][:8], tiles[0][:8], tiles[0][8:], scalars[1], taps_x, taps_b),
         ]
     )
-    state = all_lanes(scalars[1]) * (first[:HEAD] + edges[0]) + (second[:HEAD] + edges[1])
+    state = all_lanes(scalars[0]) * edges[0] + first[:HEAD]
+    state = all_lanes(scalars[1]) * (state + edges[1]) + second[:HEAD]
     joined_ref[0:HEAD] = state.astype(bf16)
     joined_ref[HEAD:] = tiles[1].astype(bf16)
     own_ref[...] = total_ref[...]
 
 
 def entering_kernel(
-    message_ref, taps_ref, prefix_ref, scale_ref, swapped_ref, crossed_ref, passed_ref, state_ref
+    message_ref, taps_ref, prefix_ref, scale_ref, edge_ref, swapped_ref, crossed_ref, passed_ref, state_ref
 ):
     group = lax.axis_index("seq") // GROUP
     crossed = crossed_ref[...].astype(f32)
@@ -317,13 +321,15 @@
             edge_rows(own[:8], before[:8], before[8:], scalars[1], taps_x, taps_b),
         ]
     )
-    entering = all_lanes(scalars[0]) * crossed[:HEAD] + (near[:HEAD] + edges[0])
+    entering = all_lanes(scalars[0]) * (crossed[:HEAD] + edges[0]) + near[:HEAD]
     entering = jnp.where(group == 2, crossed[:HEAD], entering)
+    entering = entering + edges[1]
     state_ref[0, 0:HEAD] = entering.astype(bf16)
     state_ref[0, HEAD:] = before.astype(bf16)
-    after_first = all_lanes(scalars[1]) * entering + edges[1]
+    after_first = all_lanes(scalars[1]) * entering
     for m in range(1, GROUP):
-        state_ref[m, 0:HEAD] = (prefix_ref[m] + scale_ref[m, 0:1] * after_first).astype(bf16)
+        state = prefix_ref[m] + scale_ref[m, 0:1] * after_first + edge_ref[m]
+        state_ref[m, 0:HEAD] = state.astype(bf16)
         state_ref[m, HEAD:] = message_ref[m - 1, HEAD:]
 
 
@@ -360,9 +366,7 @@
         bottom = jnp.where(low_lanes, rolled(even, HEAD, 1), odd)
         pairs.append(jnp.concatenate([top, bottom], axis=0))
     states = jnp.concatenate(pairs, axis=1)
-    b_columns = jnp.concatenate([b_first, jnp.zeros((120, STATE), f32)], axis=0).T.astype(bf16)
-    lead_rows = jnp.concatenate([lead, jnp.zeros((120, WIDTH), f32)], axis=0).astype(bf16)
-    states = (states + dot(b_columns, lead_rows)).astype(bf16)
+    states = states.astype(bf16)
     c_rows = jnp.concatenate([c_first, bc_act_ref[:, STATE:].astype(f32)[8:]], axis=0).astype(bf16)
     gated = local_ref[...] + gate_ref[...] * dot(c_rows, states)
     ahead = jnp.zeros((8, WIDTH), f32)
@@ -374,14 +378,13 @@
 
     squares = jnp.sum(gated * gated, axis=1, keepdims=True)
     scaled = (gated * gain_ref[...]).astype(bf16)
-    wide = jnp.broadcast_to(squares, (LENGTH, 128))
-    row_at = lax.broadcasted_iota(jnp.int32, (EXTRA, 128), 0)
-    extra = jnp.zeros((EXTRA, 128), f32)
+    lane = iota((BLOCK, 128), 1)
+    wide = jnp.zeros((BLOCK, 128), f32)
     for block in range(LENGTH // BLOCK):
-        row = wide[block * BLOCK : (block + 1) * BLOCK].T[0:1]
-        for k, part in enumerate(parts3(row)):
-            extra = jnp.where(row_at == 3 * block + k, part.astype(f32), extra)
-    extra = extra.astype(bf16)
+        wide = jnp.where(lane == block, squares[block * BLOCK : (block + 1) * BLOCK], wide)
+    high, middle, low = (p.astype(f32) for p in parts3(wide.T[0:8]))
+    extra = jnp.where(row < 3, high, jnp.where(row < 6, rolled(middle, 3, 0), 0.0))
+    extra = jnp.concatenate([extra, jnp.where(row < 3, low, 0.0)], axis=0).astype(bf16)
     for pair in range(SHARES // 2):
         product = dot(scaled, weight_ref[:, 256 * pair : 256 * (pair + 1)]).astype(bf16)
         share_ref[2 * pair, 0:LENGTH] = product[:, :128]
@@ -397,9 +400,7 @@
     extra = total[LENGTH:]
     for block in range(LENGTH // BLOCK):
         rows = slice(block * BLOCK, (block + 1) * BLOCK)
-        squares = extra[3 * block : 3 * block + 1] + (
-            extra[3 * block + 1 : 3 * block + 2] + extra[3 * block + 2 : 3 * block + 3]
-        )
+        squares = extra[block : block + 1] + (extra[block + 3 : block + 4] + extra[block + 8 : block + 9])
         scale = lax.rsqrt(squares / INNER + 1e-05)
         column = jnp.broadcast_to(scale, (128, 128)).T
         out_ref[rows] = (total[rows] * column).astype(bf16)
@@ -449,9 +450,9 @@
     )
     groups = [list(range(i, i + GROUP)) for i in range(0, BLOCKS, GROUP)]
     message = lax.all_to_all(message, "seq", 0, 0, tiled=True, axis_index_groups=groups)
-    prefix, scale, total = call(
+    prefix, scale, edge, total = call(
         prefix_kernel,
-        [((GROUP, HEAD, 128), f32), ((GROUP, 8, 128), f32), ((HEAD + EXTRA, 128), bf16)],
+        [((GROUP, HEAD, 128), f32), ((GROUP, 8, 128), f32), ((GROUP, HEAD, 128), f32), ((HEAD + EXTRA, 128), bf16)],
         message, taps_bc,
     )
     def later(a, distance, first, last):
@@ -476,7 +477,7 @@
     (state,) = call(
         entering_kernel,
         [((GROUP, HEAD + EXTRA, 128), bf16)],
-        message, taps_bc, prefix, scale, swapped, crossed, passed,
+        message, taps_bc, prefix, scale, edge, swapped, crossed, passed,
     )
     state = lax.all_to_all(state, "seq", 0, 0, tiled=True, axis_index_groups=groups)
     (share,) = call(

time: 72 us -> 71.9 us (level)
  no operation moved by 1% of the time
where the time goes in v7:
time: 71.9 us; the launch traced here: 71.4 us
  blocking collectives  54.9 us (76%)
  starting transfers between devices  8.76 us (12%)
  Pallas kernels  7.24 us (10%)
    all_to_all x1, blocking collectives, shards(): share = lax.all_to_all(share, 'tp', 0, 0, tiled=True)  28.2 us
    all_to_all x1, blocking collectives, shards(): lax.all_to_all(message, 'seq', 0, 0, tiled=True, axis_index_groups=groups)  15.3 us
    all_to_all x1, blocking collectives, shards(): lax.all_to_all(state, 'seq', 0, 0, tiled=True, axis_index_groups=groups)  11.4 us
    ppermute x3, starting transfers between devices, permuted(): lax.ppermute(a, 'seq', [(i + f * GROUP, i + t * GROUP) for f, t in ways f...  8.76 us
    pallas_call x7, Pallas kernels, call(): pl.pallas_call(kernel, out_shape=[jax.ShapeDtypeStruct(s, d) for s, d in...  7.24 us
  transfers between devices with their start and end apart: 3, of which 2 were waited for; matrix products, arithmetic and copies ran while one was open for 0% of the time, Pallas kernels for 2%

profile of v7, /device:TPU:1, one launch (start us, length us, event | category | flops | bytes accessed | tf_op | source)
XLA Modules:
  0.0 71.4 jit_solution(2602550961169598835)
XLA Ops:
  0.0 2.4 %shard_map.100 = (bf16[8,80,128]{2,1,0:T(8,128)(2,1)S(1)}, bf16[384,512]{1,0:T(8,128)(2,1)S(1)}, bf16[384,256]{1,0:T(8,128)(2,1)S(1)}, f32[8,384]{1,0:T(8,128)S(...) custom-call(bf16[384,512]{1,0:T(8,128)(2,1)} %x_at.1, ...), custom_call_target="tpu_custom_call" | custom-call | flops 100000000 | bytes 2000000 | tf_op jit(solution)/shard_map/pallas_call | solution.py:418
  2.5 15.3 %all_to_all.15.message_ref = bf16[8,80,128]{2,1,0:T(8,128)(2,1)S(1)} all-to-all(bf16[8,80,128]{2,1,0:T(8,128)(2,1)S(1)} %get-tuple-element.27), channel_id=1, replica_groups={{0,16,32,48,64,80,96,112},{128,144,160,176,192,208,224,240},{256,272,28..., dimensions={0} | all-to-all | bytes 327680 | tf_op jit(solution)/shard_map/all_to_all | solution.py:452
  17.7 0.4 shard_map.101
  18.1 6.8 %collective-permute-start = (bf16[80,128]{1,0:T(8,128)(2,1)S(1)}, bf16[80,128]{1,0:T(8,128)(2,1)S(1)}, u32[]{:S(2)}, u32[]{:S(2)}) collective-permute-start(bf16[80,128]{1,0:T(8,128)(2,1)S(1)} %get-tuple-element.32.after_ref.total_ref), channel_id=1, source_target_pairs={{0,128},{16,144},{32,160},{48,176},{64,192},{80,208},{96,224},{112... | collective-permute-start | bytes 61448 | tf_op jit(solution)/shard_map/ppermute | solution.py:462
  24.9 0.0 copy-start
  24.9 1.6 %shard_map.102 = (f32[384,512]{1,0:T(8,128)S(1)}, f32[384,512]{1,0:T(8,128)S(1)}, f32[8,512]{1,0:T(8,128)S(1)}, f32[8,512]{1,0:T(8,128)S(1)}) custom-call(bf16[384,512]{1,0:T(8,128)(2,1)S(1)} %get-tuple-element.33.act_ref, bf16[384,256]{1,0:T(8,128)(2,1)S(1)} %get-tuple-element.34.bc_act_ref, f32[8,384]{1,0:T(8,128)S(1)} %get-tuple-element.35.cum_ref, ...), custom_call_target="tpu_custom_call" | custom-call | flops 2000000000 | bytes 2000000 | tf_op jit(solution)/shard_map/pallas_call | solution.py:418
  26.5 0.3 collective-permute-done.swapped_ref
  26.7 0.3 shard_map.103
  27.1 1.3 %collective-permute-start.1 = (bf16[80,128]{1,0:T(8,128)(2,1)S(1)}, bf16[80,128]{1,0:T(8,128)(2,1)S(1)}, u32[]{:S(2)}, u32[]{:S(2)}) collective-permute-start(bf16[80,128]{1,0:T(8,128)(2,1)S(1)} %get-tuple-element.40), channel_id=1, source_target_pairs={{128,256},{144,272},{160,288},{176,304},{192,320},{208,336},{224,3... | collective-permute-start | bytes 61448 | tf_op jit(solution)/shard_map/ppermute | solution.py:462
  28.4 0.7 collective-permute-start.2
  29.1 0.2 collective-permute-done.1.crossed_ref
  29.3 0.0 collective-permute-done.2.passed_ref
  29.3 0.4 shard_map.104
  29.7 11.4 %all_to_all.16.state_ref = bf16[8,80,128]{2,1,0:T(8,128)(2,1)S(1)} all-to-all(bf16[8,80,128]{2,1,0:T(8,128)(2,1)S(1)} %shard_map.104), channel_id=1, replica_groups={{0,16,32,48,64,80,96,112},{128,144,160,176,192,208,224,240},{256,272,28..., dimensions={0} | all-to-all | bytes 327680 | tf_op jit(solution)/shard_map/all_to_all | solution.py:482
  41.2 0.0 copy-done
  41.2 1.2 %shard_map.105 = bf16[16,400,128]{2,1,0:T(8,128)(2,1)S(1)} custom-call(bf16[8,80,128]{2,1,0:T(8,128)(2,1)S(1)} %all_to_all.16.state_ref, bf16[384,256]{1,0:T(8,128)(2,1)S(1)} %get-tuple-element.34.bc_act_ref, f32[8,512]{1,0:T(8,128)S(1)} %get-tuple-element.42.first_x_ref, f32[8,256]{1,0:T(8,128)S(1)} %get-tuple-element.43.first_bc_ref, ...), custom_call_target="tpu_custom_call" | custom-call | flops 900000000 | bytes 2000000 | tf_op jit(solution)/shard_map/pallas_call | solution.py:418
  42.4 28.2 %all_to_all.17.share_ref = bf16[16,400,128]{2,1,0:T(8,128)(2,1)S(1)} all-to-all(bf16[16,400,128]{2,1,0:T(8,128)(2,1)S(1)} %shard_map.105), channel_id=1, replica_groups=mesh['seq'=32,'tp'=16] {'tp'}, dimensions={0} | all-to-all | bytes 3276800 | tf_op jit(solution)/shard_map/all_to_all | solution.py:489
  70.6 0.9 %shard_map.106 = bf16[384,128]{1,0:T(8,128)(2,1)} custom-call(bf16[16,400,128]{2,1,0:T(8,128)(2,1)S(1)} %all_to_all.17.share_ref), custom_call_target="tpu_custom_call" | custom-call | flops 100000000 | bytes 2000000 | tf_op jit(solution)/shard_map/pallas_call | solution.py:418
Async XLA Ops:
  18.1 8.6 %collective-permute-start = (bf16[80,128]{1,0:T(8,128)(2,1)S(1)}, bf16[80,128]{1,0:T(8,128)(2,1)S(1)}, u32[]{:S(2)}, u32[]{:S(2)}) collective-permute-start(bf16[80,128]{1,0:T(8,128)(2,1)S(1)} %get-tuple-element.32.after_ref.total_ref), channel_id=1, source_target_pairs={{0,128},{16,144},{32,160},{48,176},{64,192},{80,208},{96,224},{112... | collective-permute-start | bytes 61448 | tf_op jit(solution)/shard_map/ppermute | solution.py:462
  24.9 16.3 %copy-start = (bf16[512,2048]{1,0:T(8,128)(2,1)S(1)}, bf16[512,2048]{1,0:T(8,128)(2,1)}, u32[]{:S(2)}) copy-start(bf16[512,2048]{1,0:T(8,128)(2,1)} %weight_ref.1) | copy-start | bytes 6291460
  27.1 2.3 %collective-permute-start.1 = (bf16[80,128]{1,0:T(8,128)(2,1)S(1)}, bf16[80,128]{1,0:T(8,128)(2,1)S(1)}, u32[]{:S(2)}, u32[]{:S(2)}) collective-permute-start(bf16[80,128]{1,0:T(8,128)(2,1)S(1)} %get-tuple-element.40), channel_id=1, source_target_pairs={{128,256},{144,272},{160,288},{176,304},{192,320},{208,336},{224,3... | collective-permute-start | bytes 61448 | tf_op jit(solution)/shard_map/ppermute | solution.py:462
  28.4 0.9 %collective-permute-start.2 = (bf16[80,128]{1,0:T(8,128)(2,1)S(1)}, bf16[80,128]{1,0:T(8,128)(2,1)S(1)}, u32[]{:S(2)}, u32[]{:S(2)}) collective-permute-start(bf16[80,128]{1,0:T(8,128)(2,1)S(1)} %get-tuple-element.41), channel_id=1, source_target_pairs={{256,384},{272,400},{288,416},{304,432},{320,448},{336,464},{352,4... | collective-permute-start | bytes 61448 | tf_op jit(solution)/shard_map/ppermute | solution.py:462

commit v8 on v7

--- a/solution.py
+++ b/solution.py
@@ -304,29 +304,52 @@
     own_ref[...] = total_ref[...]
 
 
-def entering_kernel(
-    message_ref, taps_ref, prefix_ref, scale_ref, edge_ref, swapped_ref, crossed_ref, passed_ref, state_ref
-):
-    group = lax.axis_index("seq") // GROUP
-    crossed = crossed_ref[...].astype(f32)
-    near = jnp.where(group == 1, swapped_ref[...].astype(f32), passed_ref[...].astype(f32))
+def entered(message_ref, taps_ref, near, crossed, third):
     own = message_ref[0, HEAD:].astype(f32)
-    before = jnp.where(group == 2, crossed[HEAD:], near[HEAD:])
+    before = near[HEAD:] if third is None else jnp.where(third, crossed[HEAD:], near[HEAD:])
     taps_x = taps_of(own[8:])
     taps_b = [taps_ref[k : k + 1, :STATE] for k in range(4)]
     scalars = [t[6:7] + t[7:8] for t in (near[HEAD:], own)]
+    edge, last = (None, None) if crossed is None else (crossed[HEAD : HEAD + 8], crossed[HEAD + 8 :])
     edges = edge_states(
         [
-            edge_rows(near[HEAD : HEAD + 8], crossed[HEAD : HEAD + 8], crossed[HEAD + 8 :], scalars[0], taps_x, taps_b),
+            edge_rows(near[HEAD : HEAD + 8], edge, last, scalars[0], taps_x, taps_b),
             edge_rows(own[:8], before[:8], before[8:], scalars[1], taps_x, taps_b),
         ]
     )
-    entering = all_lanes(scalars[0]) * (crossed[:HEAD] + edges[0]) + near[:HEAD]
-    entering = jnp.where(group == 2, crossed[:HEAD], entering)
-    entering = entering + edges[1]
+    if crossed is None:
+        entering = all_lanes(scalars[0]) * edges[0] + near[:HEAD]
+    else:
+        entering = all_lanes(scalars[0]) * (crossed[:HEAD] + edges[0]) + near[:HEAD]
+        entering = jnp.where(third, crossed[:HEAD], entering)
+    return jnp.concatenate([entering + edges[1], before], axis=0)
+
+
+def early_kernel(own_ref, message_ref, taps_ref, swapped_ref, early_ref):
+    second = lax.axis_index("seq") // GROUP == 1
+    near = jnp.where(second, swapped_ref[...].astype(f32), 0.0)
+    early_ref[...] = entered(message_ref, taps_ref, near, None, None)
+
+
+def entering_kernel(
+    message_ref, taps_ref, prefix_ref, scale_ref, edge_ref, early_ref, crossed_ref, passed_ref, state_ref, entered_ref
+):
+    group = lax.axis_index("seq") // GROUP
+
+    @pl.when(group < 2)
+    def _():
+        entered_ref[...] = early_ref[...]
+
+    @pl.when(group >= 2)
+    def _():
+        crossed, near = crossed_ref[...].astype(f32), passed_ref[...].astype(f32)
+        entered_ref[...] = entered(message_ref, taps_ref, near, crossed, group == 2)
+
+    own = message_ref[0, HEAD:].astype(f32)
+    entering = entered_ref[0:HEAD]
     state_ref[0, 0:HEAD] = entering.astype(bf16)
-    state_ref[0, HEAD:] = before.astype(bf16)
-    after_first = all_lanes(scalars[1]) * entering
+    state_ref[0, HEAD:] = entered_ref[HEAD:].astype(bf16)
+    after_first = all_lanes(own[6:7] + own[7:8]) * entering
     for m in range(1, GROUP):
         state = prefix_ref[m] + scale_ref[m, 0:1] * after_first + edge_ref[m]
         state_ref[m, 0:HEAD] = state.astype(bf16)
@@ -474,10 +497,12 @@
         lead, total, swapped, taps_bc,
     )
     crossed, passed = permuted(joined, (1, 2), (0, 3)), permuted(own, (2, 3))
+    (early,) = call(early_kernel, [((HEAD + EXTRA, 128), f32)], own, message, taps_bc, swapped)
     (state,) = call(
         entering_kernel,
         [((GROUP, HEAD + EXTRA, 128), bf16)],
-        message, taps_bc, prefix, scale, edge, swapped, crossed, passed,
+        message, taps_bc, prefix, scale, edge, early, crossed, passed,
+        scratch=[pltpu.VMEM((HEAD + EXTRA, 128), f32)],
     )
     state = lax.all_to_all(state, "seq", 0, 0, tiled=True, axis_index_groups=groups)
     (share,) = call(

time: 71.9 us -> 71.6 us (level)
    pallas_call x7 -> x8, Pallas kernels: 7.24 us -> 7.34 us  [call(): pl.pallas_call(kernel, out_shape=[jax.ShapeDtypeStruct(s, d) for s, d in...]
  transfers between devices with their start and end apart: 3 -> 3, of which waited for: 2 -> 1; matrix products, arithmetic and copies ran while one was open for 0% -> 0% of each run, Pallas kernels for 2% -> 3%
where the time goes in v8:
time: 71.6 us; the launch traced here: 71.2 us
  blocking collectives  54.7 us (76%)
  starting transfers between devices  8.76 us (12%)
  Pallas kernels  7.34 us (10%)
    all_to_all x1, blocking collectives, shards(): share = lax.all_to_all(share, 'tp', 0, 0, tiled=True)  28.2 us
    all_to_all x1, blocking collectives, shards(): lax.all_to_all(message, 'seq', 0, 0, tiled=True, axis_index_groups=groups)  15.3 us
    all_to_all x1, blocking collectives, shards(): lax.all_to_all(state, 'seq', 0, 0, tiled=True, axis_index_groups=groups)  11.3 us
    ppermute x3, starting transfers between devices, permuted(): lax.ppermute(a, 'seq', [(i + f * GROUP, i + t * GROUP) for f, t in ways f...  8.76 us
    pallas_call x8, Pallas kernels, call(): pl.pallas_call(kernel, out_shape=[jax.ShapeDtypeStruct(s, d) for s, d in...  7.34 us
  transfers between devices with their start and end apart: 3, of which 1 were waited for; matrix products, arithmetic and copies ran while one was open for 0% of the time, Pallas kernels for 3%

profile of v8, /device:TPU:1, one launch (start us, length us, event | category | flops | bytes accessed | tf_op | source)
XLA Modules:
  0.0 71.2 jit_solution(3629964072805107354)
XLA Ops:
  0.0 2.4 %shard_map.100 = (bf16[8,80,128]{2,1,0:T(8,128)(2,1)S(1)}, bf16[384,512]{1,0:T(8,128)(2,1)S(1)}, bf16[384,256]{1,0:T(8,128)(2,1)S(1)}, f32[8,384]{1,0:T(8,128)S(...) custom-call(bf16[384,512]{1,0:T(8,128)(2,1)} %x_at.1, ...), custom_call_target="tpu_custom_call" | custom-call | flops 100000000 | bytes 2000000 | tf_op jit(solution)/shard_map/pallas_call | solution.py:441
  2.5 15.3 %all_to_all.15.message_ref = bf16[8,80,128]{2,1,0:T(8,128)(2,1)S(1)} all-to-all(bf16[8,80,128]{2,1,0:T(8,128)(2,1)S(1)} %get-tuple-element.27), channel_id=1, replica_groups={{0,16,32,48,64,80,96,112},{128,144,160,176,192,208,224,240},{256,272,28..., dimensions={0} | all-to-all | bytes 327680 | tf_op jit(solution)/shard_map/all_to_all | solution.py:475
  17.7 0.4 shard_map.101
  18.1 6.8 %collective-permute-start = (bf16[80,128]{1,0:T(8,128)(2,1)S(1)}, bf16[80,128]{1,0:T(8,128)(2,1)S(1)}, u32[]{:S(2)}, u32[]{:S(2)}) collective-permute-start(bf16[80,128]{1,0:T(8,128)(2,1)S(1)} %get-tuple-element.38.after_ref.total_ref), channel_id=1, source_target_pairs={{0,128},{16,144},{32,160},{48,176},{64,192},{80,208},{96,224},{112... | collective-permute-start | bytes 61448 | tf_op jit(solution)/shard_map/ppermute | solution.py:485
  24.9 0.0 copy-start
  24.9 1.6 %shard_map.102 = (f32[384,512]{1,0:T(8,128)S(1)}, f32[384,512]{1,0:T(8,128)S(1)}, f32[8,512]{1,0:T(8,128)S(1)}, f32[8,512]{1,0:T(8,128)S(1)}) custom-call(bf16[384,512]{1,0:T(8,128)(2,1)S(1)} %get-tuple-element.32.act_ref, bf16[384,256]{1,0:T(8,128)(2,1)S(1)} %get-tuple-element.33.bc_act_ref, f32[8,384]{1,0:T(8,128)S(1)} %get-tuple-element.34.cum_ref, ...), custom_call_target="tpu_custom_call" | custom-call | flops 2000000000 | bytes 2000000 | tf_op jit(solution)/shard_map/pallas_call | solution.py:441
  26.5 0.3 collective-permute-done.swapped_ref
  26.7 0.3 shard_map.103
  27.1 1.3 %collective-permute-start.1 = (bf16[80,128]{1,0:T(8,128)(2,1)S(1)}, bf16[80,128]{1,0:T(8,128)(2,1)S(1)}, u32[]{:S(2)}, u32[]{:S(2)}) collective-permute-start(bf16[80,128]{1,0:T(8,128)(2,1)S(1)} %get-tuple-element.41), channel_id=1, source_target_pairs={{128,256},{144,272},{160,288},{176,304},{192,320},{208,336},{224,3... | collective-permute-start | bytes 61448 | tf_op jit(solution)/shard_map/ppermute | solution.py:485
  28.4 0.7 collective-permute-start.2
  29.1 0.3 shard_map.104.early_ref
  29.5 0.0 collective-permute-done.1.crossed_ref
  29.5 0.0 collective-permute-done.2.passed_ref
  29.5 0.1 shard_map.105
  29.6 11.3 %all_to_all.16.state_ref = bf16[8,80,128]{2,1,0:T(8,128)(2,1)S(1)} all-to-all(bf16[8,80,128]{2,1,0:T(8,128)(2,1)S(1)} %shard_map.105), channel_id=1, replica_groups={{0,16,32,48,64,80,96,112},{128,144,160,176,192,208,224,240},{256,272,28..., dimensions={0} | all-to-all | bytes 327680 | tf_op jit(solution)/shard_map/all_to_all | solution.py:507
  40.9 0.0 copy-done
  40.9 1.2 %shard_map.106 = bf16[16,400,128]{2,1,0:T(8,128)(2,1)S(1)} custom-call(bf16[8,80,128]{2,1,0:T(8,128)(2,1)S(1)} %all_to_all.16.state_ref, bf16[384,256]{1,0:T(8,128)(2,1)S(1)} %get-tuple-element.33.bc_act_ref, f32[8,512]{1,0:T(8,128)S(1)} %get-tuple-element.42.first_x_ref, f32[8,256]{1,0:T(8,128)S(1)} %get-tuple-element.43.first_bc_ref, ...), custom_call_target="tpu_custom_call" | custom-call | flops 900000000 | bytes 2000000 | tf_op jit(solution)/shard_map/pallas_call | solution.py:441
  42.1 28.2 %all_to_all.17.share_ref = bf16[16,400,128]{2,1,0:T(8,128)(2,1)S(1)} all-to-all(bf16[16,400,128]{2,1,0:T(8,128)(2,1)S(1)} %shard_map.106), channel_id=1, replica_groups=mesh['seq'=32,'tp'=16] {'tp'}, dimensions={0} | all-to-all | bytes 3276800 | tf_op jit(solution)/shard_map/all_to_all | solution.py:514
  70.3 0.9 %shard_map.107 = bf16[384,128]{1,0:T(8,128)(2,1)} custom-call(bf16[16,400,128]{2,1,0:T(8,128)(2,1)S(1)} %all_to_all.17.share_ref), custom_call_target="tpu_custom_call" | custom-call | flops 100000000 | bytes 2000000 | tf_op jit(solution)/shard_map/pallas_call | solution.py:441
Async XLA Ops:
  18.1 8.6 %collective-permute-start = (bf16[80,128]{1,0:T(8,128)(2,1)S(1)}, bf16[80,128]{1,0:T(8,128)(2,1)S(1)}, u32[]{:S(2)}, u32[]{:S(2)}) collective-permute-start(bf16[80,128]{1,0:T(8,128)(2,1)S(1)} %get-tuple-element.38.after_ref.total_ref), channel_id=1, source_target_pairs={{0,128},{16,144},{32,160},{48,176},{64,192},{80,208},{96,224},{112... | collective-permute-start | bytes 61448 | tf_op jit(solution)/shard_map/ppermute | solution.py:485
  24.9 16.0 %copy-start = (bf16[512,2048]{1,0:T(8,128)(2,1)S(1)}, bf16[512,2048]{1,0:T(8,128)(2,1)}, u32[]{:S(2)}) copy-start(bf16[512,2048]{1,0:T(8,128)(2,1)} %weight_ref.1) | copy-start | bytes 6291460
  27.1 2.4 %collective-permute-start.1 = (bf16[80,128]{1,0:T(8,128)(2,1)S(1)}, bf16[80,128]{1,0:T(8,128)(2,1)S(1)}, u32[]{:S(2)}, u32[]{:S(2)}) collective-permute-start(bf16[80,128]{1,0:T(8,128)(2,1)S(1)} %get-tuple-element.41), channel_id=1, source_target_pairs={{128,256},{144,272},{160,288},{176,304},{192,320},{208,336},{224,3... | collective-permute-start | bytes 61448 | tf_op jit(solution)/shard_map/ppermute | solution.py:485
  28.4 1.0 %collective-permute-start.2 = (bf16[80,128]{1,0:T(8,128)(2,1)S(1)}, bf16[80,128]{1,0:T(8,128)(2,1)S(1)}, u32[]{:S(2)}, u32[]{:S(2)}) collective-permute-start(bf16[80,128]{1,0:T(8,128)(2,1)S(1)} %get-tuple-element.40.own_ref), channel_id=1, source_target_pairs={{256,384},{272,400},{288,416},{304,432},{320,448},{336,464},{352,4... | collective-permute-start | bytes 61448 | tf_op jit(solution)/shard_map/ppermute | solution.py:485

commit v9 on v8

--- a/solution.py
+++ b/solution.py
@@ -408,12 +408,11 @@
     high, middle, low = (p.astype(f32) for p in parts3(wide.T[0:8]))
     extra = jnp.where(row < 3, high, jnp.where(row < 6, rolled(middle, 3, 0), 0.0))
     extra = jnp.concatenate([extra, jnp.where(row < 3, low, 0.0)], axis=0).astype(bf16)
-    for pair in range(SHARES // 2):
-        product = dot(scaled, weight_ref[:, 256 * pair : 256 * (pair + 1)]).astype(bf16)
-        share_ref[2 * pair, 0:LENGTH] = product[:, :128]
-        share_ref[2 * pair, LENGTH:] = extra
-        share_ref[2 * pair + 1, 0:LENGTH] = product[:, 128:]
-        share_ref[2 * pair + 1, LENGTH:] = extra
+    for four in range(SHARES // 4):
+        product = dot(scaled, weight_ref[:, 512 * four : 512 * (four + 1)]).astype(bf16)
+        for k in range(4):
+            share_ref[4 * four + k, 0:LENGTH] = product[:, 128 * k : 128 * (k + 1)]
+            share_ref[4 * four + k, LENGTH:] = extra
 
 
 def sum_kernel(share_ref, out_ref):

time: 71.6 us -> 71.6 us (level)
  no operation moved by 1% of the time
where the time goes in v9:
time: 71.6 us; the launch traced here: 71.2 us
  blocking collectives  54.7 us (76%)
  starting transfers between devices  8.76 us (12%)
  Pallas kernels  7.34 us (10%)
    all_to_all x1, blocking collectives, shards(): share = lax.all_to_all(share, 'tp', 0, 0, tiled=True)  28.2 us
    all_to_all x1, blocking collectives, shards(): lax.all_to_all(message, 'seq', 0, 0, tiled=True, axis_index_groups=groups)  15.3 us
    all_to_all x1, blocking collectives, shards(): lax.all_to_all(state, 'seq', 0, 0, tiled=True, axis_index_groups=groups)  11.3 us
    ppermute x3, starting transfers between devices, permuted(): lax.ppermute(a, 'seq', [(i + f * GROUP, i + t * GROUP) for f, t in ways f...  8.76 us
    pallas_call x8, Pallas kernels, call(): pl.pallas_call(kernel, out_shape=[jax.ShapeDtypeStruct(s, d) for s, d in...  7.34 us
  transfers between devices with their start and end apart: 3, of which 1 were waited for; matrix products, arithmetic and copies ran while one was open for 0% of the time, Pallas kernels for 3%

profile of v9, /device:TPU:1, one launch (start us, length us, event | category | flops | bytes accessed | tf_op | source)
XLA Modules:
  0.0 71.2 jit_solution(3629964072805107354)
XLA Ops:
  0.0 2.4 %shard_map.100 = (bf16[8,80,128]{2,1,0:T(8,128)(2,1)S(1)}, bf16[384,512]{1,0:T(8,128)(2,1)S(1)}, bf16[384,256]{1,0:T(8,128)(2,1)S(1)}, f32[8,384]{1,0:T(8,128)S(...) custom-call(bf16[384,512]{1,0:T(8,128)(2,1)} %x_at.1, ...), custom_call_target="tpu_custom_call" | custom-call | flops 100000000 | bytes 2000000 | tf_op jit(solution)/shard_map/pallas_call | solution.py:440
  2.5 15.3 %all_to_all.15.message_ref = bf16[8,80,128]{2,1,0:T(8,128)(2,1)S(1)} all-to-all(bf16[8,80,128]{2,1,0:T(8,128)(2,1)S(1)} %get-tuple-element.27), channel_id=1, replica_groups={{0,16,32,48,64,80,96,112},{128,144,160,176,192,208,224,240},{256,272,28..., dimensions={0} | all-to-all | bytes 327680 | tf_op jit(solution)/shard_map/all_to_all | solution.py:474
  17.7 0.4 shard_map.101
  18.1 6.8 %collective-permute-start = (bf16[80,128]{1,0:T(8,128)(2,1)S(1)}, bf16[80,128]{1,0:T(8,128)(2,1)S(1)}, u32[]{:S(2)}, u32[]{:S(2)}) collective-permute-start(bf16[80,128]{1,0:T(8,128)(2,1)S(1)} %get-tuple-element.38.after_ref.total_ref), channel_id=1, source_target_pairs={{0,128},{16,144},{32,160},{48,176},{64,192},{80,208},{96,224},{112... | collective-permute-start | bytes 61448 | tf_op jit(solution)/shard_map/ppermute | solution.py:484
  24.9 0.0 copy-start
  24.9 1.6 %shard_map.102 = (f32[384,512]{1,0:T(8,128)S(1)}, f32[384,512]{1,0:T(8,128)S(1)}, f32[8,512]{1,0:T(8,128)S(1)}, f32[8,512]{1,0:T(8,128)S(1)}) custom-call(bf16[384,512]{1,0:T(8,128)(2,1)S(1)} %get-tuple-element.32.act_ref, bf16[384,256]{1,0:T(8,128)(2,1)S(1)} %get-tuple-element.33.bc_act_ref, f32[8,384]{1,0:T(8,128)S(1)} %get-tuple-element.34.cum_ref, ...), custom_call_target="tpu_custom_call" | custom-call | flops 2000000000 | bytes 2000000 | tf_op jit(solution)/shard_map/pallas_call | solution.py:440
  26.5 0.3 collective-permute-done.swapped_ref
  26.7 0.3 shard_map.103
  27.1 1.3 %collective-permute-start.1 = (bf16[80,128]{1,0:T(8,128)(2,1)S(1)}, bf16[80,128]{1,0:T(8,128)(2,1)S(1)}, u32[]{:S(2)}, u32[]{:S(2)}) collective-permute-start(bf16[80,128]{1,0:T(8,128)(2,1)S(1)} %get-tuple-element.41), channel_id=1, source_target_pairs={{128,256},{144,272},{160,288},{176,304},{192,320},{208,336},{224,3... | collective-permute-start | bytes 61448 | tf_op jit(solution)/shard_map/ppermute | solution.py:484
  28.4 0.7 collective-permute-start.2
  29.1 0.3 shard_map.104.early_ref
  29.5 0.0 collective-permute-done.1.crossed_ref
  29.5 0.0 collective-permute-done.2.passed_ref
  29.5 0.1 shard_map.105
  29.6 11.3 %all_to_all.16.state_ref = bf16[8,80,128]{2,1,0:T(8,128)(2,1)S(1)} all-to-all(bf16[8,80,128]{2,1,0:T(8,128)(2,1)S(1)} %shard_map.105), channel_id=1, replica_groups={{0,16,32,48,64,80,96,112},{128,144,160,176,192,208,224,240},{256,272,28..., dimensions={0} | all-to-all | bytes 327680 | tf_op jit(solution)/shard_map/all_to_all | solution.py:506
  40.9 0.0 copy-done
  40.9 1.2 %shard_map.106 = bf16[16,400,128]{2,1,0:T(8,128)(2,1)S(1)} custom-call(bf16[8,80,128]{2,1,0:T(8,128)(2,1)S(1)} %all_to_all.16.state_ref, bf16[384,256]{1,0:T(8,128)(2,1)S(1)} %get-tuple-element.33.bc_act_ref, f32[8,512]{1,0:T(8,128)S(1)} %get-tuple-element.42.first_x_ref, f32[8,256]{1,0:T(8,128)S(1)} %get-tuple-element.43.first_bc_ref, ...), custom_call_target="tpu_custom_call" | custom-call | flops 900000000 | bytes 2000000 | tf_op jit(solution)/shard_map/pallas_call | solution.py:440
  42.1 28.2 %all_to_all.17.share_ref = bf16[16,400,128]{2,1,0:T(8,128)(2,1)S(1)} all-to-all(bf16[16,400,128]{2,1,0:T(8,128)(2,1)S(1)} %shard_map.106), channel_id=1, replica_groups=mesh['seq'=32,'tp'=16] {'tp'}, dimensions={0} | all-to-all | bytes 3276800 | tf_op jit(solution)/shard_map/all_to_all | solution.py:513
  70.3 0.9 %shard_map.107 = bf16[384,128]{1,0:T(8,128)(2,1)} custom-call(bf16[16,400,128]{2,1,0:T(8,128)(2,1)S(1)} %all_to_all.17.share_ref), custom_call_target="tpu_custom_call" | custom-call | flops 100000000 | bytes 2000000 | tf_op jit(solution)/shard_map/pallas_call | solution.py:440
Async XLA Ops:
  18.1 8.6 %collective-permute-start = (bf16[80,128]{1,0:T(8,128)(2,1)S(1)}, bf16[80,128]{1,0:T(8,128)(2,1)S(1)}, u32[]{:S(2)}, u32[]{:S(2)}) collective-permute-start(bf16[80,128]{1,0:T(8,128)(2,1)S(1)} %get-tuple-element.38.after_ref.total_ref), channel_id=1, source_target_pairs={{0,128},{16,144},{32,160},{48,176},{64,192},{80,208},{96,224},{112... | collective-permute-start | bytes 61448 | tf_op jit(solution)/shard_map/ppermute | solution.py:484
  24.9 16.0 %copy-start = (bf16[512,2048]{1,0:T(8,128)(2,1)S(1)}, bf16[512,2048]{1,0:T(8,128)(2,1)}, u32[]{:S(2)}) copy-start(bf16[512,2048]{1,0:T(8,128)(2,1)} %weight_ref.1) | copy-start | bytes 6291460
  27.1 2.4 %collective-permute-start.1 = (bf16[80,128]{1,0:T(8,128)(2,1)S(1)}, bf16[80,128]{1,0:T(8,128)(2,1)S(1)}, u32[]{:S(2)}, u32[]{:S(2)}) collective-permute-start(bf16[80,128]{1,0:T(8,128)(2,1)S(1)} %get-tuple-element.41), channel_id=1, source_target_pairs={{128,256},{144,272},{160,288},{176,304},{192,320},{208,336},{224,3... | collective-permute-start | bytes 61448 | tf_op jit(solution)/shard_map/ppermute | solution.py:484
  28.4 1.0 %collective-permute-start.2 = (bf16[80,128]{1,0:T(8,128)(2,1)S(1)}, bf16[80,128]{1,0:T(8,128)(2,1)S(1)}, u32[]{:S(2)}, u32[]{:S(2)}) collective-permute-start(bf16[80,128]{1,0:T(8,128)(2,1)S(1)} %get-tuple-element.40.own_ref), channel_id=1, source_target_pairs={{256,384},{272,400},{288,416},{304,432},{320,448},{336,464},{352,4... | collective-permute-start | bytes 61448 | tf_op jit(solution)/shard_map/ppermute | solution.py:484

commit v10 on v8

--- a/solution.py
+++ b/solution.py
@@ -417,16 +417,19 @@
 
 
 def sum_kernel(share_ref, out_ref):
-    total = share_ref[0].astype(f32)
-    for d in range(1, SHARES):
-        total = total + share_ref[d].astype(f32)
-    extra = total[LENGTH:]
+    def summed(rows):
+        parts = [share_ref[d, rows].astype(f32) for d in range(SHARES)]
+        while len(parts) > 1:
+            parts = [x + y for x, y in zip(parts[::2], parts[1::2])]
+        return parts[0]
+
+    extra = summed(slice(LENGTH, LENGTH + EXTRA))
     for block in range(LENGTH // BLOCK):
-        rows = slice(block * BLOCK, (block + 1) * BLOCK)
         squares = extra[block : block + 1] + (extra[block + 3 : block + 4] + extra[block + 8 : block + 9])
         scale = lax.rsqrt(squares / INNER + 1e-05)
         column = jnp.broadcast_to(scale, (128, 128)).T
-        out_ref[rows] = (total[rows] * column).astype(bf16)
+        rows = slice(block * BLOCK, (block + 1) * BLOCK)
+        out_ref[rows] = (summed(rows) * column).astype(bf16)
 
 
 HERE = pl.BlockSpec(memory_space=pltpu.VMEM)

time: 71.6 us -> 71.6 us (level)
  no operation moved by 1% of the time
where the time goes in v10:
time: 71.6 us; the launch traced here: 71.2 us
  blocking collectives  54.7 us (76%)
  starting transfers between devices  8.76 us (12%)
  Pallas kernels  7.34 us (10%)
    all_to_all x1, blocking collectives, shards(): share = lax.all_to_all(share, 'tp', 0, 0, tiled=True)  28.2 us
    all_to_all x1, blocking collectives, shards(): lax.all_to_all(message, 'seq', 0, 0, tiled=True, axis_index_groups=groups)  15.3 us
    all_to_all x1, blocking collectives, shards(): lax.all_to_all(state, 'seq', 0, 0, tiled=True, axis_index_groups=groups)  11.3 us
    ppermute x3, starting transfers between devices, permuted(): lax.ppermute(a, 'seq', [(i + f * GROUP, i + t * GROUP) for f, t in ways f...  8.76 us
    pallas_call x8, Pallas kernels, call(): pl.pallas_call(kernel, out_shape=[jax.ShapeDtypeStruct(s, d) for s, d in...  7.34 us
  transfers between devices with their start and end apart: 3, of which 1 were waited for; matrix products, arithmetic and copies ran while one was open for 0% of the time, Pallas kernels for 3%

profile of v10, /device:TPU:1, one launch (start us, length us, event | category | flops | bytes accessed | tf_op | source)
XLA Modules:
  0.0 71.2 jit_solution(10133420465526178688)
XLA Ops:
  0.0 2.4 %shard_map.100 = (bf16[8,80,128]{2,1,0:T(8,128)(2,1)S(1)}, bf16[384,512]{1,0:T(8,128)(2,1)S(1)}, bf16[384,256]{1,0:T(8,128)(2,1)S(1)}, f32[8,384]{1,0:T(8,128)S(...) custom-call(bf16[384,512]{1,0:T(8,128)(2,1)} %x_at.1, ...), custom_call_target="tpu_custom_call" | custom-call | flops 100000000 | bytes 2000000 | tf_op jit(solution)/shard_map/pallas_call | solution.py:444
  2.5 15.3 %all_to_all.15.message_ref = bf16[8,80,128]{2,1,0:T(8,128)(2,1)S(1)} all-to-all(bf16[8,80,128]{2,1,0:T(8,128)(2,1)S(1)} %get-tuple-element.27), channel_id=1, replica_groups={{0,16,32,48,64,80,96,112},{128,144,160,176,192,208,224,240},{256,272,28..., dimensions={0} | all-to-all | bytes 327680 | tf_op jit(solution)/shard_map/all_to_all | solution.py:478
  17.7 0.4 shard_map.101
  18.1 6.8 %collective-permute-start = (bf16[80,128]{1,0:T(8,128)(2,1)S(1)}, bf16[80,128]{1,0:T(8,128)(2,1)S(1)}, u32[]{:S(2)}, u32[]{:S(2)}) collective-permute-start(bf16[80,128]{1,0:T(8,128)(2,1)S(1)} %get-tuple-element.38.after_ref.total_ref), channel_id=1, source_target_pairs={{0,128},{16,144},{32,160},{48,176},{64,192},{80,208},{96,224},{112... | collective-permute-start | bytes 61448 | tf_op jit(solution)/shard_map/ppermute | solution.py:488
  24.9 0.0 copy-start
  24.9 1.6 %shard_map.102 = (f32[384,512]{1,0:T(8,128)S(1)}, f32[384,512]{1,0:T(8,128)S(1)}, f32[8,512]{1,0:T(8,128)S(1)}, f32[8,512]{1,0:T(8,128)S(1)}) custom-call(bf16[384,512]{1,0:T(8,128)(2,1)S(1)} %get-tuple-element.32.act_ref, bf16[384,256]{1,0:T(8,128)(2,1)S(1)} %get-tuple-element.33.bc_act_ref, f32[8,384]{1,0:T(8,128)S(1)} %get-tuple-element.34.cum_ref, ...), custom_call_target="tpu_custom_call" | custom-call | flops 2000000000 | bytes 2000000 | tf_op jit(solution)/shard_map/pallas_call | solution.py:444
  26.5 0.3 collective-permute-done.swapped_ref
  26.7 0.3 shard_map.103
  27.1 1.3 %collective-permute-start.1 = (bf16[80,128]{1,0:T(8,128)(2,1)S(1)}, bf16[80,128]{1,0:T(8,128)(2,1)S(1)}, u32[]{:S(2)}, u32[]{:S(2)}) collective-permute-start(bf16[80,128]{1,0:T(8,128)(2,1)S(1)} %get-tuple-element.41), channel_id=1, source_target_pairs={{128,256},{144,272},{160,288},{176,304},{192,320},{208,336},{224,3... | collective-permute-start | bytes 61448 | tf_op jit(solution)/shard_map/ppermute | solution.py:488
  28.4 0.7 collective-permute-start.2
  29.1 0.3 shard_map.104.early_ref
  29.5 0.0 collective-permute-done.1.crossed_ref
  29.5 0.0 collective-permute-done.2.passed_ref
  29.5 0.1 shard_map.105
  29.6 11.3 %all_to_all.16.state_ref = bf16[8,80,128]{2,1,0:T(8,128)(2,1)S(1)} all-to-all(bf16[8,80,128]{2,1,0:T(8,128)(2,1)S(1)} %shard_map.105), channel_id=1, replica_groups={{0,16,32,48,64,80,96,112},{128,144,160,176,192,208,224,240},{256,272,28..., dimensions={0} | all-to-all | bytes 327680 | tf_op jit(solution)/shard_map/all_to_all | solution.py:510
  40.9 0.0 copy-done
  40.9 1.2 %shard_map.106 = bf16[16,400,128]{2,1,0:T(8,128)(2,1)S(1)} custom-call(bf16[8,80,128]{2,1,0:T(8,128)(2,1)S(1)} %all_to_all.16.state_ref, bf16[384,256]{1,0:T(8,128)(2,1)S(1)} %get-tuple-element.33.bc_act_ref, f32[8,512]{1,0:T(8,128)S(1)} %get-tuple-element.42.first_x_ref, f32[8,256]{1,0:T(8,128)S(1)} %get-tuple-element.43.first_bc_ref, ...), custom_call_target="tpu_custom_call" | custom-call | flops 900000000 | bytes 2000000 | tf_op jit(solution)/shard_map/pallas_call | solution.py:444
  42.1 28.2 %all_to_all.17.share_ref = bf16[16,400,128]{2,1,0:T(8,128)(2,1)S(1)} all-to-all(bf16[16,400,128]{2,1,0:T(8,128)(2,1)S(1)} %shard_map.106), channel_id=1, replica_groups=mesh['seq'=32,'tp'=16] {'tp'}, dimensions={0} | all-to-all | bytes 3276800 | tf_op jit(solution)/shard_map/all_to_all | solution.py:517
  70.3 0.9 %shard_map.107 = bf16[384,128]{1,0:T(8,128)(2,1)} custom-call(bf16[16,400,128]{2,1,0:T(8,128)(2,1)S(1)} %all_to_all.17.share_ref), custom_call_target="tpu_custom_call" | custom-call | flops 100000000 | bytes 2000000 | tf_op jit(solution)/shard_map/pallas_call | solution.py:444
Async XLA Ops:
  18.1 8.6 %collective-permute-start = (bf16[80,128]{1,0:T(8,128)(2,1)S(1)}, bf16[80,128]{1,0:T(8,128)(2,1)S(1)}, u32[]{:S(2)}, u32[]{:S(2)}) collective-permute-start(bf16[80,128]{1,0:T(8,128)(2,1)S(1)} %get-tuple-element.38.after_ref.total_ref), channel_id=1, source_target_pairs={{0,128},{16,144},{32,160},{48,176},{64,192},{80,208},{96,224},{112... | collective-permute-start | bytes 61448 | tf_op jit(solution)/shard_map/ppermute | solution.py:488
  24.9 16.0 %copy-start = (bf16[512,2048]{1,0:T(8,128)(2,1)S(1)}, bf16[512,2048]{1,0:T(8,128)(2,1)}, u32[]{:S(2)}) copy-start(bf16[512,2048]{1,0:T(8,128)(2,1)} %weight_ref.1) | copy-start | bytes 6291460
  27.1 2.4 %collective-permute-start.1 = (bf16[80,128]{1,0:T(8,128)(2,1)S(1)}, bf16[80,128]{1,0:T(8,128)(2,1)S(1)}, u32[]{:S(2)}, u32[]{:S(2)}) collective-permute-start(bf16[80,128]{1,0:T(8,128)(2,1)S(1)} %get-tuple-element.41), channel_id=1, source_target_pairs={{128,256},{144,272},{160,288},{176,304},{192,320},{208,336},{224,3... | collective-permute-start | bytes 61448 | tf_op jit(solution)/shard_map/ppermute | solution.py:488
  28.4 1.0 %collective-permute-start.2 = (bf16[80,128]{1,0:T(8,128)(2,1)S(1)}, bf16[80,128]{1,0:T(8,128)(2,1)S(1)}, u32[]{:S(2)}, u32[]{:S(2)}) collective-permute-start(bf16[80,128]{1,0:T(8,128)(2,1)S(1)} %get-tuple-element.40.own_ref), channel_id=1, source_target_pairs={{256,384},{272,400},{288,416},{304,432},{320,448},{336,464},{352,4... | collective-permute-start | bytes 61448 | tf_op jit(solution)/shard_map/ppermute | solution.py:488
